TPU v7x, 32 devices: a whole 2x2x4 slice. The times are simulated.
32 devices in a mesh: dp: 4 (over y, x), chan: 8 (over z, core).
Axes of the slice: x: 2, y: 2, z: 4, core: 2. Of those that a mesh axis runs over, the one named last changes fastest.
Arguments:
- images: bfloat16 [4, 768, 128, 128], P('dp', 'chan'), may hold values from -6 to 6
- cotangent: bfloat16 [4, 768, 128, 128], P('dp', 'chan'), may hold values from -6 to 6
- image_sizes: int32 [4, 2], replicated, may hold values from 64 to 128
- slot_image: int32 [4], replicated, may hold values from 0 to 3, each once
- rows_rate: float32 [768, 32], P('chan'), may hold values from 0.01 to 0.3
- rows_freq: float32 [768, 32], P('chan'), may hold values from 0 to 1.5
- rows_real: float32 [768, 32], P('chan'), may hold values from -0.36 to 0.36
- rows_imag: float32 [768, 32], P('chan'), may hold values from -0.36 to 0.36
- cols_rate: float32 [768, 32], P('chan'), may hold values from 0.01 to 0.3
- cols_freq: float32 [768, 32], P('chan'), may hold values from 0 to 1.5
- cols_real: float32 [768, 32], P('chan'), may hold values from -0.36 to 0.36
- cols_imag: float32 [768, 32], P('chan'), may hold values from -0.36 to 0.36
- skip_gain: float32 [768], P('chan'), may hold values from 0.25 to 1.75
- norm_gain: float32 [768], replicated, may hold values from 0.5 to 1.5
- norm_bias: float32 [768], replicated, may hold values from -1.8 to 1.8
- weight_in: bfloat16 [768, 3072], P(None, 'chan'), may hold values from -0.21875 to 0.21875
- bias_in: bfloat16 [3072], P('chan'), may hold values from -1.796875 to 1.796875
- weight_out: bfloat16 [3072, 768], P('chan'), may hold values from -0.15625 to 0.15625
- bias_out: float32 [768], P('chan'), may hold values from -3 to 3
- layer_scale: float32 [768], P('chan'), may hold values from 0.5 to 1.5
Outputs:
- output: bfloat16 [4, 768, 128, 128], P('dp', 'chan')
- input_grad: float32 [4, 768, 128, 128], P('dp', 'chan')
- rows_rate_grad: float32 [768, 32], P('chan')
- rows_freq_grad: float32 [768, 32], P('chan')
- rows_real_grad: float32 [768, 32], P('chan')
- rows_imag_grad: float32 [768, 32], P('chan')
- cols_rate_grad: float32 [768, 32], P('chan')
- cols_freq_grad: float32 [768, 32], P('chan')
- cols_real_grad: float32 [768, 32], P('chan')
- cols_imag_grad: float32 [768, 32], P('chan')
- skip_gain_grad: float32 [768], P('chan')
- norm_gain_grad: float32 [768], replicated
- norm_bias_grad: float32 [768], replicated
- weight_in_grad: float32 [768, 3072], P(None, 'chan')
- bias_in_grad: float32 [3072], P('chan')
- weight_out_grad: float32 [3072, 768], P('chan')
- bias_out_grad: float32 [768], P('chan')
- layer_scale_grad: float32 [768], P('chan')
Inputs may be any that keep to these rules, and one draw needn't show every extreme that they name: `image_sizes`: heights (column 0) and widths (column 1) of the images, in list order. Slot s of the batch holds image slot_image[s] of the list; each image once.
All inputs are finite; a program needn't handle non-finite values.
Results may differ from a plain program's by a relative error of at most 0.0074.
Values may be sent and summed in bfloat16 or wider, within the bound.
A program may use at most 640 MiB of HBM per device.

v0:
```python
import jax
import jax.numpy as jnp
from jax import lax
from jax.sharding import PartitionSpec as P

eps_norm = 1e-06
highest = lax.Precision.HIGHEST


def kernel_taps(rate_vals, freq_vals, real_part, imag_part, length):
    offsets = jnp.arange(length, dtype=jnp.float32)
    decays = jnp.exp(-rate_vals[:, :, None] * offsets)
    angles = freq_vals[:, :, None] * offsets
    return jnp.sum(
        decays
        * (real_part[:, :, None] * jnp.cos(angles) - imag_part[:, :, None] * jnp.sin(angles)),
        axis=1,
    )


def toeplitz(filter_taps):
    length = filter_taps.shape[1]
    offsets = jnp.arange(length, dtype=jnp.int32)
    lag_index = offsets[:, None] - offsets[None, :]
    return jnp.where(lag_index[None] >= 0, filter_taps[:, jnp.maximum(lag_index, 0)], 0.0)


def mixer(
    masked_in,
    rows_rate,
    rows_freq,
    rows_real,
    rows_imag,
    cols_rate,
    cols_freq,
    cols_real,
    cols_imag,
    skip_gain,
):
    rows_op = toeplitz(kernel_taps(rows_rate, rows_freq, rows_real, rows_imag, masked_in.shape[2]))
    cols_op = toeplitz(kernel_taps(cols_rate, cols_freq, cols_real, cols_imag, masked_in.shape[3]))
    along_rows = jnp.einsum("chi,ncij->nchj", rows_op, masked_in, precision=highest)
    return (
        jnp.einsum("nchj,cwj->nchw", along_rows, cols_op, precision=highest)
        + skip_gain[None, :, None, None] * masked_in
    )


def normalize(values, norm_gain, norm_bias):
    center = values - jnp.mean(values, axis=-2, keepdims=True)
    inverse = lax.rsqrt(jnp.mean(center * center, axis=-2, keepdims=True) + eps_norm)
    scaled = center * inverse
    return (scaled * norm_gain[:, None] + norm_bias[:, None], scaled, inverse)


def gelu_exact(values):
    return jax.nn.gelu(values, approximate=False)


def body(
    images,
    cotangent,
    image_sizes,
    slot_image,
    rows_rate,
    rows_freq,
    rows_real,
    rows_imag,
    cols_rate,
    cols_freq,
    cols_real,
    cols_imag,
    skip_gain,
    norm_gain,
    norm_bias,
    weight_in,
    bias_in,
    weight_out,
    bias_out,
    layer_scale,
):
    slot_count, chan_count, length = (images.shape[0], images.shape[1], images.shape[2])
    pixels = length * length
    image_count = slot_image.shape[0]
    slot_ids = lax.axis_index("dp") * slot_count + jnp.arange(slot_count, dtype=jnp.int32)
    choose = (slot_ids[:, None] == jnp.arange(image_count, dtype=jnp.int32)[None, :]).astype(
        jnp.int32
    )
    picked = jnp.sum(choose * slot_image[None, :], axis=1)
    owners = (picked[:, None] == jnp.arange(image_count, dtype=jnp.int32)[None, :]).astype(
        jnp.int32
    )
    heights = jnp.sum(owners * image_sizes[None, :, 0], axis=1)
    widths = jnp.sum(owners * image_sizes[None, :, 1], axis=1)
    offsets = jnp.arange(length, dtype=jnp.int32)
    inside = (
        (offsets[None, :, None] < heights[:, None, None])
        & (offsets[None, None, :] < widths[:, None, None])
    ).astype(jnp.float32)
    masked_in = images.astype(jnp.float32) * inside[:, None]
    mixed_out, mixer_pull = jax.vjp(
        mixer,
        masked_in,
        rows_rate,
        rows_freq,
        rows_real,
        rows_imag,
        cols_rate,
        cols_freq,
        cols_real,
        cols_imag,
        skip_gain,
    )
    mixed_low = mixed_out.astype(jnp.bfloat16).reshape(slot_count, chan_count, pixels)
    mask_flat = inside.reshape(slot_count, 1, pixels)
    residual = images.astype(jnp.float32).reshape(slot_count, chan_count, pixels)
    grad_out = cotangent.astype(jnp.float32).reshape(slot_count, chan_count, pixels) * mask_flat
    chan_offset = lax.axis_index("chan") * chan_count
    all_channels = norm_gain.shape[0]
    slot_item = 0
    gathered = lax.all_gather(mixed_low[slot_item], "chan", axis=0, tiled=True)
    normed, scaled, inverse = normalize(gathered.astype(jnp.float32), norm_gain, norm_bias)
    normed_low = normed.astype(jnp.bfloat16)
    before = (
        jnp.einsum("cf,cp->fp", weight_in, normed_low, preferred_element_type=jnp.float32)
        + bias_in.astype(jnp.float32)[:, None]
    )
    active = gelu_exact(before).astype(jnp.bfloat16)

    def project(first_row, row_count, active=active):
        return jnp.einsum("fc,fp->cp", weight_out, active, preferred_element_type=jnp.float32)

    branch_list = [
        lax.psum_scatter(
            project(jnp.int32(0), chan_count * lax.axis_size("chan")),
            "chan",
            scatter_dimension=0,
            tiled=True,
        )
    ]
    scaled_part = lax.dynamic_slice_in_dim(scaled, chan_offset, chan_count, 0)
    stored = [(normed_low, before, active, scaled_part, inverse)]
    branch_all = jnp.stack(branch_list)
    shifted = branch_all + bias_out[None, :, None]
    output = (
        (mask_flat * (residual + layer_scale[None, :, None] * shifted))
        .astype(jnp.bfloat16)
        .reshape(images.shape)
    )
    scale_grad = jnp.sum(grad_out * shifted, axis=(0, 2))
    branch_grad = layer_scale[None, :, None] * grad_out
    bias_out_grad = jnp.sum(branch_grad, axis=(0, 2))
    branch_low = branch_grad.astype(jnp.bfloat16)
    hidden_count = weight_in.shape[1]
    out_weight_grad = jnp.zeros((hidden_count, all_channels), jnp.float32)
    gain_shard = lax.dynamic_slice_in_dim(norm_gain, chan_offset, chan_count, 0)
    slot_item = 0
    normed_low, before, active, scaled_part, inverse = stored[slot_item]

    def absorb(totals, shard_rows, first_row, active=active):
        hidden_grad = jnp.einsum(
            "fc,cp->fp", weight_out, shard_rows, preferred_element_type=jnp.float32
        )
        product_part = jnp.einsum(
            "fp,cp->fc", active, shard_rows, preferred_element_type=jnp.float32
        )
        return (hidden_grad, product_part)

    hidden_start = jnp.zeros((hidden_count, pixels), jnp.float32)
    hidden_grad, out_weight_grad = absorb(
        (hidden_start, out_weight_grad),
        lax.all_gather(branch_low[slot_item], "chan", axis=0, tiled=True),
        jnp.int32(0),
    )
    gelu_pull = jax.vjp(gelu_exact, before)[1]
    before_grad = gelu_pull(hidden_grad)[0].astype(jnp.bfloat16)
    in_weight_grad = jnp.einsum(
        "cp,fp->cf", normed_low, before_grad, preferred_element_type=jnp.float32
    )
    in_bias_grad = jnp.sum(before_grad.astype(jnp.float32), axis=1)

    def spread_back(first_row, row_count, before_grad=before_grad):
        return jnp.einsum("cf,fp->cp", weight_in, before_grad, preferred_element_type=jnp.float32)

    normed_grad = lax.psum_scatter(
        spread_back(jnp.int32(0), chan_count * lax.axis_size("chan")),
        "chan",
        scatter_dimension=0,
        tiled=True,
    )
    weighted = normed_grad * gain_shard[:, None]
    pixel_sums = (
        lax.psum(jnp.sum(weighted, axis=0).astype(jnp.bfloat16), "chan").astype(jnp.float32),
        lax.psum(jnp.sum(weighted * scaled_part, axis=0).astype(jnp.bfloat16), "chan").astype(
            jnp.float32
        ),
    )
    mixed_grads = [
        inverse
        * (
            weighted
            - pixel_sums[0][None, :] / all_channels
            - scaled_part * pixel_sums[1][None, :] / all_channels
        )
    ]
    gain_part = jnp.sum(normed_grad * scaled_part, axis=1)
    shift_part = jnp.sum(normed_grad, axis=1)
    mixed_grad_all = jnp.stack(mixed_grads)
    gain_grad = lax.dynamic_update_slice_in_dim(
        jnp.zeros((all_channels,), jnp.float32), gain_part, chan_offset, 0
    )
    shift_grad = lax.dynamic_update_slice_in_dim(
        jnp.zeros((all_channels,), jnp.float32), shift_part, chan_offset, 0
    )
    pulled = mixer_pull(mixed_grad_all.reshape(images.shape))
    input_grad = inside[:, None] * (cotangent.astype(jnp.float32) + pulled[0])
    summed = lax.psum(
        (
            in_weight_grad,
            out_weight_grad,
            in_bias_grad,
            bias_out_grad,
            scale_grad,
            pulled[1],
            pulled[2],
            pulled[3],
            pulled[4],
            pulled[5],
            pulled[6],
            pulled[7],
            pulled[8],
            pulled[9],
        ),
        "dp",
    )
    norm_sums = lax.psum((gain_grad, shift_grad), ("dp", "chan"))
    return (
        output,
        input_grad,
        summed[5],
        summed[6],
        summed[7],
        summed[8],
        summed[9],
        summed[10],
        summed[11],
        summed[12],
        summed[13],
        norm_sums[0],
        norm_sums[1],
        summed[0],
        summed[2],
        summed[1],
        summed[3],
        summed[4],
    )


def solution(mesh):
    in_specs = (
        P("dp", "chan", None, None),
        P("dp", "chan", None, None),
        P(),
        P(),
        P("chan", None),
        P("chan", None),
        P("chan", None),
        P("chan", None),
        P("chan", None),
        P("chan", None),
        P("chan", None),
        P("chan", None),
        P("chan"),
        P(),
        P(),
        P(None, "chan"),
        P("chan"),
        P("chan", None),
        P("chan"),
        P("chan"),
    )
    out_specs = (
        P("dp", "chan", None, None),
        P("dp", "chan", None, None),
        P("chan", None),
        P("chan", None),
        P("chan", None),
        P("chan", None),
        P("chan", None),
        P("chan", None),
        P("chan", None),
        P("chan", None),
        P("chan"),
        P(),
        P(),
        P(None, "chan"),
        P("chan"),
        P("chan", None),
        P("chan"),
        P("chan"),
    )
    return jax.shard_map(body, mesh=mesh, in_specs=in_specs, out_specs=out_specs, check_vma=False)
```

profile of v0, /device:TPU:9, one launch (start us, length us, event | category | flops | bytes accessed | tf_op | source)
XLA Modules:
  0.0 2422.0 jit_solution(10489563424850664839)
XLA Ops:
  8.7 2.0 fusion.96
  16.1 6.8 multiply_reduce_fusion.14
  23.0 54.4 %gather_fusion.1 = f32[16384,96]{1,0:T(8,128)} fusion(f32[96,128]{0,1:T(8,128)S(1)} %copy.140, s32[16384]{0:T(1024)S(1)} %broadcast_clamp_fusion), kind=kCustom, calls=%fused_computation.1 | custom fusion | bytes 12648448 | tf_op jit(solution)/shard_map/jvp()/gather | solution.py:25
  77.4 8.6 copy.141
  86.0 4.7 copy.127
  91.4 6.8 multiply_reduce_fusion.15
  98.3 54.4 %gather_fusion = f32[16384,96]{1,0:T(8,128)} fusion(f32[96,128]{0,1:T(8,128)S(1)} %copy.133, s32[16384]{0:T(1024)S(1)} %broadcast_clamp_fusion), kind=kCustom, calls=%fused_computation | custom fusion | bytes 12648448 | tf_op jit(solution)/shard_map/jvp()/gather | solution.py:25
  152.8 8.6 copy.134
  161.4 15.5 fusion.42
  176.9 2.6 copy-done.7
  179.5 9.4 fusion.29
  189.0 4.6 copy.143
  193.6 6.0 copy.195
  199.8 218.6 %all-gather.3.cloned.1.call-done = bf16[768,16384]{1,0:T(8,128)(2,1)} async-done(((bf16[96,16384]{1,0:T(8,128)(2,1)}), bf16[768,16384]{1,0:T(8,128)(2,1)}) %all-gather.3.cloned.1.call-update) | async-done | bytes 25165840 | tf_op jit(solution)/shard_map/all_gather | solution.py:121
  418.3 10.1 convert_reduce_fusion
  428.4 5.4 copy-done.1
  433.8 7.1 fusion.2
  441.0 31.1 %fusion = (f32[768,16384]{1,0:T(8,128)}, bf16[768,16384]{1,0:T(8,128)(2,1)}) fusion(bf16[768,16384]{1,0:T(8,128)(2,1)} %all-gather.3.cloned.1.call-done, f32[16384]{0:T(1024)S(1)} %add_rsqrt_fusion, f32[16384]{0:T(1024)S(1)} %broadcast_multiply_fusion, f32[768]{0:T(1024)S(1)} %copy-done.39, f32[768]{0:T(1024)S(1)} %copy-done.40), kind=kLoop, calls=%fused_computation.6 | loop fusion | flops 75497472 | bytes 100800512 | tf_op jit(solution)/shard_map/mul | solution.py:52
  472.1 71.0 %fusion.12 = (bf16[384,16384]{0,1:T(8,128)(2,1)}, f32[384,16384]{0,1:T(8,128)}, f32[16384,384]{1,0:T(8,128)}) fusion(f32[384]{0:T(512)S(1)} %convert_element_type.74, bf16[768,16384]{1,0:T(8,128)(2,1)} %get-tuple-element.129, bf16[768,384]{1,0:T(8,128)(2,1)S(1)} %copy-done), kind=kOutput, calls=%fused_computation.29 | convolution fusion | flops 10078912512 | bytes 88671744 | tf_op jit(solution)/shard_map/cf,cp->fp/dot_general | solution.py:125
  543.1 25.8 %convolution_bitcast_fusion.1 = f32[768,16384]{0,1:T(8,128)} fusion(bf16[384,16384]{0,1:T(8,128)(2,1)} %get-tuple-element.126, bf16[384,768]{1,0:T(8,128)(2,1)S(1)} %copy-done.14), kind=kOutput, calls=%fused_computation.12 | convolution fusion | flops 9663676416 | bytes 63504384 | tf_op jit(solution)/shard_map/fc,fp->cp/dot_general | solution.py:131
  568.9 48.8 %copy.176 = f32[768,16384]{1,0:T(8,128)} copy(f32[768,16384]{0,1:T(8,128)} %convolution_bitcast_fusion.1) | data formatting | bytes 100663296
  617.8 5.4 copy.128
  623.2 4.9 copy.145
  628.1 5.4 copy.146
  633.6 466.6 %reduce-scatter.7.cloned.1.call-done = f32[96,16384]{1,0:T(8,128)} async-done(((f32[768,16384]{1,0:T(8,128)}), f32[96,16384]{1,0:T(8,128)}) %reduce-scatter.7.cloned.1.call-update) | async-done | bytes 6291472 | tf_op jit(solution)/shard_map/reduce_scatter | solution.py:134
  1100.3 18.0 multiply_reduce_fusion
  1118.3 217.3 %all-gather.5.cloned.1.call-done = bf16[768,16384]{1,0:T(8,128)(2,1)} async-done(((bf16[96,16384]{1,0:T(8,128)(2,1)}), bf16[768,16384]{1,0:T(8,128)(2,1)}) %all-gather.5.cloned.1.call-update) | async-done | bytes 25165840 | tf_op jit(solution)/shard_map/all_gather | solution.py:172
  1335.6 34.2 %convert_reduce_fusion.1 = (f32[384]{0:T(512)}, bf16[384,16384]{0,1:T(8,128)(2,1)}) fusion(f32[384,16384]{0,1:T(8,128)} %get-tuple-element.127, f32[16384,384]{1,0:T(8,128)} %get-tuple-element.133, bf16[768,16384]{1,0:T(8,128)(2,1)} %all-gather.5.cloned.1.call-done, bf16[384,768]{1,0:T(8,128)(2,1)S(1)} %copy-done.14), kind=kOutput, calls=%fused_computation.30 | convolution fusion | flops 9764339712 | bytes 88671744 | tf_op jit(solution)/shard_map/fc,cp->fp/dot_general | solution.py:161
  1369.8 25.5 %convolution_bitcast_fusion = f32[768,16384]{0,1:T(8,128)} fusion(bf16[384,16384]{0,1:T(8,128)(2,1)} %get-tuple-element.135, bf16[768,384]{1,0:T(8,128)(2,1)S(1)} %copy-done), kind=kOutput, calls=%fused_computation.11 | convolution fusion | flops 9663676416 | bytes 63504384 | tf_op jit(solution)/shard_map/cf,fp->cp/dot_general | solution.py:183
  1395.3 48.8 %copy.178 = f32[768,16384]{1,0:T(8,128)} copy(f32[768,16384]{0,1:T(8,128)} %convolution_bitcast_fusion) | data formatting | bytes 100663296
  1444.2 5.4 copy.159
  1450.4 10.7 multiply_reduce_fusion.1
  1461.0 465.6 %reduce-scatter.9.cloned.1.call-done = f32[96,16384]{1,0:T(8,128)} async-done(((f32[768,16384]{1,0:T(8,128)}), f32[96,16384]{1,0:T(8,128)}) %reduce-scatter.9.cloned.1.call-update) | async-done | bytes 6291472 | tf_op jit(solution)/shard_map/reduce_scatter | solution.py:185
  1926.7 6.2 multiply_reduce_fusion.2
  1933.0 20.9 fusion.106
  1953.9 30.6 %all-reduce.12.cloned.1.call-done = (bf16[16384]{0:T(1024)(128)(2,1)}, bf16[16384]{0:T(1024)(128)(2,1)}) async-done(((bf16[16384]{0:T(1024)(128)(2,1)}, bf16[16384]{0:T(1024)(128)(2,1)}), (bf16[16384]{0:T(1024)(128)(2,1)}, bf16[16384]{0:T(1024)(128)(2,1)})) %all-reduce.12.cloned.1.call-update) | async-done | bytes 65552 | tf_op jit(solution)/shard_map/psum | solution.py:194
  1986.0 6.2 multiply_bitcast_fusion
  1993.3 2.6 copy-done.4
  1995.9 13.9 select_bitcast_fusion
  2009.8 8.5 copy.175
  2018.3 98.3 %scatter_custom_fusion.1 = f32[96,128]{0,1:T(8,128)S(1)} fusion(s32[16384]{0:T(1024)S(1)} %maximum_bitcast_fusion, f32[16384,96]{1,0:T(8,128)} %bitcast.245, f32[]{:T(128)} %constant.40.clone.1), kind=kCustom, calls=%fused_computation.134 | custom fusion | flops 1572864 | bytes 49664 | tf_op jit(solution)/shard_map/transpose(jvp())/scatter-add | solution.py:25
  2116.7 10.0 multiply_reduce_fusion.6
  2127.3 9.1 fusion.35
  2136.5 2.6 copy-done.6
  2139.0 8.5 select_bitcast_fusion.1
  2147.6 8.5 copy.174
  2156.1 98.3 %scatter_custom_fusion = f32[96,128]{0,1:T(8,128)S(1)} fusion(s32[16384]{0:T(1024)S(1)} %maximum_bitcast_fusion, f32[16384,96]{1,0:T(8,128)} %bitcast.244, f32[]{:T(128)} %constant.40.clone.1), kind=kCustom, calls=%fused_computation.136 | custom fusion | flops 1572864 | bytes 49664 | tf_op jit(solution)/shard_map/transpose(jvp())/scatter-add | solution.py:25
  2254.5 10.0 multiply_reduce_fusion.10
  2265.2 6.6 copy.148
  2271.8 5.3 multiply_reduce_fusion.3
  2277.2 18.2 fusion.107
  2295.4 4.5 copy.183
  2300.3 42.3 %all-reduce = (f32[768]{0:T(1024)}, f32[768]{0:T(1024)}) all-reduce(f32[768]{0:T(1024)S(1)} %dynamic_update_slice.6, f32[768]{0:T(1024)S(1)} %dynamic_update_slice.7), channel_id=1, replica_groups=mesh['dp'=4,'chan'=8] {'dp','chan'}, use_global_device_ids=true, to_apply=%region_34.35 | all-reduce | flops 1536 | bytes 12288 | tf_op jit(solution)/shard_map/psum | solution.py:236
  2342.6 17.6 fusion.28
  2360.2 6.6 copy.160
  2366.8 1.5 copy.161
  2369.7 1.5 copy.163
  2372.7 1.5 copy.165
  2374.1 1.5 copy.166
  2375.6 1.5 copy.167
  2377.1 1.5 copy.168
  2378.6 26.7 %all-reduce.10.cloned.1.call-done = (f32[768,384]{1,0:T(8,128)}, f32[384,768]{1,0:T(8,128)}) async-done(((f32[768,384]{1,0:T(8,128)}, f32[384,768]{1,0:T(8,128)}), (f32[768,384]{1,0:T(8,128)}, f32[384,768]{1,0:T(8,128)})) %all-reduce.10.cloned.1.call-update) | async-done | bytes 2359312 | tf_op jit(solution)/shard_map/psum | solution.py:217
  2406.4 2.4 copy.217
  2410.0 2.4 copy.219
  (144 shorter events, 21.0 us)
Async XLA Ops:
  7.2 464.9 %copy-start = (bf16[768,384]{1,0:T(8,128)(2,1)S(1)}, bf16[768,384]{1,0:T(8,128)(2,1)}, u32[]{:S(2)}) copy-start(bf16[768,384]{1,0:T(8,128)(2,1)} %param.35) | copy-start | bytes 1769476
  7.2 411.1 %all-gather.3.cloned.1.call-start = ((), (), s32[]{:S(2)}) async-start(), calls=%async_computation.2 | async-start | bytes 28311552 | tf_op jit(solution)/shard_map/all_gather | solution.py:121
  7.3 169.6 %copy-start.10 = (pred[128,128]{1,0:T(8,128)(4,1)}, pred[128,128]{1,0:T(8,128)(4,1)S(1)}, u32[]{:S(2)}) copy-start(pred[128,128]{1,0:T(8,128)(4,1)S(1)} %subtract_compare_fusion) | copy-start | bytes 49156
  12.0 0.5 copy-start.35
  12.0 0.5 copy-start.37
  12.7 164.2 %copy-start.8 = (f32[128,128]{0,1:T(8,128)}, f32[128,128]{0,1:T(8,128)S(1)}, u32[]{:S(2)}) copy-start(f32[128,128]{0,1:T(8,128)S(1)} %copy.135) | copy-start | bytes 196612
  13.6 2.5 copy-start.15
  14.4 63.0 %copy-start.17 = (f32[96,32]{1,0:T(8,128)}, f32[96,32]{1,0:T(8,128)S(1)}, u32[]{:S(2)}) copy-start(f32[96,32]{1,0:T(8,128)S(1)} %copy.137) | copy-start | bytes 36868
  15.2 62.2 %copy-start.19 = (f32[96,32]{1,0:T(8,128)}, f32[96,32]{1,0:T(8,128)S(1)}, u32[]{:S(2)}) copy-start(f32[96,32]{1,0:T(8,128)S(1)} %copy.138) | copy-start | bytes 36868
  16.1 61.4 %copy-start.21 = (f32[96,32]{1,0:T(8,128)}, f32[96,32]{1,0:T(8,128)S(1)}, u32[]{:S(2)}) copy-start(f32[96,32]{1,0:T(8,128)S(1)} %copy.139) | copy-start | bytes 36868
  86.0 4.7 copy-start.31
  86.0 4.8 copy-start.32
  86.0 4.9 copy-start.33
  86.0 5.0 copy-start.34
  90.8 0.6 copy-start.23
  90.9 61.8 %copy-start.25 = (f32[96,32]{1,0:T(8,128)}, f32[96,32]{1,0:T(8,128)S(1)}, u32[]{:S(2)}) copy-start(f32[96,32]{1,0:T(8,128)S(1)} %copy.130) | copy-start | bytes 36868
  91.0 61.7 %copy-start.27 = (f32[96,32]{1,0:T(8,128)}, f32[96,32]{1,0:T(8,128)S(1)}, u32[]{:S(2)}) copy-start(f32[96,32]{1,0:T(8,128)S(1)} %copy.131) | copy-start | bytes 36868
  91.4 61.3 %copy-start.29 = (f32[96,32]{1,0:T(8,128)}, f32[96,32]{1,0:T(8,128)S(1)}, u32[]{:S(2)}) copy-start(f32[96,32]{1,0:T(8,128)S(1)} %copy.132) | copy-start | bytes 36868
  161.4 18.2 copy-start.2
  161.4 18.2 copy-start.5
  161.4 18.2 copy-start.41
  176.9 2.6 copy-start.7
  193.6 6.1 copy-start.44
  199.7 900.6 %reduce-scatter.7.cloned.1.call-start = ((), (), s32[]{:S(2)}) async-start(), calls=%async_computation.4 | async-start | bytes 56623104 | tf_op jit(solution)/shard_map/reduce_scatter | solution.py:134
  418.3 15.5 copy-start.1
  433.8 7.1 copy-start.39
  433.8 7.1 copy-start.40
  440.9 31.2 %copy-start.12 = (f32[16384]{0:T(1024)}, f32[16384]{0:T(1024)S(1)}, u32[]{:S(2)}) copy-start(f32[16384]{0:T(1024)S(1)} %add_rsqrt_fusion) | copy-start | bytes 196612
  472.1 71.0 %copy-start.14 = (bf16[384,768]{1,0:T(8,128)(2,1)S(1)}, bf16[384,768]{1,0:T(8,128)(2,1)}, u32[]{:S(2)}) copy-start(bf16[384,768]{1,0:T(8,128)(2,1)} %param.37) | copy-start | bytes 1769476
  617.7 717.9 %all-gather.5.cloned.1.call-start = ((), (), s32[]{:S(2)}) async-start(), calls=%async_computation.3 | async-start | bytes 28311552 | tf_op jit(solution)/shard_map/all_gather | solution.py:172
  623.2 10.4 copy-start.36
  623.2 10.4 copy-start.38
  628.1 472.2 %copy-start.43 = (f32[96]{0:T(128)S(1)}, f32[96]{0:T(128)}, u32[]{:S(2)}) copy-start(f32[96]{0:T(128)} %param.39) | copy-start | bytes 1156
  628.1 472.2 %copy-start.45 = (f32[96]{0:T(128)S(1)}, f32[96]{0:T(128)}, u32[]{:S(2)}) copy-start(f32[96]{0:T(128)} %param.38) | copy-start | bytes 1156
  1118.3 808.4 %reduce-scatter.9.cloned.1.call-start = ((), (), s32[]{:S(2)}) async-start(), calls=%async_computation.5 | async-start | bytes 56623104 | tf_op jit(solution)/shard_map/reduce_scatter | solution.py:185
  1444.2 540.3 %all-reduce.12.cloned.1.call-start = ((), (), s32[]{:S(2)}) async-start(), calls=%async_computation.8 | async-start | bytes 131072 | tf_op jit(solution)/shard_map/psum | solution.py:194
  1932.9 53.1 %copy-start.13 = (f32[16384]{0:T(1024)S(1)}, f32[16384]{0:T(1024)}, u32[]{:S(2)}) copy-start(f32[16384]{0:T(1024)} %copy-done.12) | copy-start | bytes 196612
  1932.9 433.8 %all-reduce.8.cloned.1.call-start = ((), (), s32[]{:S(2)}) async-start(), calls=%async_computation.6 | async-start | bytes 793600 | tf_op jit(solution)/shard_map/psum | solution.py:217
  1992.2 3.7 copy-start.11
  1993.3 2.6 copy-start.4
  2009.8 106.9 %copy-start.24 = (f32[96,32]{1,0:T(8,128)S(1)}, f32[96,32]{1,0:T(8,128)}, u32[]{:S(2)}) copy-start(f32[96,32]{1,0:T(8,128)} %copy-done.23) | copy-start | bytes 36868
  2009.8 106.9 %copy-start.26 = (f32[96,32]{1,0:T(8,128)S(1)}, f32[96,32]{1,0:T(8,128)}, u32[]{:S(2)}) copy-start(f32[96,32]{1,0:T(8,128)} %copy-done.25) | copy-start | bytes 36868
  2009.8 106.9 %copy-start.28 = (f32[96,32]{1,0:T(8,128)S(1)}, f32[96,32]{1,0:T(8,128)}, u32[]{:S(2)}) copy-start(f32[96,32]{1,0:T(8,128)} %copy-done.27) | copy-start | bytes 36868
  2009.8 106.9 %copy-start.30 = (f32[96,32]{1,0:T(8,128)S(1)}, f32[96,32]{1,0:T(8,128)}, u32[]{:S(2)}) copy-start(f32[96,32]{1,0:T(8,128)} %copy-done.29) | copy-start | bytes 36868
  2127.3 11.7 copy-start.3
  2127.3 11.7 copy-start.9
  2136.5 2.6 copy-start.6
  2147.6 106.9 %copy-start.16 = (f32[96,32]{1,0:T(8,128)S(1)}, f32[96,32]{1,0:T(8,128)}, u32[]{:S(2)}) copy-start(f32[96,32]{1,0:T(8,128)} %copy-done.15) | copy-start | bytes 36868
  2147.6 106.9 %copy-start.18 = (f32[96,32]{1,0:T(8,128)S(1)}, f32[96,32]{1,0:T(8,128)}, u32[]{:S(2)}) copy-start(f32[96,32]{1,0:T(8,128)} %copy-done.17) | copy-start | bytes 36868
  2147.6 106.9 %copy-start.20 = (f32[96,32]{1,0:T(8,128)S(1)}, f32[96,32]{1,0:T(8,128)}, u32[]{:S(2)}) copy-start(f32[96,32]{1,0:T(8,128)} %copy-done.19) | copy-start | bytes 36868
  2147.6 107.0 %copy-start.22 = (f32[96,32]{1,0:T(8,128)S(1)}, f32[96,32]{1,0:T(8,128)}, u32[]{:S(2)}) copy-start(f32[96,32]{1,0:T(8,128)} %copy-done.21) | copy-start | bytes 36868
  2277.1 128.1 %all-reduce.10.cloned.1.call-start = ((), (), s32[]{:S(2)}) async-start(), calls=%async_computation.7 | async-start | bytes 4718592 | tf_op jit(solution)/shard_map/psum | solution.py:217
  2295.4 47.2 %copy-start.42 = (f32[96]{0:T(128)S(1)}, f32[96]{0:T(128)}, u32[]{:S(2)}) copy-start(f32[96]{0:T(128)} %param.32) | copy-start | bytes 1156
Sparse Core Ops, SparseCore 0:
  199.8 218.4 all-gather.2
  617.9 482.3 reduce-scatter.6
  1118.4 217.1 all-gather.4
  1444.3 482.3 reduce-scatter.8
  1933.1 51.3 all-reduce.11
  2277.2 49.5 all-reduce.7
  2330.5 74.7 all-reduce.9
where the time goes:
time: 2430 us; the launch traced here: 2420 us
  waiting for transfers between devices  1430 us (59%)
  local copies, waits for them, and re-layouts  336 us (14%)
  other arithmetic  333 us (14%)
  matrix products  270 us (11%)
  blocking collectives  42.3 us (2%)
    reduce_scatter x1, waiting for transfers between devices, body(): lax.psum_scatter(project(jnp.int32(0), chan_count * lax.axis_size('chan')...  467 us
    reduce_scatter x1, waiting for transfers between devices, body(): lax.psum_scatter(spread_back(jnp.int32(0), chan_count * lax.axis_size('ch...  466 us
    all_gather x1, waiting for transfers between devices, body(): gathered = lax.all_gather(mixed_low[slot_item], 'chan', axis=0, tiled=True)  219 us
    all_gather x1, waiting for transfers between devices, body(): lax.all_gather(branch_low[slot_item], 'chan', axis=0, tiled=True)  217 us
    scatter-add x2, other arithmetic, toeplitz(): filter_taps[:, jnp.maximum(lag_index, 0)]  197 us
    unnamed x120, local copies, waits for them, and re-layouts  163 us
    gather x4, local copies, waits for them, and re-layouts, toeplitz(): filter_taps[:, jnp.maximum(lag_index, 0)]  126 us
    dot_general x1, matrix products, body(): jnp.einsum('cf,cp->fp', weight_in, normed_low, preferred_element_type=jnp...  71 us
  transfers between devices with their start and end apart: 7, of which 6 were waited for; matrix products, arithmetic and copies ran while one was open for 5% of the time, Pallas kernels for 0%

commit v1 on v0

--- a/solution.py
+++ b/solution.py
@@ -1,6 +1,10 @@
+import functools
+
 import jax
 import jax.numpy as jnp
 from jax import lax
+from jax.experimental import pallas as pl
+from jax.experimental.pallas import tpu as pltpu
 from jax.sharding import PartitionSpec as P
 
 eps_norm = 1e-06
@@ -57,7 +61,7 @@
     return jax.nn.gelu(values, approximate=False)
 
 
-def body(
+def plain_body(
     images,
     cotangent,
     image_sizes,
@@ -256,6 +260,632 @@
     )
 
 
+MESH = pl.DeviceIdType.MESH
+GROUP = 16
+LINES = 4
+STEP_HIDDEN = 512
+mebi = 1024 * 1024
+
+
+def dot_nn(left, right):
+    return lax.dot_general(left, right, (((1,), (0,)), ((), ())), preferred_element_type=jnp.float32)
+
+
+def dot_nt(left, right):
+    return lax.dot_general(left, right, (((1,), (1,)), ((), ())), preferred_element_type=jnp.float32)
+
+
+def split_low(values):
+    high = values.astype(jnp.bfloat16)
+    return high, (values - high.astype(jnp.float32)).astype(jnp.bfloat16)
+
+
+def lag_matrix(line, side, keep):
+    spread = pltpu.roll(jnp.broadcast_to(line, (side, side)), 0, 1, stride=1, stride_axis=0)
+    return jnp.where(keep, spread, 0.0)
+
+
+def lag_sums(matrix, side, keep):
+    turned = pltpu.roll(jnp.where(keep, matrix, 0.0), 0, 1, stride=1, stride_axis=0)
+    return jnp.sum(turned, axis=0, keepdims=True)
+
+
+def meet(n):
+    me = lax.axis_index("chan")
+    barrier = pltpu.get_barrier_semaphore()
+    for shift in range(1, n):
+        pl.semaphore_signal(
+            barrier, inc=1, device_id={"chan": lax.rem(me + shift, n)}, device_id_type=MESH
+        )
+    pl.semaphore_wait(barrier, n - 1)
+    return me
+
+
+def send_part(stage, target, me, peer, part, send_sem, recv_sem, shift):
+    return pltpu.make_async_remote_copy(
+        src_ref=stage.at[peer, part],
+        dst_ref=target.at[me, part],
+        send_sem=send_sem.at[shift],
+        recv_sem=recv_sem.at[shift],
+        device_id={"chan": peer},
+        device_id_type=MESH,
+    )
+
+
+def wait_parts(stage, target, me, n, send_sem, recv_sem):
+    for shift in range(1, n):
+        peer = lax.rem(me + shift, n)
+        origin = lax.rem(me + n - shift, n)
+        pltpu.make_async_remote_copy(
+            src_ref=stage.at[peer],
+            dst_ref=target.at[origin],
+            send_sem=send_sem.at[shift],
+            recv_sem=recv_sem.at[shift],
+            device_id={"chan": peer},
+            device_id_type=MESH,
+        ).wait()
+
+
+def mixer_kernel(
+    n,
+    sizes_ref,
+    image_ref,
+    cot_ref,
+    rows_ref,
+    cols_ref,
+    skip_ref,
+    scale_ref,
+    mixed_ref,
+    back_ref,
+    sums_ref,
+    mixed_stage,
+    back_stage,
+    wide,
+    send_m,
+    recv_m,
+    send_b,
+    recv_b,
+    own_sem,
+):
+    count, side, _ = image_ref.shape
+    parts = count // GROUP
+    block = side // n
+    me = meet(n)
+    row_at = lax.broadcasted_iota(jnp.int32, (side, side), 0)
+    col_at = lax.broadcasted_iota(jnp.int32, (side, side), 1)
+    inside = (row_at < sizes_ref[0]) & (col_at < sizes_ref[1])
+    lower = row_at >= col_at
+    upper = row_at <= col_at
+
+    def turn(stage, part):
+        @pl.loop(0, n)
+        def _(owner):
+            for line in range(block):
+                tile = wide[pl.ds(owner * block + line, GROUP, stride=side), :]
+                stage[owner, part, line] = tile.astype(jnp.bfloat16)
+
+    def send(stage, target, part, send_sem, recv_sem):
+        for shift in range(1, n):
+            send_part(stage, target, me, lax.rem(me + shift, n), part, send_sem, recv_sem, shift).start()
+
+    @pl.loop(0, parts)
+    def _(part):
+        @pl.loop(0, GROUP)
+        def _(item):
+            chan = part * GROUP + item
+            grad_out = jnp.where(inside, cot_ref[chan].astype(jnp.float32), 0.0)
+            scaled = grad_out * scale_ref[pl.ds(chan, 1), :]
+            sums_ref[pl.ds(chan, 1), :] = jnp.sum(scaled, axis=0, keepdims=True)
+            wide[pl.ds(pl.multiple_of(item * side, side), side), :] = scaled
+
+        turn(back_stage, part)
+        send(back_stage, back_ref, part, send_b, recv_b)
+
+    @pl.loop(0, parts)
+    def _(part):
+        @pl.loop(0, GROUP)
+        def _(item):
+            chan = part * GROUP + item
+            masked = jnp.where(inside, image_ref[chan].astype(jnp.float32), 0.0)
+            masked_low = masked.astype(jnp.bfloat16)
+            rows_high, rows_low = split_low(lag_matrix(rows_ref[pl.ds(chan, 1), 0, :], side, lower))
+            cols_high, cols_low = split_low(lag_matrix(cols_ref[pl.ds(chan, 1), 1, :], side, upper))
+            along = dot_nn(
+                jnp.concatenate([rows_high, rows_low], axis=1),
+                jnp.concatenate([masked_low, masked_low], axis=0),
+            )
+            along_high, along_low = split_low(along)
+            mixed = dot_nn(
+                jnp.concatenate([along_high, along_low], axis=1),
+                jnp.concatenate([cols_high, cols_high], axis=0),
+            ) + dot_nn(along_high, cols_low)
+            mixed = mixed + skip_ref[pl.ds(chan, 1), :] * masked
+            wide[pl.ds(pl.multiple_of(item * side, side), side), :] = mixed
+
+        turn(mixed_stage, part)
+        send(mixed_stage, mixed_ref, part, send_m, recv_m)
+
+    own_b = pltpu.make_async_copy(back_stage.at[me], back_ref.at[me], own_sem.at[0])
+    own_m = pltpu.make_async_copy(mixed_stage.at[me], mixed_ref.at[me], own_sem.at[1])
+    own_b.start()
+    own_m.start()
+    own_b.wait()
+    own_m.wait()
+    wait_parts(back_stage, back_ref, me, n, send_b, recv_b)
+    wait_parts(mixed_stage, mixed_ref, me, n, send_m, recv_m)
+
+
+def mixer_forward(n, sizes, images, cotangent, rows_pair, cols_pair, skip_wide, scale_wide):
+    count, side, _ = images.shape
+    shape = (n, count // GROUP, side // n, GROUP, side)
+    vmem = pl.BlockSpec(memory_space=pltpu.VMEM)
+    hbm = pl.BlockSpec(memory_space=pl.ANY)
+    return pl.pallas_call(
+        functools.partial(mixer_kernel, n),
+        out_shape=(
+            jax.ShapeDtypeStruct(shape, jnp.bfloat16),
+            jax.ShapeDtypeStruct(shape, jnp.bfloat16),
+            jax.ShapeDtypeStruct((count, side), jnp.float32),
+        ),
+        in_specs=[pl.BlockSpec(memory_space=pltpu.SMEM)] + [vmem] * 6,
+        out_specs=(hbm, hbm, vmem),
+        scratch_shapes=[
+            pltpu.VMEM(shape, jnp.bfloat16),
+            pltpu.VMEM(shape, jnp.bfloat16),
+            pltpu.VMEM((GROUP * side, side), jnp.float32),
+            pltpu.SemaphoreType.DMA((n,)),
+            pltpu.SemaphoreType.DMA((n,)),
+            pltpu.SemaphoreType.DMA((n,)),
+            pltpu.SemaphoreType.DMA((n,)),
+            pltpu.SemaphoreType.DMA((2,)),
+        ],
+        compiler_params=pltpu.CompilerParams(
+            collective_id=0, has_side_effects=True, vmem_limit_bytes=40 * mebi
+        ),
+        name="mixer_forward",
+    )(sizes, images, cotangent, rows_pair, cols_pair, skip_wide, scale_wide)
+
+
+def gelu_parts(value):
+    bell = jnp.exp(-0.5 * value * value)
+    inner = 1.0 / (1.0 + (0.3275911 * 0.7071067811865476) * jnp.abs(value))
+    series = 1.061405429 * inner - 1.453152027
+    series = series * inner + 1.421413741
+    series = series * inner - 0.284496736
+    series = series * inner + 0.254829592
+    tail = (0.5 * inner) * series * bell
+    return jnp.where(value < 0.0, tail, 1.0 - tail), bell * 0.3989422804014327
+
+
+def mlp_kernel(
+    n,
+    mixed_ref,
+    back_ref,
+    in_turned_ref,
+    in_ref,
+    out_ref,
+    out_turned_ref,
+    gain_ref,
+    shift_ref,
+    bias_ref,
+    grad_ref,
+    branch_ref,
+    active_ref,
+    before_grad_ref,
+    normed_ref,
+    cots_ref,
+    gain_grad_ref,
+    shift_grad_ref,
+    grad_stage,
+    branch_stage,
+    active_keep,
+    before_keep,
+    normed_keep,
+    cots_keep,
+    scaled_keep,
+    inverse_keep,
+    branch_sum,
+    grad_sum,
+    send_g,
+    recv_g,
+    send_r,
+    recv_r,
+    own_sem,
+    keep_sem,
+):
+    side = mixed_ref.shape[-1]
+    groups = mixed_ref.shape[1]
+    block = mixed_ref.shape[2]
+    hidden, channels = out_ref.shape
+    local = channels // n
+    steps = block // LINES
+    width = LINES * side
+    me = meet(n)
+    gain_grad_ref[...] = jnp.zeros_like(gain_grad_ref)
+    shift_grad_ref[...] = jnp.zeros_like(shift_grad_ref)
+
+    def keeps(slot, step):
+        span = pl.ds(pl.multiple_of(step * width, width), width)
+        pairs = (
+            (active_keep, active_ref),
+            (before_keep, before_grad_ref),
+            (normed_keep, normed_ref),
+            (cots_keep, cots_ref),
+        )
+        return [
+            pltpu.make_async_copy(kept.at[slot], whole.at[:, span], keep_sem.at[slot, at])
+            for at, (kept, whole) in enumerate(pairs)
+        ]
+
+    @pl.loop(0, steps)
+    def _(step):
+        slot = lax.rem(step, 2)
+
+        @pl.when(step >= 2)
+        def _():
+            for copy in keeps(slot, step - 2):
+                copy.wait()
+
+        for line in range(LINES):
+            row = step * LINES + line
+            lanes = pl.ds(line * side, side)
+            order = [(owner, group) for owner in range(n) for group in range(groups)]
+            mixed = jnp.concatenate(
+                [mixed_ref[owner, group, row].astype(jnp.float32) for owner, group in order], axis=0
+            )
+            mean = jnp.sum(mixed, axis=0, keepdims=True) * (1.0 / channels)
+            center = mixed - mean
+            var = jnp.sum(center * center, axis=0, keepdims=True) * (1.0 / channels)
+            inverse = lax.rsqrt(var + eps_norm)
+            scaled = center * inverse
+            normed_keep[slot, :, lanes] = (scaled * gain_ref[...] + shift_ref[...]).astype(jnp.bfloat16)
+            scaled_keep[:, lanes] = scaled
+            inverse_keep[:, lanes] = inverse
+            cots_keep[slot, :, lanes] = jnp.concatenate(
+                [back_ref[owner, group, row] for owner, group in order], axis=0
+            )
+
+        @pl.loop(0, hidden // STEP_HIDDEN)
+        def _(part):
+            span = pl.ds(pl.multiple_of(part * STEP_HIDDEN, STEP_HIDDEN), STEP_HIDDEN)
+            before = dot_nn(in_turned_ref[span, :], normed_keep[slot]) + bias_ref[span, :]
+            inside, bell = gelu_parts(before)
+            active = (before * inside).astype(jnp.bfloat16)
+            active_grad = dot_nn(out_ref[span, :], cots_keep[slot])
+            before_grad = (active_grad * (inside + before * bell)).astype(jnp.bfloat16)
+            active_keep[slot, span, :] = active
+            before_keep[slot, span, :] = before_grad
+            branch = dot_nn(out_turned_ref[:, span], active)
+            grad = dot_nn(in_ref[:, span], before_grad)
+
+            @pl.when(part == 0)
+            def _():
+                branch_sum[...] = branch
+                grad_sum[...] = grad
+
+            @pl.when(part > 0)
+            def _():
+                branch_sum[...] += branch
+                grad_sum[...] += grad
+
+        for copy in keeps(slot, step):
+            copy.start()
+
+        for line in range(LINES):
+            lanes = pl.ds(line * side, side)
+            grad = grad_sum[:, lanes]
+            scaled = scaled_keep[:, lanes]
+            gain_grad_ref[...] += grad * scaled
+            shift_grad_ref[...] += grad
+            weighted = grad * gain_ref[...]
+            first = jnp.sum(weighted, axis=0, keepdims=True) * (1.0 / channels)
+            second = jnp.sum(weighted * scaled, axis=0, keepdims=True) * (1.0 / channels)
+            mixed_grad = (inverse_keep[:, lanes] * (weighted - first - scaled * second)).astype(jnp.bfloat16)
+            branch = branch_sum[:, lanes].astype(jnp.bfloat16)
+            for owner in range(n):
+                grad_stage[owner, step, line] = mixed_grad[owner * local : (owner + 1) * local]
+                branch_stage[owner, step, line] = branch[owner * local : (owner + 1) * local]
+
+        for shift in range(1, n):
+            send_part(grad_stage, grad_ref, me, lax.rem(me + shift, n), step, send_g, recv_g, shift).start()
+        for shift in range(1, n):
+            send_part(branch_stage, branch_ref, me, lax.rem(me + shift, n), step, send_r, recv_r, shift).start()
+
+    own_g = pltpu.make_async_copy(grad_stage.at[me], grad_ref.at[me], own_sem.at[0])
+    own_r = pltpu.make_async_copy(branch_stage.at[me], branch_ref.at[me], own_sem.at[1])
+    own_g.start()
+    own_r.start()
+    own_g.wait()
+    own_r.wait()
+    for step in range(max(steps - 2, 0), steps):
+        for copy in keeps(step % 2, step):
+            copy.wait()
+    wait_parts(grad_stage, grad_ref, me, n, send_g, recv_g)
+    wait_parts(branch_stage, branch_ref, me, n, send_r, recv_r)
+
+
+def mlp(n, mixed, back, in_turned, in_full, out_full, out_turned, gain, shift, bias):
+    _, groups, block, group, side = mixed.shape
+    hidden, channels = out_full.shape
+    local = channels // n
+    pixels = block * side
+    width = LINES * side
+    shape = (n, block // LINES, LINES, local, side)
+    vmem = pl.BlockSpec(memory_space=pltpu.VMEM)
+    hbm = pl.BlockSpec(memory_space=pl.ANY)
+    return pl.pallas_call(
+        functools.partial(mlp_kernel, n),
+        out_shape=(
+            jax.ShapeDtypeStruct(shape, jnp.bfloat16),
+            jax.ShapeDtypeStruct(shape, jnp.bfloat16),
+            jax.ShapeDtypeStruct((hidden, pixels), jnp.bfloat16),
+            jax.ShapeDtypeStruct((hidden, pixels), jnp.bfloat16),
+            jax.ShapeDtypeStruct((channels, pixels), jnp.bfloat16),
+            jax.ShapeDtypeStruct((channels, pixels), jnp.bfloat16),
+            jax.ShapeDtypeStruct((channels, side), jnp.float32),
+            jax.ShapeDtypeStruct((channels, side), jnp.float32),
+        ),
+        in_specs=[vmem] * 9,
+        out_specs=(hbm,) * 6 + (vmem, vmem),
+        scratch_shapes=[
+            pltpu.VMEM(shape, jnp.bfloat16),
+            pltpu.VMEM(shape, jnp.bfloat16),
+            pltpu.VMEM((2, hidden, width), jnp.bfloat16),
+            pltpu.VMEM((2, hidden, width), jnp.bfloat16),
+            pltpu.VMEM((2, channels, width), jnp.bfloat16),
+            pltpu.VMEM((2, channels, width), jnp.bfloat16),
+            pltpu.VMEM((channels, width), jnp.float32),
+            pltpu.VMEM((1, width), jnp.float32),
+            pltpu.VMEM((channels, width), jnp.float32),
+            pltpu.VMEM((channels, width), jnp.float32),
+            pltpu.SemaphoreType.DMA((n,)),
+            pltpu.SemaphoreType.DMA((n,)),
+            pltpu.SemaphoreType.DMA((n,)),
+            pltpu.SemaphoreType.DMA((n,)),
+            pltpu.SemaphoreType.DMA((2,)),
+            pltpu.SemaphoreType.DMA((2, 4)),
+        ],
+        compiler_params=pltpu.CompilerParams(
+            collective_id=1, has_side_effects=True, vmem_limit_bytes=63 * mebi
+        ),
+        name="mlp",
+    )(mixed, back, in_turned, in_full, out_full, out_turned, gain, shift, bias)
+
+
+def back_kernel(
+    sizes_ref,
+    image_ref,
+    cot_ref,
+    grad_ref,
+    branch_ref,
+    rows_ref,
+    cols_ref,
+    skip_ref,
+    scale_ref,
+    bias_ref,
+    output_ref,
+    input_grad_ref,
+    rows_sums_ref,
+    cols_sums_ref,
+    skip_sums_ref,
+    scale_sums_ref,
+    grad_wide,
+    branch_wide,
+):
+    count, side, _ = image_ref.shape
+    row_at = lax.broadcasted_iota(jnp.int32, (side, side), 0)
+    col_at = lax.broadcasted_iota(jnp.int32, (side, side), 1)
+    inside = (row_at < sizes_ref[0]) & (col_at < sizes_ref[1])
+    lower = row_at >= col_at
+    upper = row_at <= col_at
+    flip = (row_at + col_at == side - 1).astype(jnp.bfloat16)
+
+    @pl.loop(0, side)
+    def _(row):
+        span = pl.ds(pl.multiple_of(row * count, count), count)
+        grad_wide[span, :] = grad_ref[row].astype(jnp.float32)
+        branch_wide[span, :] = branch_ref[row].astype(jnp.float32)
+
+    @pl.loop(0, count)
+    def _(chan):
+        one = pl.ds(chan, 1)
+        grad = grad_wide[pl.ds(chan, side, stride=count), :]
+        branch = branch_wide[pl.ds(chan, side, stride=count), :]
+        image = image_ref[chan].astype(jnp.float32)
+        grad_out = jnp.where(inside, cot_ref[chan].astype(jnp.float32), 0.0)
+        shifted = branch + bias_ref[one, :]
+        output_ref[chan] = jnp.where(inside, image + scale_ref[one, :] * shifted, 0.0).astype(jnp.bfloat16)
+        scale_sums_ref[one, :] = jnp.sum(grad_out * shifted, axis=0, keepdims=True)
+        masked = jnp.where(inside, image, 0.0)
+        skip_sums_ref[one, :] = jnp.sum(grad * masked, axis=0, keepdims=True)
+        masked_low = masked.astype(jnp.bfloat16)
+        grad_low = grad.astype(jnp.bfloat16)
+        grad_turned = dot_nt(flip, grad_low).astype(jnp.bfloat16)
+        masked_turned = dot_nn(flip, masked_low).astype(jnp.bfloat16)
+        rows_high, rows_low = split_low(lag_matrix(rows_ref[one, 0, :], side, lower))
+        turned_high, turned_low = split_low(lag_matrix(rows_ref[one, 1, :], side, upper))
+        cols_high, cols_low = split_low(lag_matrix(cols_ref[one, 0, :], side, lower))
+        along = dot_nn(
+            jnp.concatenate([rows_high, rows_low], axis=1),
+            jnp.concatenate([masked_low, masked_low], axis=0),
+        )
+        along_grad = dot_nn(
+            jnp.concatenate([grad_low, grad_low], axis=1),
+            jnp.concatenate([cols_high, cols_low], axis=0),
+        )
+        along_high, along_low = split_low(along)
+        grad_high, grad_rest = split_low(along_grad)
+        cols_grad = dot_nn(
+            jnp.concatenate([grad_turned, grad_turned], axis=1),
+            jnp.concatenate([along_high, along_low], axis=0),
+        )
+        rows_grad = dot_nt(
+            jnp.concatenate([grad_high, grad_rest], axis=1),
+            jnp.concatenate([masked_turned, masked_turned], axis=1),
+        )
+        masked_grad = dot_nn(
+            jnp.concatenate([turned_high, turned_low], axis=1),
+            jnp.concatenate([grad_high, grad_high], axis=0),
+        ) + dot_nn(turned_high, grad_rest)
+        masked_grad = masked_grad + skip_ref[one, :] * grad
+        input_grad_ref[chan] = jnp.where(inside, grad_out + masked_grad, 0.0)
+        rows_sums_ref[one, :] = lag_sums(rows_grad, side, row_at + col_at >= side - 1)
+        cols_sums_ref[one, :] = lag_sums(cols_grad, side, row_at + col_at <= side - 1)
+
+
+def mixer_back(sizes, images, cotangent, grad, branch, rows_pair, cols_pair, skip_wide, scale_wide, bias_wide):
+    count, side, _ = images.shape
+    line = jax.ShapeDtypeStruct((count, side), jnp.float32)
+    vmem = pl.BlockSpec(memory_space=pltpu.VMEM)
+    return pl.pallas_call(
+        back_kernel,
+        out_shape=(
+            jax.ShapeDtypeStruct(images.shape, jnp.bfloat16),
+            jax.ShapeDtypeStruct(images.shape, jnp.float32),
+            line,
+            line,
+            line,
+            line,
+        ),
+        in_specs=[pl.BlockSpec(memory_space=pltpu.SMEM)] + [vmem] * 9,
+        out_specs=(vmem,) * 6,
+        scratch_shapes=[
+            pltpu.VMEM((count * side, side), jnp.float32),
+            pltpu.VMEM((count * side, side), jnp.float32),
+        ],
+        compiler_params=pltpu.CompilerParams(vmem_limit_bytes=60 * mebi),
+        name="mixer_back",
+    )(sizes, images, cotangent, grad, branch, rows_pair, cols_pair, skip_wide, scale_wide, bias_wide)
+
+
+def lag_pair(taps):
+    return jnp.stack([jnp.roll(taps[:, ::-1], 1, axis=1), taps], axis=1)
+
+
+def pixel_body(
+    n,
+    images,
+    cotangent,
+    image_sizes,
+    slot_image,
+    rows_rate,
+    rows_freq,
+    rows_real,
+    rows_imag,
+    cols_rate,
+    cols_freq,
+    cols_real,
+    cols_imag,
+    skip_gain,
+    norm_gain,
+    norm_bias,
+    weight_in,
+    bias_in,
+    weight_out,
+    bias_out,
+    layer_scale,
+):
+    _, count, side, _ = images.shape
+    channels = norm_gain.shape[0]
+    picked = slot_image[lax.axis_index("dp")]
+    sizes = image_sizes[picked]
+    image, cot = images[0], cotangent[0]
+
+    def both_taps(*params):
+        return kernel_taps(*params[:4], side), kernel_taps(*params[4:], side)
+
+    (rows_taps, cols_taps), taps_pull = jax.vjp(
+        both_taps,
+        rows_rate,
+        rows_freq,
+        rows_real,
+        rows_imag,
+        cols_rate,
+        cols_freq,
+        cols_real,
+        cols_imag,
+    )
+    rows_pair, cols_pair = lag_pair(rows_taps), lag_pair(cols_taps)
+    skip_wide = jnp.broadcast_to(skip_gain[:, None], (count, side))
+    scale_wide = jnp.broadcast_to(layer_scale[:, None], (count, side))
+    bias_wide = jnp.broadcast_to(bias_out[:, None], (count, side))
+
+    in_turned = lax.all_gather(weight_in.T, "chan", axis=0, tiled=True)
+    out_full = lax.all_gather(weight_out, "chan", axis=0, tiled=True)
+    bias_full = lax.all_gather(bias_in, "chan", axis=0, tiled=True).astype(jnp.float32)
+
+    mixed, back, bias_out_sums = mixer_forward(
+        n, sizes, image, cot, rows_pair, cols_pair, skip_wide, scale_wide
+    )
+    grad, branch, active, before_grad, normed, cots, gain_sums, shift_sums = mlp(
+        n,
+        mixed,
+        back,
+        in_turned,
+        in_turned.T,
+        out_full,
+        out_full.T,
+        jnp.broadcast_to(norm_gain[:, None], (channels, side)),
+        jnp.broadcast_to(norm_bias[:, None], (channels, side)),
+        bias_full[:, None],
+    )
+    out_weight_grad = lax.psum_scatter(dot_nt(active, cots), "chan", scatter_dimension=0, tiled=True)
+    in_weight_grad = lax.psum_scatter(dot_nt(before_grad, normed), "chan", scatter_dimension=0, tiled=True)
+    in_bias_grad = lax.psum_scatter(
+        jnp.sum(before_grad.astype(jnp.float32), axis=1), "chan", scatter_dimension=0, tiled=True
+    )
+    output, input_grad, rows_sums, cols_sums, skip_sums, scale_sums = mixer_back(
+        sizes,
+        image,
+        cot,
+        grad.reshape(side, count, side),
+        branch.reshape(side, count, side),
+        rows_pair,
+        cols_pair,
+        skip_wide,
+        scale_wide,
+        bias_wide,
+    )
+    params_grad = taps_pull(
+        (jnp.roll(rows_sums, 1, axis=1), cols_sums[:, ::-1])
+    )
+    in_weight_grad, out_weight_grad = lax.psum((in_weight_grad, out_weight_grad), "dp")
+    small = lax.psum(
+        (
+            *params_grad,
+            jnp.sum(skip_sums, axis=1),
+            in_bias_grad,
+            jnp.sum(bias_out_sums, axis=1),
+            jnp.sum(scale_sums, axis=1),
+        ),
+        "dp",
+    )
+    norm_sums = lax.psum((jnp.sum(gain_sums, axis=1), jnp.sum(shift_sums, axis=1)), ("dp", "chan"))
+    return (
+        output[None],
+        input_grad[None],
+        *small[:9],
+        *norm_sums,
+        in_weight_grad.T,
+        small[9],
+        out_weight_grad,
+        small[10],
+        small[11],
+    )
+
+
+def choose_body(n, images, *rest):
+    slots, count, side, _ = images.shape
+    fits = (
+        slots == 1
+        and side == 128
+        and count % GROUP == 0
+        and side % (n * LINES) == 0
+        and (rest[15].shape[0] * n) % STEP_HIDDEN == 0
+    )
+    return pixel_body(n, images, *rest) if fits else plain_body(images, *rest)
+
+
 def solution(mesh):
     in_specs = (
         P("dp", "chan", None, None),
@@ -299,4 +929,4 @@
         P("chan"),
         P("chan"),
     )
-    return jax.shard_map(body, mesh=mesh, in_specs=in_specs, out_specs=out_specs, check_vma=False)
+    return jax.shard_map(functools.partial(choose_body, mesh.shape["chan"]), mesh=mesh, in_specs=in_specs, out_specs=out_specs, check_vma=False)

time: 2430 us -> 781 us (0.32)
  waiting for transfers between devices: 1430 us -> 146 us
  Pallas kernels: 0 us -> 413 us
  other arithmetic: 333 us -> 43.5 us
  local copies, waits for them, and re-layouts: 336 us -> 49.2 us
  matrix products: 270 us -> 32.4 us
  blocking collectives: 42.3 us -> 76 us
    reduce_scatter x2, waiting for transfers between devices: 932 us -> 67.7 us  [the longest x1 67.6 us: pixel_body(): lax.psum_scatter(dot_nt(before_grad, normed), 'chan', scatter_dimension=0...]
    all_gather x2, waiting for transfers between devices: 436 us -> 0.01 us  [the longest x1 0.01 us: pixel_body(): out_full = lax.all_gather(weight_out, 'chan', axis=0, tiled=True)]
    pallas_call x0 -> x3, Pallas kernels: none -> 413 us  [the longest x1 186 us: mixer_forward(): pl.pallas_call(functools.partial(mixer_kernel, n), out_shape=(jax.ShapeDt...]
    dot_general x12 -> x2, matrix products: 270 us -> 32.4 us  [dot_nt(): lax.dot_general(left, right, (((1,), (1,)), ((), ())), preferred_element_...]
    scatter-add x2 -> x0, other arithmetic: 197 us -> none  [toeplitz(): filter_taps[:, jnp.maximum(lag_index, 0)]]
    unnamed x120 -> x98, local copies, waits for them, and re-layouts: 163 us -> 29.6 us
    gather x4 -> x0, local copies, waits for them, and re-layouts: 126 us -> none  [toeplitz(): filter_taps[:, jnp.maximum(lag_index, 0)]]
    reduce_sum x8 -> x6, other arithmetic: 60.8 us -> 8.65 us  [the longest x1 6.43 us: pixel_body(): jnp.sum(before_grad.astype(jnp.float32), axis=1)]
  transfers between devices with their start and end apart: 7 -> 6, of which waited for: 6 -> 3; matrix products, arithmetic and copies ran while one was open for 5% -> 11% of each run, Pallas kernels for 0% -> 32%
where the time goes in v1:
time: 781 us; the launch traced here: 778 us
  Pallas kernels  413 us (53%)
  waiting for transfers between devices  146 us (19%)
  blocking collectives  76 us (10%)
  local copies, waits for them, and re-layouts  49.2 us (6%)
  other arithmetic  43.5 us (6%)
  matrix products  32.4 us (4%)
  between operations  17.2 us (2%)
    pallas_call x1, Pallas kernels, mixer_forward(): pl.pallas_call(functools.partial(mixer_kernel, n), out_shape=(jax.ShapeDt...  186 us
    pallas_call x1, Pallas kernels, mlp(): pl.pallas_call(functools.partial(mlp_kernel, n), out_shape=(jax.ShapeDtyp...  167 us
    reduce_scatter x1, waiting for transfers between devices, pixel_body(): lax.psum_scatter(dot_nt(before_grad, normed), 'chan', scatter_dimension=0...  67.6 us
    psum x1, waiting for transfers between devices, pixel_body(): lax.psum((in_weight_grad, out_weight_grad), 'dp')  65.9 us
    pallas_call x1, Pallas kernels, mixer_back(): pl.pallas_call(back_kernel, out_shape=(jax.ShapeDtypeStruct(images.shape,...  59.6 us
    psum x1, blocking collectives, pixel_body(): lax.psum((jnp.sum(gain_sums, axis=1), jnp.sum(shift_sums, axis=1)), ('dp'...  40.8 us
    dot_general x2, matrix products, dot_nt(): lax.dot_general(left, right, (((1,), (1,)), ((), ())), preferred_element_...  32.4 us
    unnamed x98, local copies, waits for them, and re-layouts  29.6 us
  transfers between devices with their start and end apart: 6, of which 3 were waited for; matrix products, arithmetic and copies ran while one was open for 11% of the time, Pallas kernels for 32%

profile of v1, /device:TPU:9, one launch (start us, length us, event | category | flops | bytes accessed | tf_op | source)
XLA Modules:
  0.0 777.9 jit_solution(17937632881963207564)
XLA Ops:
  7.3 2.1 copy.90
  9.5 0.7 all-gather.4.cloned.1.call-update
  10.3 0.6 dynamic_slice.6
  12.2 0.1 copy.86
  12.3 0.1 copy.87
  12.4 0.1 copy.88
  12.5 0.1 copy.89
  12.6 6.8 multiply_reduce_fusion.8
  19.6 0.1 copy.82
  19.7 0.1 copy.83
  19.8 0.1 copy.84
  19.9 0.1 copy.85
  20.0 6.8 multiply_reduce_fusion.9
  27.0 13.6 %all-gather = bf16[8,1,384]{2,1,0:T(2,128)(2,1)S(1)} all-gather(bf16[1,1,384]{2,1,0:T(2,128)(2,1)S(1)} %reshape.86), channel_id=1, replica_groups=mesh['dp'=4,'chan'=8] {'chan'}, dimensions={0}, use_global_device_ids=true | all-gather | bytes 6912 | tf_op jit(solution)/shard_map/all_gather | solution.py:815
  40.6 1.5 copy.93.bias_ref
  42.7 0.2 dynamic-slice_reduce_fusion.sizes_ref
  43.1 0.2 pad_maximum_fusion
  43.5 1.9 copy-done.2
  45.4 2.0 copy-done.3
  47.4 186.3 %mixer_forward.1 = (bf16[8,6,16,16,128]{4,3,2,1,0:T(8,128)(2,1)S(1)}, bf16[8,6,16,16,128]{4,3,2,1,0:T(8,128)(2,1)S(1)}, f32[96,128]{1,0:T(8,128)S(1)}) custom-call(s32[2]{0:T(128)S(1)} %dynamic-slice_reduce_fusion.sizes_ref, bf16[96,128,128]{2,1,0:T(8,128)(2,1)S(1)} %bitcast.26, bf16[96,128,128]{2,1,0:T(8,128)(2,1)S(1)} %bitcast.28, ...), custom_call_target="tpu_custom_call" | custom-call | tf_op jit(solution)/shard_map/mixer_forward/pallas_call | solution.py:423
  233.7 1.7 copy-done.4
  235.4 1.7 copy-done.5
  237.1 6.6 copy.92.out_ref
  243.7 6.6 copy.91.in_turned_ref
  250.4 0.9 broadcast_in_dim.24.gain_ref
  251.3 0.9 broadcast_in_dim.25.shift_ref
  252.2 167.0 %mlp.1 = (bf16[8,4,4,96,128]{4,3,2,1,0:T(8,128)(2,1)}, bf16[8,4,4,96,128]{4,3,2,1,0:T(8,128)(2,1)}, bf16[3072,2048]{1,0:T(8,128)(2,1)}, bf16[3072,2048]{1,0:T(8,...) custom-call(bf16[8,6,16,16,128]{4,3,2,1,0:T(8,128)(2,1)} %copy-done., ...), custom_call_target="tpu_custom_call" | custom-call | tf_op jit(solution)/shard_map/mlp/pallas_call | solution.py:616
  419.2 16.1 %fusion.9 = f32[3072,768]{1,0:T(8,128)} fusion(bf16[3072,2048]{1,0:T(8,128)(2,1)} %get-tuple-element.48, bf16[768,2048]{1,0:T(8,128)(2,1)} %get-tuple-element.49), kind=kOutput, calls=%fused_computation.32 | convolution fusion | flops 9663676416 | bytes 25165824 | tf_op jit(solution)/shard_map/dot_general | solution.py:275
  435.4 16.3 %fusion.8 = f32[3072,768]{1,0:T(8,128)} fusion(bf16[3072,2048]{1,0:T(8,128)(2,1)} %get-tuple-element.46, bf16[768,2048]{1,0:T(8,128)(2,1)} %get-tuple-element.47), kind=kOutput, calls=%fused_computation.31 | convolution fusion | flops 9663676416 | bytes 25165824 | tf_op jit(solution)/shard_map/dot_general | solution.py:275
  451.8 0.6 copy-done.36
  452.4 0.6 dynamic-slice
  453.6 0.6 reduce_sum.163
  454.2 0.7 broadcast_in_dim.28.bias_ref
  454.9 59.6 %mixer_back.1 = (bf16[96,128,128]{2,1,0:T(8,128)(2,1)}, f32[96,128,128]{2,1,0:T(8,128)}, f32[96,128]{1,0:T(8,128)}, f32[96,128]{1,0:T(8,128)}, f32[96,128]{1,0:T(8,128)}, /*index=5*/f32[96,128]{1,0:T(8,128)}) custom-call(s32[2]{0:T(128)} %copy-done.10, bf16[96,128,128]{2,1,0:T(8,128)(2,1)} %bitcast.25, bf16[96,128,128]{2,1,0:T(8,128)(2,1)} %bitcast.27, ...), custom_call_target="tpu_custom_call" | custom-call | tf_op jit(solution)/shard_map/mixer_back/pallas_call | solution.py:740
  514.5 0.9 rev.2
  515.4 9.8 %multiply_reduce_fusion = (f32[96,32]{1,0:T(8,128)}, f32[96,32]{1,0:T(8,128)}, f32[96,32]{1,0:T(8,128)S(1)}, f32[96,32]{1,0:T(8,128)}) fusion(f32[96,128]{1,0:T(8,128)S(1)} %rev.2, f32[96,32]{1,0:T(8,128)S(1)} %copy.88, f32[96,32]{1,0:T(8,128)S(1)} %copy.86, f32[96,32]{1,0:T(8,128)S(1)} %copy.89, f32[96,32]{1,0:T(8,128)S(1)} %copy.87), kind=kLoop, calls=%fused_computation.1 | loop fusion | flops 9031680 | bytes 147456 | tf_op jit(solution)/shard_map/transpose(jvp())/reduce_sum | solution.py:20
  525.2 0.6 neg.37
  526.0 9.8 %multiply_reduce_fusion.4 = (f32[96,32]{1,0:T(8,128)}, f32[96,32]{1,0:T(8,128)}, f32[96,32]{1,0:T(8,128)S(1)}, f32[96,32]{1,0:T(8,128)}) fusion(f32[96,128]{1,0:T(8,128)S(1)} %pad_maximum_fusion.4, f32[96,32]{1,0:T(8,128)S(1)} %copy.84, f32[96,32]{1,0:T(8,128)S(1)} %copy.82, f32[96,32]{1,0:T(8,128)S(1)} %copy.85, f32[96,32]{1,0:T(8,128)S(1)} %copy.83), kind=kLoop, calls=%fused_computation.5 | loop fusion | flops 9031680 | bytes 147456 | tf_op jit(solution)/shard_map/transpose(jvp())/reduce_sum | solution.py:20
  535.8 0.6 neg.34
  536.4 0.6 reduce_sum.156
  537.0 0.6 reduce_sum.167
  537.7 6.4 convert_reduce_fusion
  544.1 21.5 %all-reduce = f32[3072]{0:T(1024)S(1)} all-reduce(f32[3072]{0:T(1024)S(1)} %convert_reduce_fusion), channel_id=3, replica_groups=mesh['dp'=4,'chan'=8] {'chan'}, use_global_device_ids=true, to_apply=%region_27.28.clone | all-reduce | flops 3072 | bytes 24576
  565.6 0.7 dynamic-slice.1
  566.4 67.6 %reduce-scatter.3.cloned.1.call-done = f32[384,768]{1,0:T(8,128)} async-done(((f32[3072,768]{1,0:T(8,128)}), f32[384,768]{1,0:T(8,128)}) %reduce-scatter.3.cloned.1.call-update) | async-done | bytes 1179664 | tf_op jit(solution)/shard_map/reduce_scatter | solution.py:833
  634.1 0.2 reduce_sum.160
  634.2 0.2 reduce_sum.161
  634.4 40.8 %all-reduce.1 = (f32[768]{0:T(1024)}, f32[768]{0:T(1024)}) all-reduce(f32[768]{0:T(1024)S(1)} %reduce_sum.160, f32[768]{0:T(1024)S(1)} %reduce_sum.161), channel_id=1, replica_groups=mesh['dp'=4,'chan'=8] {'dp','chan'}, use_global_device_ids=true, to_apply=%region_21.22 | all-reduce | flops 1536 | bytes 12288 | tf_op jit(solution)/shard_map/psum | solution.py:863
  675.3 12.2 %all-reduce.7.cloned.1.call-done = (f32[96,32]{1,0:T(8,128)}, f32[96,32]{1,0:T(8,128)}, f32[96,32]{1,0:T(8,128)}, f32[96,32]{1,0:T(8,128)}, f32[96,32]{1,0:T(8,1...) async-done(((f32[96,32]{1,0:T(8,128)}, f32[96,32]{1,0:T(8,128)}, ...) | async-done | bytes 101008 | tf_op jit(solution)/shard_map/psum | solution.py:853
  687.5 1.5 copy.100
  688.9 1.5 copy.101
  690.4 1.5 copy.94
  691.9 1.5 copy.95
  693.4 1.5 copy.96
  694.9 1.5 copy.97
  696.3 1.5 copy.98
  697.8 1.5 copy.99
  699.3 65.9 %all-reduce.9.cloned.1.call-done = (f32[768,384]{0,1:T(8,128)}, f32[384,768]{1,0:T(8,128)}) async-done(((f32[768,384]{0,1:T(8,128)}, f32[384,768]{1,0:T(8,128)}), (f32[768,384]{0,1:T(8,128)}, f32[384,768]{1,0:T(8,128)})) %all-reduce.9.cloned.1.call-update) | async-done | bytes 2359312 | tf_op jit(solution)/shard_map/psum | solution.py:852
  765.2 2.7 copy.102
  767.9 0.5 copy.117
  768.4 0.6 copy.118
  769.0 1.0 copy.119
  770.0 0.5 copy.120
  770.6 0.5 copy.121
  (96 shorter events, 1.3 us)
Async XLA Ops:
  7.2 35.5 %copy-start = (s32[4,2]{0,1:T(2,128)S(1)}, s32[4,2]{0,1:T(2,128)}, u32[]{:S(2)}) copy-start(s32[4,2]{0,1:T(2,128)} %param.22) | copy-start | bytes 100
  7.2 3.1 copy-start.32
  7.2 5.0 copy-start.17
  7.2 5.1 copy-start.19
  7.2 5.1 copy-start.20
  7.2 5.2 copy-start.21
  7.3 229.8 %all-gather.6.cloned.1.call-start = ((), (), s32[]{:S(2)}) async-start(), calls=%async_computation.3 | async-start | bytes 5308416 | tf_op jit(solution)/shard_map/all_gather | solution.py:814
  9.4 234.3 %all-gather.4.cloned.1.call-start = ((), (), s32[]{:S(2)}) async-start(), calls=%async_computation.2 | async-start | bytes 5308416 | tf_op jit(solution)/shard_map/all_gather | solution.py:813
  9.5 10.1 %copy-start.18 = (f32[96,32]{0,1:T(8,128)S(1)}, f32[96,32]{0,1:T(8,128)}, u32[]{:S(2)}) copy-start(f32[96,32]{0,1:T(8,128)} %param.24) | copy-start | bytes 36868
  9.5 10.2 %copy-start.22 = (f32[96,32]{0,1:T(8,128)S(1)}, f32[96,32]{0,1:T(8,128)}, u32[]{:S(2)}) copy-start(f32[96,32]{0,1:T(8,128)} %param.26) | copy-start | bytes 36868
  10.2 9.6 %copy-start.23 = (f32[96,32]{0,1:T(8,128)S(1)}, f32[96,32]{0,1:T(8,128)}, u32[]{:S(2)}) copy-start(f32[96,32]{0,1:T(8,128)} %param.25) | copy-start | bytes 36868
  10.2 9.7 %copy-start.24 = (f32[96,32]{0,1:T(8,128)S(1)}, f32[96,32]{0,1:T(8,128)}, u32[]{:S(2)}) copy-start(f32[96,32]{0,1:T(8,128)} %param.27) | copy-start | bytes 36868
  10.2 556.2 %reduce-scatter.5.cloned.1.call-start = ((), (), s32[]{:S(2)}) async-start(), calls=%async_computation.5 | async-start | bytes 10616832 | tf_op jit(solution)/shard_map/reduce_scatter | solution.py:832
  19.4 7.6 copy-start.28
  26.8 16.5 %copy-start.29 = (f32[96]{0:T(128)S(1)}, f32[96]{0:T(128)}, u32[]{:S(2)}) copy-start(f32[96]{0:T(128)} %param.32) | copy-start | bytes 1156
  26.8 16.6 %copy-start.30 = (f32[96]{0:T(128)S(1)}, f32[96]{0:T(128)}, u32[]{:S(2)}) copy-start(f32[96]{0:T(128)} %param.39) | copy-start | bytes 1156
  42.9 190.7 %copy-start.10 = (s32[2]{0:T(128)}, s32[2]{0:T(128)S(1)}, u32[]{:S(2)}) copy-start(s32[2]{0:T(128)S(1)} %dynamic-slice_reduce_fusion.sizes_ref) | copy-start | bytes 28
  43.3 190.4 %copy-start.6 = (f32[96,2,128]{2,1,0:T(2,128)}, f32[96,2,128]{2,1,0:T(2,128)S(1)}, u32[]{:S(2)}) copy-start(f32[96,2,128]{2,1,0:T(2,128)S(1)} %get-tuple-element.152.rows_ref) | copy-start | bytes 294916
  43.3 190.4 %copy-start.7 = (f32[96,2,128]{2,1,0:T(2,128)}, f32[96,2,128]{2,1,0:T(2,128)S(1)}, u32[]{:S(2)}) copy-start(f32[96,2,128]{2,1,0:T(2,128)S(1)} %get-tuple-element.153.cols_ref) | copy-start | bytes 294916
  43.4 190.3 %copy-start.8 = (f32[96,128]{1,0:T(8,128)}, f32[96,128]{1,0:T(8,128)S(1)}, u32[]{:S(2)}) copy-start(f32[96,128]{1,0:T(8,128)S(1)} %broadcast_in_dim.22.skip_ref) | copy-start | bytes 147460
  43.5 190.2 %copy-start.9 = (f32[96,128]{1,0:T(8,128)}, f32[96,128]{1,0:T(8,128)S(1)}, u32[]{:S(2)}) copy-start(f32[96,128]{1,0:T(8,128)S(1)} %broadcast_in_dim.23.scale_ref) | copy-start | bytes 147460
  43.5 1.9 copy-start.2
  45.4 2.0 copy-start.3
  233.7 1.7 copy-start.4
  235.4 1.7 copy-start.5
  243.7 6.6 copy-start.25
  243.7 7.6 copy-start.26
  435.3 198.7 %reduce-scatter.3.cloned.1.call-start = ((), (), s32[]{:S(2)}) async-start(), calls=%async_computation.4 | async-start | bytes 10616832 | tf_op jit(solution)/shard_map/reduce_scatter | solution.py:833
  451.7 0.7 copy-start.36
  451.7 2.5 copy-start.31
  451.7 235.7 %all-reduce.7.cloned.1.call-start = ((), (), s32[]{:S(2)}) async-start(), calls=%async_computation.6 | async-start | bytes 793600 | tf_op jit(solution)/shard_map/psum | solution.py:853
  514.5 11.3 %copy-start.14 = (f32[96,128]{1,0:T(8,128)S(1)}, f32[96,128]{1,0:T(8,128)}, u32[]{:S(2)}) copy-start(f32[96,128]{1,0:T(8,128)} %get-tuple-element.41) | copy-start | bytes 147460
  525.2 11.2 %copy-start.16 = (f32[96,128]{1,0:T(8,128)S(1)}, f32[96,128]{1,0:T(8,128)}, u32[]{:S(2)}) copy-start(f32[96,128]{1,0:T(8,128)} %get-tuple-element.43) | copy-start | bytes 147460
  525.2 11.8 %copy-start.15 = (f32[96,128]{1,0:T(8,128)S(1)}, f32[96,128]{1,0:T(8,128)}, u32[]{:S(2)}) copy-start(f32[96,128]{1,0:T(8,128)} %get-tuple-element.51) | copy-start | bytes 147460
  544.1 90.0 %copy-start.13 = (f32[768,128]{1,0:T(8,128)S(1)}, f32[768,128]{1,0:T(8,128)}, u32[]{:S(2)}) copy-start(f32[768,128]{1,0:T(8,128)} %get-tuple-element.44) | copy-start | bytes 1179652
  566.3 68.0 %copy-start.12 = (f32[768,128]{1,0:T(8,128)S(1)}, f32[768,128]{1,0:T(8,128)}, u32[]{:S(2)}) copy-start(f32[768,128]{1,0:T(8,128)} %get-tuple-element.45) | copy-start | bytes 1179652
  566.3 198.9 %all-reduce.9.cloned.1.call-start = ((), (), s32[]{:S(2)}) async-start(), calls=%async_computation.7 | async-start | bytes 4718592 | tf_op jit(solution)/shard_map/psum | solution.py:852
  687.5 80.5 %copy-start.35 = (f32[96]{0:T(128)S(1)}, f32[96]{0:T(128)}, u32[]{:S(2)}) copy-start(f32[96]{0:T(128)} %get-tuple-element.164) | copy-start | bytes 1156
  687.5 81.0 %copy-start.27 = (f32[384]{0:T(512)S(1)}, f32[384]{0:T(512)}, u32[]{:S(2)}) copy-start(f32[384]{0:T(512)} %get-tuple-element.168) | copy-start | bytes 4612
  765.2 3.9 copy-start.11
  765.2 5.9 copy-start.1
  767.9 2.1 copy-start.34
  767.9 2.6 copy-start.33
Sparse Core Ops, SparseCore 0:
  10.3 59.4 all-gather.5
  71.4 111.6 all-gather.3
  435.4 97.8 reduce-scatter.4
  535.5 98.4 reduce-scatter.2
  639.3 48.1 all-reduce.6
  690.8 74.3 all-reduce.8

commit v2 on v1

--- a/solution.py
+++ b/solution.py
@@ -275,6 +275,10 @@
     return lax.dot_general(left, right, (((1,), (1,)), ((), ())), preferred_element_type=jnp.float32)
 
 
+def dot_tn(left, right):
+    return lax.dot_general(left, right, (((0,), (0,)), ((), ())), preferred_element_type=jnp.float32)
+
+
 def split_low(values):
     high = values.astype(jnp.bfloat16)
     return high, (values - high.astype(jnp.float32)).astype(jnp.bfloat16)
@@ -290,15 +294,130 @@
     return jnp.sum(turned, axis=0, keepdims=True)
 
 
-def meet(n):
-    me = lax.axis_index("chan")
+cos_terms = (
+    1.0, -19.7392087, 64.9393891, -85.4566583, 60.242131, -26.4046662, 7.8001253, -1.45310477
+)
+sin_terms = (6.2831853, -41.3417004, 81.6051314, -76.703015, 42.0259236, -14.8998335, 3.23811835)
+
+
+def polynomial(terms, at):
+    value = terms[-1]
+    for term in terms[-2::-1]:
+        value = value * at + term
+    return value
+
+
+def taps_tile(rate, freq, real, imag, lag):
+    turns = freq * 0.15915494309189535
+    total = jnp.zeros((rate.shape[0], lag.shape[1]), jnp.float32)
+    for mode in range(rate.shape[1]):
+        one = slice(mode, mode + 1)
+        angle = turns[:, one] * lag
+        angle = angle - jnp.floor(angle + 0.5)
+        square = angle * angle
+        wave = real[:, one] * polynomial(cos_terms, square)
+        wave = wave - (imag[:, one] * angle) * polynomial(sin_terms, square)
+        total = total + jnp.exp(-rate[:, one] * lag) * wave
+    return total
+
+
+def meet(n, shares):
+    me, share = lax.axis_index("chan"), lax.axis_index("dp")
     barrier = pltpu.get_barrier_semaphore()
     for shift in range(1, n):
         pl.semaphore_signal(
             barrier, inc=1, device_id={"chan": lax.rem(me + shift, n)}, device_id_type=MESH
         )
-    pl.semaphore_wait(barrier, n - 1)
-    return me
+    for shift in range(1, shares):
+        pl.semaphore_signal(
+            barrier, inc=1, device_id={"dp": lax.rem(share + shift, shares)}, device_id_type=MESH
+        )
+    pl.semaphore_wait(barrier, n + shares - 2)
+    return me, share
+
+
+def push(source, target, send_sem, recv_sem, **peer):
+    return pltpu.make_async_remote_copy(
+        src_ref=source,
+        dst_ref=target,
+        send_sem=send_sem,
+        recv_sem=recv_sem,
+        device_id=peer,
+        device_id_type=MESH,
+    )
+
+
+def weight_rounds(n, shares, me, share, pairs, sems):
+    near, far = n // 2, me // 2
+    core = lax.rem(me, 2)
+    own_sem, send1, recv1, send2, recv2, send3, recv3 = sems
+
+    def own(at):
+        local, whole = pairs[at]
+        return pltpu.make_async_copy(local, whole.at[core, :, far], own_sem.at[at])
+
+    def first(at, shift, back=False):
+        local, whole = pairs[at]
+        origin = lax.rem(far + near - shift, near) if back else far
+        return push(
+            local.at[share],
+            whole.at[core, share, origin],
+            send1.at[at, shift],
+            recv1.at[at, shift],
+            chan=lax.rem(far + shift, near) * 2 + core,
+        )
+
+    def second(at, shift, turn, back=False):
+        whole = pairs[at][1]
+        origin = lax.rem(far + near - shift, near)
+        holder = lax.rem(share + shares - turn, shares) if back else share
+        return push(
+            whole.at[core, share, origin],
+            whole.at[core, holder, origin],
+            send2.at[at, shift, turn],
+            recv2.at[at, shift, turn],
+            dp=lax.rem(share + turn, shares),
+        )
+
+    def third(at, back=False):
+        whole = pairs[at][1]
+        return push(
+            whole.at[core], whole.at[1 - core if back else core], send3.at[at], recv3.at[at], chan=far * 2 + 1 - core
+        )
+
+    both = range(len(pairs))
+
+    def start_first():
+        for at in both:
+            own(at).start()
+            for shift in range(1, near):
+                first(at, shift).start()
+
+    def start_second():
+        for at in both:
+            for shift in range(1, near):
+                first(at, shift, True).wait_recv()
+                for turn in range(1, shares):
+                    second(at, shift, turn).start()
+
+    def start_third():
+        for at in both:
+            own(at).wait()
+            for shift in range(1, near):
+                for turn in range(1, shares):
+                    second(at, shift, turn, True).wait_recv()
+            third(at).start()
+
+    def finish():
+        for at in both:
+            third(at, True).wait_recv()
+            third(at).wait_send()
+            for shift in range(1, near):
+                first(at, shift).wait_send()
+                for turn in range(1, shares):
+                    second(at, shift, turn).wait_send()
+
+    return start_first, start_second, start_third, finish
 
 
 def send_part(stage, target, me, peer, part, send_sem, recv_sem, shift):
@@ -328,16 +447,31 @@
 
 def mixer_kernel(
     n,
+    shares,
     sizes_ref,
     image_ref,
     cot_ref,
-    rows_ref,
-    cols_ref,
+    rate_ref,
+    freq_ref,
+    real_ref,
+    imag_ref,
+    cols_rate_ref,
+    cols_freq_ref,
+    cols_real_ref,
+    cols_imag_ref,
     skip_ref,
     scale_ref,
+    in_part_ref,
+    out_part_ref,
     mixed_ref,
     back_ref,
+    in_whole_ref,
+    out_whole_ref,
     sums_ref,
+    rows_back_ref,
+    rows_ref,
+    cols_back_ref,
+    cols_ref,
     mixed_stage,
     back_stage,
     wide,
@@ -346,11 +480,16 @@
     send_b,
     recv_b,
     own_sem,
+    *weight_sems,
 ):
     count, side, _ = image_ref.shape
     parts = count // GROUP
     block = side // n
-    me = meet(n)
+    me, share = meet(n, shares)
+    start_first, start_second, start_third, finish = weight_rounds(
+        n, shares, me, share, ((in_part_ref, in_whole_ref), (out_part_ref, out_whole_ref)), weight_sems
+    )
+    start_first()
     row_at = lax.broadcasted_iota(jnp.int32, (side, side), 0)
     col_at = lax.broadcasted_iota(jnp.int32, (side, side), 1)
     inside = (row_at < sizes_ref[0]) & (col_at < sizes_ref[1])
@@ -381,6 +520,22 @@
         turn(back_stage, part)
         send(back_stage, back_ref, part, send_b, recv_b)
 
+    lag = lax.broadcasted_iota(jnp.int32, (1, side), 1)
+    lag_back = jnp.where(lag == 0, 0, side - lag).astype(jnp.float32)
+    lag = lag.astype(jnp.float32)
+
+    @pl.loop(0, count // 8)
+    def _(tile):
+        few = pl.ds(pl.multiple_of(tile * 8, 8), 8)
+        rows = (rate_ref[few, :], freq_ref[few, :], real_ref[few, :], imag_ref[few, :])
+        cols = (cols_rate_ref[few, :], cols_freq_ref[few, :], cols_real_ref[few, :], cols_imag_ref[few, :])
+        rows_back_ref[few, :] = taps_tile(*rows, lag_back)
+        rows_ref[few, :] = taps_tile(*rows, lag)
+        cols_back_ref[few, :] = taps_tile(*cols, lag_back)
+        cols_ref[few, :] = taps_tile(*cols, lag)
+
+    start_second()
+
     @pl.loop(0, parts)
     def _(part):
         @pl.loop(0, GROUP)
@@ -388,8 +543,8 @@
             chan = part * GROUP + item
             masked = jnp.where(inside, image_ref[chan].astype(jnp.float32), 0.0)
             masked_low = masked.astype(jnp.bfloat16)
-            rows_high, rows_low = split_low(lag_matrix(rows_ref[pl.ds(chan, 1), 0, :], side, lower))
-            cols_high, cols_low = split_low(lag_matrix(cols_ref[pl.ds(chan, 1), 1, :], side, upper))
+            rows_high, rows_low = split_low(lag_matrix(rows_back_ref[pl.ds(chan, 1), :], side, lower))
+            cols_high, cols_low = split_low(lag_matrix(cols_ref[pl.ds(chan, 1), :], side, upper))
             along = dot_nn(
                 jnp.concatenate([rows_high, rows_low], axis=1),
                 jnp.concatenate([masked_low, masked_low], axis=0),
@@ -405,6 +560,7 @@
         turn(mixed_stage, part)
         send(mixed_stage, mixed_ref, part, send_m, recv_m)
 
+    start_third()
     own_b = pltpu.make_async_copy(back_stage.at[me], back_ref.at[me], own_sem.at[0])
     own_m = pltpu.make_async_copy(mixed_stage.at[me], mixed_ref.at[me], own_sem.at[1])
     own_b.start()
@@ -413,22 +569,29 @@
     own_m.wait()
     wait_parts(back_stage, back_ref, me, n, send_b, recv_b)
     wait_parts(mixed_stage, mixed_ref, me, n, send_m, recv_m)
-
-
-def mixer_forward(n, sizes, images, cotangent, rows_pair, cols_pair, skip_wide, scale_wide):
+    finish()
+
+
+def mixer_forward(n, shares, sizes, images, cotangent, params, skip_wide, scale_wide, in_part, out_part):
+    near = n // 2
     count, side, _ = images.shape
+    line = jax.ShapeDtypeStruct((count, side), jnp.float32)
     shape = (n, count // GROUP, side // n, GROUP, side)
     vmem = pl.BlockSpec(memory_space=pltpu.VMEM)
     hbm = pl.BlockSpec(memory_space=pl.ANY)
     return pl.pallas_call(
-        functools.partial(mixer_kernel, n),
+        functools.partial(mixer_kernel, n, shares),
         out_shape=(
             jax.ShapeDtypeStruct(shape, jnp.bfloat16),
             jax.ShapeDtypeStruct(shape, jnp.bfloat16),
-            jax.ShapeDtypeStruct((count, side), jnp.float32),
-        ),
-        in_specs=[pl.BlockSpec(memory_space=pltpu.SMEM)] + [vmem] * 6,
-        out_specs=(hbm, hbm, vmem),
+        )
+        + tuple(
+            jax.ShapeDtypeStruct((2, shares, near, *part.shape[1:]), jnp.bfloat16)
+            for part in (in_part, out_part)
+        )
+        + (line,) * 5,
+        in_specs=[pl.BlockSpec(memory_space=pltpu.SMEM)] + [vmem] * 12 + [hbm] * 2,
+        out_specs=(hbm,) * 4 + (vmem,) * 5,
         scratch_shapes=[
             pltpu.VMEM(shape, jnp.bfloat16),
             pltpu.VMEM(shape, jnp.bfloat16),
@@ -438,12 +601,19 @@
             pltpu.SemaphoreType.DMA((n,)),
             pltpu.SemaphoreType.DMA((n,)),
             pltpu.SemaphoreType.DMA((2,)),
+            pltpu.SemaphoreType.DMA((2,)),
+            pltpu.SemaphoreType.DMA((2, near)),
+            pltpu.SemaphoreType.DMA((2, near)),
+            pltpu.SemaphoreType.DMA((2, near, shares)),
+            pltpu.SemaphoreType.DMA((2, near, shares)),
+            pltpu.SemaphoreType.DMA((2,)),
+            pltpu.SemaphoreType.DMA((2,)),
         ],
         compiler_params=pltpu.CompilerParams(
             collective_id=0, has_side_effects=True, vmem_limit_bytes=40 * mebi
         ),
         name="mixer_forward",
-    )(sizes, images, cotangent, rows_pair, cols_pair, skip_wide, scale_wide)
+    )(sizes, images, cotangent, *params, skip_wide, scale_wide, in_part, out_part)
 
 
 def gelu_parts(value):
@@ -459,39 +629,44 @@
 
 def mlp_kernel(
     n,
+    shares,
     mixed_ref,
     back_ref,
-    in_turned_ref,
     in_ref,
     out_ref,
-    out_turned_ref,
     gain_ref,
     shift_ref,
-    bias_ref,
     grad_ref,
     branch_ref,
     active_ref,
     before_grad_ref,
-    normed_ref,
-    cots_ref,
+    out_own_ref,
+    out_got_ref,
+    in_own_ref,
+    in_got_ref,
     gain_grad_ref,
     shift_grad_ref,
     grad_stage,
     branch_stage,
-    active_keep,
-    before_keep,
+    active_ring,
+    before_ring,
     normed_keep,
     cots_keep,
     scaled_keep,
     inverse_keep,
     branch_sum,
     grad_sum,
+    hidden_sum,
+    pieces,
+    rows_stage,
     send_g,
     recv_g,
-    send_r,
-    recv_r,
     own_sem,
-    keep_sem,
+    ring_sem,
+    piece_sem,
+    half_sem,
+    send_h,
+    recv_h,
 ):
     side = mixed_ref.shape[-1]
     groups = mixed_ref.shape[1]
@@ -500,32 +675,25 @@
     local = channels // n
     steps = block // LINES
     width = LINES * side
-    me = meet(n)
+    parts = hidden // STEP_HIDDEN
+    ring = active_ring.shape[0]
+    me, _ = meet(n, shares)
+    core = lax.rem(me, 2)
+    sibling = me + 1 - 2 * core
     gain_grad_ref[...] = jnp.zeros_like(gain_grad_ref)
     shift_grad_ref[...] = jnp.zeros_like(shift_grad_ref)
-
-    def keeps(slot, step):
-        span = pl.ds(pl.multiple_of(step * width, width), width)
-        pairs = (
-            (active_keep, active_ref),
-            (before_keep, before_grad_ref),
-            (normed_keep, normed_ref),
-            (cots_keep, cots_ref),
-        )
+    hidden_sum[...] = jnp.zeros_like(hidden_sum)
+
+    def keeps(turn):
+        slot = lax.rem(turn, ring)
+        span = pl.ds(pl.multiple_of(lax.rem(turn, parts) * STEP_HIDDEN, STEP_HIDDEN), STEP_HIDDEN)
         return [
-            pltpu.make_async_copy(kept.at[slot], whole.at[:, span], keep_sem.at[slot, at])
-            for at, (kept, whole) in enumerate(pairs)
+            pltpu.make_async_copy(kept.at[slot], whole.at[turn // parts, span], ring_sem.at[at, slot])
+            for at, (kept, whole) in enumerate(((active_ring, active_ref), (before_ring, before_grad_ref)))
         ]
 
     @pl.loop(0, steps)
     def _(step):
-        slot = lax.rem(step, 2)
-
-        @pl.when(step >= 2)
-        def _():
-            for copy in keeps(slot, step - 2):
-                copy.wait()
-
         for line in range(LINES):
             row = step * LINES + line
             lanes = pl.ds(line * side, side)
@@ -538,25 +706,37 @@
             var = jnp.sum(center * center, axis=0, keepdims=True) * (1.0 / channels)
             inverse = lax.rsqrt(var + eps_norm)
             scaled = center * inverse
-            normed_keep[slot, :, lanes] = (scaled * gain_ref[...] + shift_ref[...]).astype(jnp.bfloat16)
+            normed_keep[step, :, lanes] = (scaled * gain_ref[...] + shift_ref[...]).astype(jnp.bfloat16)
             scaled_keep[:, lanes] = scaled
             inverse_keep[:, lanes] = inverse
-            cots_keep[slot, :, lanes] = jnp.concatenate(
+            cots_keep[step, :, lanes] = jnp.concatenate(
                 [back_ref[owner, group, row] for owner, group in order], axis=0
             )
 
-        @pl.loop(0, hidden // STEP_HIDDEN)
+        @pl.loop(0, parts)
         def _(part):
+            turn = step * parts + part
+            slot = lax.rem(turn, ring)
+
+            @pl.when(turn >= ring)
+            def _():
+                for copy in keeps(turn - ring):
+                    copy.wait()
+
             span = pl.ds(pl.multiple_of(part * STEP_HIDDEN, STEP_HIDDEN), STEP_HIDDEN)
-            before = dot_nn(in_turned_ref[span, :], normed_keep[slot]) + bias_ref[span, :]
+            bias = in_ref[span, channels:].astype(jnp.float32)[:, :1]
+            before = dot_nn(in_ref[span, :channels], normed_keep[step]) + bias
             inside, bell = gelu_parts(before)
             active = (before * inside).astype(jnp.bfloat16)
-            active_grad = dot_nn(out_ref[span, :], cots_keep[slot])
+            active_grad = dot_nn(out_ref[span, :], cots_keep[step])
             before_grad = (active_grad * (inside + before * bell)).astype(jnp.bfloat16)
-            active_keep[slot, span, :] = active
-            before_keep[slot, span, :] = before_grad
-            branch = dot_nn(out_turned_ref[:, span], active)
-            grad = dot_nn(in_ref[:, span], before_grad)
+            active_ring[slot] = active
+            before_ring[slot] = before_grad
+            hidden_sum[span, :] += sum(
+                before_grad[:, line * side : (line + 1) * side].astype(jnp.float32) for line in range(LINES)
+            )
+            branch = dot_tn(out_ref[span, :], active)
+            grad = dot_tn(in_ref[span, :channels], before_grad)
 
             @pl.when(part == 0)
             def _():
@@ -568,8 +748,8 @@
                 branch_sum[...] += branch
                 grad_sum[...] += grad
 
-        for copy in keeps(slot, step):
-            copy.start()
+            for copy in keeps(turn):
+                copy.start()
 
         for line in range(LINES):
             lanes = pl.ds(line * side, side)
@@ -588,91 +768,254 @@
 
         for shift in range(1, n):
             send_part(grad_stage, grad_ref, me, lax.rem(me + shift, n), step, send_g, recv_g, shift).start()
-        for shift in range(1, n):
-            send_part(branch_stage, branch_ref, me, lax.rem(me + shift, n), step, send_r, recv_r, shift).start()
 
     own_g = pltpu.make_async_copy(grad_stage.at[me], grad_ref.at[me], own_sem.at[0])
-    own_r = pltpu.make_async_copy(branch_stage.at[me], branch_ref.at[me], own_sem.at[1])
+    own_r = pltpu.make_async_copy(branch_stage, branch_ref, own_sem.at[1])
     own_g.start()
     own_r.start()
+    turns = steps * parts
+    for turn in range(turns - ring, turns):
+        for copy in keeps(turn):
+            copy.wait()
+
+    half = parts // 2
+
+    kinds = (
+        (active_ref, cots_keep, out_own_ref, out_got_ref, channels),
+        (before_grad_ref, normed_keep, in_own_ref, in_got_ref, channels + side),
+    )
+
+    def fetch(whole, job, slot):
+        place = lax.rem((1 - core) * half + job, parts)
+        span = pl.ds(pl.multiple_of(place * STEP_HIDDEN, STEP_HIDDEN), STEP_HIDDEN)
+        return pltpu.make_async_copy(whole.at[:, span], pieces.at[slot], piece_sem.at[slot])
+
+    def give(kind, job):
+        _, _, _, got, wide = kinds[kind]
+        return push(
+            rows_stage.at[job, :, pl.ds(0, wide)],
+            got.at[pl.ds(job * STEP_HIDDEN, STEP_HIDDEN)],
+            send_h.at[kind, job],
+            recv_h.at[kind, job],
+            chan=sibling,
+        )
+
+    def keep(kind, job):
+        _, _, own, _, wide = kinds[kind]
+        return pltpu.make_async_copy(
+            rows_stage.at[job, :, pl.ds(0, wide)],
+            own.at[pl.ds((job - half) * STEP_HIDDEN, STEP_HIDDEN)],
+            half_sem.at[kind, job],
+        )
+
+    jobs = [(kind, job) for kind in range(2) for job in range(parts)]
+    fetch(kinds[0][0], 0, 0).start()
+    for at, (kind, job) in enumerate(jobs):
+        whole, right = kinds[kind][:2]
+        slot = at % 2
+        if at + 1 < len(jobs):
+            fetch(kinds[jobs[at + 1][0]][0], jobs[at + 1][1], (at + 1) % 2).start()
+        fetch(whole, job, slot).wait()
+        if kind == 1:
+            (give if job < half else keep)(0, job).wait()
+        total = dot_nt(pieces[slot, 0], right[0])
+        for step in range(1, steps):
+            total = total + dot_nt(pieces[slot, step], right[step])
+        rows_stage[job, :, :channels] = total.astype(jnp.bfloat16)
+        if kind == 1:
+            place = lax.rem((1 - core) * half + job, parts)
+            span = pl.ds(pl.multiple_of(place * STEP_HIDDEN, STEP_HIDDEN), STEP_HIDDEN)
+            rows_stage[job, :, channels:] = hidden_sum[span, :].astype(jnp.bfloat16)
+        (give if job < half else keep)(kind, job).start()
+    for job in range(parts):
+        (give if job < half else keep)(1, job).wait()
     own_g.wait()
     own_r.wait()
-    for step in range(max(steps - 2, 0), steps):
-        for copy in keeps(step % 2, step):
-            copy.wait()
     wait_parts(grad_stage, grad_ref, me, n, send_g, recv_g)
-    wait_parts(branch_stage, branch_ref, me, n, send_r, recv_r)
-
-
-def mlp(n, mixed, back, in_turned, in_full, out_full, out_turned, gain, shift, bias):
+
+
+def mlp(n, shares, mixed, back, in_full, out_full, gain, shift):
     _, groups, block, group, side = mixed.shape
     hidden, channels = out_full.shape
     local = channels // n
-    pixels = block * side
+    steps = block // LINES
     width = LINES * side
-    shape = (n, block // LINES, LINES, local, side)
+    parts = hidden // STEP_HIDDEN
+    shape = (n, steps, LINES, local, side)
+    ring = 4
+    low = functools.partial(jax.ShapeDtypeStruct, dtype=jnp.bfloat16)
     vmem = pl.BlockSpec(memory_space=pltpu.VMEM)
     hbm = pl.BlockSpec(memory_space=pl.ANY)
     return pl.pallas_call(
-        functools.partial(mlp_kernel, n),
+        functools.partial(mlp_kernel, n, shares),
         out_shape=(
-            jax.ShapeDtypeStruct(shape, jnp.bfloat16),
-            jax.ShapeDtypeStruct(shape, jnp.bfloat16),
-            jax.ShapeDtypeStruct((hidden, pixels), jnp.bfloat16),
-            jax.ShapeDtypeStruct((hidden, pixels), jnp.bfloat16),
-            jax.ShapeDtypeStruct((channels, pixels), jnp.bfloat16),
-            jax.ShapeDtypeStruct((channels, pixels), jnp.bfloat16),
+            low(shape),
+            low(shape),
+            low((steps, hidden, width)),
+            low((steps, hidden, width)),
+            low((hidden // 2, channels)),
+            low((hidden // 2, channels)),
+            low((hidden // 2, channels + side)),
+            low((hidden // 2, channels + side)),
             jax.ShapeDtypeStruct((channels, side), jnp.float32),
             jax.ShapeDtypeStruct((channels, side), jnp.float32),
         ),
-        in_specs=[vmem] * 9,
-        out_specs=(hbm,) * 6 + (vmem, vmem),
+        in_specs=[vmem] * 6,
+        out_specs=(hbm,) * 8 + (vmem, vmem),
         scratch_shapes=[
             pltpu.VMEM(shape, jnp.bfloat16),
             pltpu.VMEM(shape, jnp.bfloat16),
-            pltpu.VMEM((2, hidden, width), jnp.bfloat16),
-            pltpu.VMEM((2, hidden, width), jnp.bfloat16),
-            pltpu.VMEM((2, channels, width), jnp.bfloat16),
-            pltpu.VMEM((2, channels, width), jnp.bfloat16),
+            pltpu.VMEM((ring, STEP_HIDDEN, width), jnp.bfloat16),
+            pltpu.VMEM((ring, STEP_HIDDEN, width), jnp.bfloat16),
+            pltpu.VMEM((steps, channels, width), jnp.bfloat16),
+            pltpu.VMEM((steps, channels, width), jnp.bfloat16),
             pltpu.VMEM((channels, width), jnp.float32),
             pltpu.VMEM((1, width), jnp.float32),
             pltpu.VMEM((channels, width), jnp.float32),
             pltpu.VMEM((channels, width), jnp.float32),
-            pltpu.SemaphoreType.DMA((n,)),
-            pltpu.SemaphoreType.DMA((n,)),
+            pltpu.VMEM((hidden, side), jnp.float32),
+            pltpu.VMEM((2, steps, STEP_HIDDEN, width), jnp.bfloat16),
+            pltpu.VMEM((parts, STEP_HIDDEN, channels + side), jnp.bfloat16),
             pltpu.SemaphoreType.DMA((n,)),
             pltpu.SemaphoreType.DMA((n,)),
             pltpu.SemaphoreType.DMA((2,)),
-            pltpu.SemaphoreType.DMA((2, 4)),
+            pltpu.SemaphoreType.DMA((2, ring)),
+            pltpu.SemaphoreType.DMA((2,)),
+            pltpu.SemaphoreType.DMA((2, parts)),
+            pltpu.SemaphoreType.DMA((2, parts)),
+            pltpu.SemaphoreType.DMA((2, parts)),
         ],
         compiler_params=pltpu.CompilerParams(
             collective_id=1, has_side_effects=True, vmem_limit_bytes=63 * mebi
         ),
         name="mlp",
-    )(mixed, back, in_turned, in_full, out_full, out_turned, gain, shift, bias)
+    )(mixed, back, in_full, out_full, gain, shift)
+
+
+def sum_rounds(n, shares, me, share, own, got, final, stage2, take2, stage3, take3, keep3, sems):
+    near, far = n // 2, me // 2
+    core = lax.rem(me, 2)
+    send2, recv2, send3, recv3, send4, recv4, own_sem = sems
+    rows = keep3.shape[0]
+    block = near * rows
+
+    def second(turn):
+        peer = lax.rem(share + turn, shares)
+        return push(stage2.at[peer], take2.at[turn], send2.at[turn], recv2.at[turn], dp=peer)
+
+    def third(turn):
+        peer = lax.rem(far + turn, near)
+        return push(stage3.at[peer], take3.at[turn], send3.at[turn], recv3.at[turn], chan=peer * 2 + core)
+
+    def fourth(turn, back=False):
+        holder = lax.rem(share + shares - turn, shares) if back else share
+        peer = lax.rem(share + turn, shares)
+        return push(keep3, final.at[holder], send4.at[turn], recv4.at[turn], dp=peer)
+
+    def mine():
+        return pltpu.make_async_copy(keep3, final.at[share], own_sem.at[0])
+
+    def start_second():
+        for at in range(shares):
+            span = slice(at * block, (at + 1) * block)
+            stage2[at] = (own[span].astype(jnp.float32) + got[span].astype(jnp.float32)).astype(jnp.bfloat16)
+        for turn in range(1, shares):
+            second(turn).start()
+
+    def start_third():
+        for turn in range(1, shares):
+            second(turn).wait()
+        for at in range(near):
+            base = pl.ds(pl.multiple_of(share * block + at * rows, rows), rows)
+            span = slice(at * rows, (at + 1) * rows)
+            total = own[base, :].astype(jnp.float32) + got[base, :].astype(jnp.float32)
+            for turn in range(1, shares):
+                total = total + take2[turn, span].astype(jnp.float32)
+            stage3[at] = total.astype(jnp.bfloat16)
+
+            @pl.when(far == at)
+            def _():
+                keep3[...] = total
+
+        for turn in range(1, near):
+            third(turn).start()
+
+    def start_fourth():
+        for turn in range(1, near):
+            third(turn).wait()
+        total = keep3[...]
+        for turn in range(1, near):
+            total = total + take3[turn].astype(jnp.float32)
+        keep3[...] = total
+        mine().start()
+        for turn in range(1, shares):
+            fourth(turn).start()
+
+    def finish():
+        mine().wait()
+        for turn in range(1, shares):
+            fourth(turn, True).wait_recv()
+            fourth(turn).wait_send()
+
+    return start_second, start_third, start_fourth, finish
 
 
 def back_kernel(
+    n,
+    shares,
     sizes_ref,
     image_ref,
     cot_ref,
     grad_ref,
     branch_ref,
+    rows_back_ref,
     rows_ref,
-    cols_ref,
+    cols_back_ref,
     skip_ref,
     scale_ref,
     bias_ref,
+    out_own_ref,
+    out_got_ref,
+    in_own_ref,
+    in_got_ref,
     output_ref,
     input_grad_ref,
     rows_sums_ref,
     cols_sums_ref,
     skip_sums_ref,
     scale_sums_ref,
-    grad_wide,
-    branch_wide,
+    out_final_ref,
+    in_final_ref,
+    wide,
+    branch_got,
+    send_sem,
+    recv_sem,
+    own_sem,
+    *rest,
 ):
     count, side, _ = image_ref.shape
+    steps, lines = branch_ref.shape[1], branch_ref.shape[2]
+    me, share = meet(n, shares)
+    out_rounds = sum_rounds(
+        n, shares, me, share, out_own_ref, out_got_ref, out_final_ref, *rest[:5], rest[10:17]
+    )
+    in_rounds = sum_rounds(
+        n, shares, me, share, in_own_ref, in_got_ref, in_final_ref, *rest[5:10], rest[17:24]
+    )
+    out_rounds[0]()
+    for shift in range(1, n):
+        peer = lax.rem(me + shift, n)
+        pltpu.make_async_remote_copy(
+            src_ref=branch_ref.at[peer],
+            dst_ref=branch_got.at[me],
+            send_sem=send_sem.at[shift],
+            recv_sem=recv_sem.at[shift],
+            device_id={"chan": peer},
+            device_id_type=MESH,
+        ).start()
+    own = pltpu.make_async_copy(branch_ref.at[me], branch_got.at[me], own_sem.at[0])
+    own.start()
+    in_rounds[0]()
     row_at = lax.broadcasted_iota(jnp.int32, (side, side), 0)
     col_at = lax.broadcasted_iota(jnp.int32, (side, side), 1)
     inside = (row_at < sizes_ref[0]) & (col_at < sizes_ref[1])
@@ -683,28 +1026,26 @@
     @pl.loop(0, side)
     def _(row):
         span = pl.ds(pl.multiple_of(row * count, count), count)
-        grad_wide[span, :] = grad_ref[row].astype(jnp.float32)
-        branch_wide[span, :] = branch_ref[row].astype(jnp.float32)
+        wide[span, :] = grad_ref[row].astype(jnp.float32)
 
     @pl.loop(0, count)
     def _(chan):
+        pl.when(chan == count // 2)(out_rounds[1])
+        pl.when(chan == count * 3 // 4)(out_rounds[2])
+        pl.when(chan == count * 15 // 16)(in_rounds[1])
         one = pl.ds(chan, 1)
-        grad = grad_wide[pl.ds(chan, side, stride=count), :]
-        branch = branch_wide[pl.ds(chan, side, stride=count), :]
+        grad = wide[pl.ds(chan, side, stride=count), :]
         image = image_ref[chan].astype(jnp.float32)
         grad_out = jnp.where(inside, cot_ref[chan].astype(jnp.float32), 0.0)
-        shifted = branch + bias_ref[one, :]
-        output_ref[chan] = jnp.where(inside, image + scale_ref[one, :] * shifted, 0.0).astype(jnp.bfloat16)
-        scale_sums_ref[one, :] = jnp.sum(grad_out * shifted, axis=0, keepdims=True)
         masked = jnp.where(inside, image, 0.0)
         skip_sums_ref[one, :] = jnp.sum(grad * masked, axis=0, keepdims=True)
         masked_low = masked.astype(jnp.bfloat16)
         grad_low = grad.astype(jnp.bfloat16)
         grad_turned = dot_nt(flip, grad_low).astype(jnp.bfloat16)
         masked_turned = dot_nn(flip, masked_low).astype(jnp.bfloat16)
-        rows_high, rows_low = split_low(lag_matrix(rows_ref[one, 0, :], side, lower))
-        turned_high, turned_low = split_low(lag_matrix(rows_ref[one, 1, :], side, upper))
-        cols_high, cols_low = split_low(lag_matrix(cols_ref[one, 0, :], side, lower))
+        rows_high, rows_low = split_low(lag_matrix(rows_back_ref[one, :], side, lower))
+        turned_high, turned_low = split_low(lag_matrix(rows_ref[one, :], side, upper))
+        cols_high, cols_low = split_low(lag_matrix(cols_back_ref[one, :], side, lower))
         along = dot_nn(
             jnp.concatenate([rows_high, rows_low], axis=1),
             jnp.concatenate([masked_low, masked_low], axis=0),
@@ -732,13 +1073,48 @@
         rows_sums_ref[one, :] = lag_sums(rows_grad, side, row_at + col_at >= side - 1)
         cols_sums_ref[one, :] = lag_sums(cols_grad, side, row_at + col_at <= side - 1)
 
-
-def mixer_back(sizes, images, cotangent, grad, branch, rows_pair, cols_pair, skip_wide, scale_wide, bias_wide):
+    own.wait()
+    for shift in range(1, n):
+        peer = lax.rem(me + shift, n)
+        pltpu.make_async_remote_copy(
+            src_ref=branch_ref.at[peer],
+            dst_ref=branch_got.at[lax.rem(me + n - shift, n)],
+            send_sem=send_sem.at[shift],
+            recv_sem=recv_sem.at[shift],
+            device_id={"chan": peer},
+            device_id_type=MESH,
+        ).wait()
+
+    @pl.loop(0, n * steps)
+    def _(step):
+        for line in range(lines):
+            span = pl.ds(pl.multiple_of((step * lines + line) * count, count), count)
+            wide[span, :] = branch_got[step // steps, lax.rem(step, steps), line].astype(jnp.float32)
+
+    @pl.loop(0, count)
+    def _(chan):
+        one = pl.ds(chan, 1)
+        shifted = wide[pl.ds(chan, side, stride=count), :] + bias_ref[one, :]
+        image = image_ref[chan].astype(jnp.float32)
+        grad_out = jnp.where(inside, cot_ref[chan].astype(jnp.float32), 0.0)
+        output_ref[chan] = jnp.where(inside, image + scale_ref[one, :] * shifted, 0.0).astype(jnp.bfloat16)
+        scale_sums_ref[one, :] = jnp.sum(grad_out * shifted, axis=0, keepdims=True)
+
+    in_rounds[2]()
+    out_rounds[3]()
+    in_rounds[3]()
+
+
+def mixer_back(n, shares, sizes, images, cotangent, grad, branch, lines, halves):
     count, side, _ = images.shape
+    near = n // 2
+    rows = halves[0].shape[0] // (shares * near)
+    wides = (halves[0].shape[1], halves[2].shape[1])
+    hbm = pl.BlockSpec(memory_space=pl.ANY)
     line = jax.ShapeDtypeStruct((count, side), jnp.float32)
     vmem = pl.BlockSpec(memory_space=pltpu.VMEM)
     return pl.pallas_call(
-        back_kernel,
+        functools.partial(back_kernel, n, shares),
         out_shape=(
             jax.ShapeDtypeStruct(images.shape, jnp.bfloat16),
             jax.ShapeDtypeStruct(images.shape, jnp.float32),
@@ -746,20 +1122,38 @@
             line,
             line,
             line,
-        ),
-        in_specs=[pl.BlockSpec(memory_space=pltpu.SMEM)] + [vmem] * 9,
-        out_specs=(vmem,) * 6,
+        )
+        + tuple(jax.ShapeDtypeStruct((shares, rows, wide), jnp.float32) for wide in wides),
+        in_specs=[pl.BlockSpec(memory_space=pltpu.SMEM)] + [vmem] * 3 + [hbm] + [vmem] * 10,
+        out_specs=(vmem,) * 6 + (hbm,) * 2,
         scratch_shapes=[
             pltpu.VMEM((count * side, side), jnp.float32),
-            pltpu.VMEM((count * side, side), jnp.float32),
+            pltpu.VMEM(branch.shape, jnp.bfloat16),
+            pltpu.SemaphoreType.DMA((n,)),
+            pltpu.SemaphoreType.DMA((n,)),
+            pltpu.SemaphoreType.DMA((1,)),
+        ]
+        + [
+            kind
+            for wide in wides
+            for kind in (
+                pltpu.VMEM((shares, near * rows, wide), jnp.bfloat16),
+                pltpu.VMEM((shares, near * rows, wide), jnp.bfloat16),
+                pltpu.VMEM((near, rows, wide), jnp.bfloat16),
+                pltpu.VMEM((near, rows, wide), jnp.bfloat16),
+                pltpu.VMEM((rows, wide), jnp.float32),
+            )
+        ]
+        + [
+            pltpu.SemaphoreType.DMA((size,))
+            for _ in wides
+            for size in (shares, shares, near, near, shares, shares, 1)
         ],
-        compiler_params=pltpu.CompilerParams(vmem_limit_bytes=60 * mebi),
+        compiler_params=pltpu.CompilerParams(
+            collective_id=2, has_side_effects=True, vmem_limit_bytes=62 * mebi
+        ),
         name="mixer_back",
-    )(sizes, images, cotangent, grad, branch, rows_pair, cols_pair, skip_wide, scale_wide, bias_wide)
-
-
-def lag_pair(taps):
-    return jnp.stack([jnp.roll(taps[:, ::-1], 1, axis=1), taps], axis=1)
+    )(sizes, images, cotangent, grad, branch, *lines, *halves)
 
 
 def pixel_body(
@@ -791,11 +1185,7 @@
     sizes = image_sizes[picked]
     image, cot = images[0], cotangent[0]
 
-    def both_taps(*params):
-        return kernel_taps(*params[:4], side), kernel_taps(*params[4:], side)
-
-    (rows_taps, cols_taps), taps_pull = jax.vjp(
-        both_taps,
+    params = (
         rows_rate,
         rows_freq,
         rows_real,
@@ -805,72 +1195,70 @@
         cols_real,
         cols_imag,
     )
-    rows_pair, cols_pair = lag_pair(rows_taps), lag_pair(cols_taps)
+
+    def both_taps(*params):
+        return kernel_taps(*params[:4], side), kernel_taps(*params[4:], side)
+
     skip_wide = jnp.broadcast_to(skip_gain[:, None], (count, side))
     scale_wide = jnp.broadcast_to(layer_scale[:, None], (count, side))
     bias_wide = jnp.broadcast_to(bias_out[:, None], (count, side))
 
-    in_turned = lax.all_gather(weight_in.T, "chan", axis=0, tiled=True)
-    out_full = lax.all_gather(weight_out, "chan", axis=0, tiled=True)
-    bias_full = lax.all_gather(bias_in, "chan", axis=0, tiled=True).astype(jnp.float32)
-
-    mixed, back, bias_out_sums = mixer_forward(
-        n, sizes, image, cot, rows_pair, cols_pair, skip_wide, scale_wide
-    )
-    grad, branch, active, before_grad, normed, cots, gain_sums, shift_sums = mlp(
+    shares = lax.axis_size("dp")
+    hidden = weight_out.shape[0]
+    spread = jnp.broadcast_to(bias_in[:, None], (hidden, side))
+    in_part = jnp.concatenate([weight_in.T, spread], axis=1).reshape(shares, -1, channels + side)
+    out_part = weight_out.reshape(shares, -1, channels)
+    mixed, back, in_whole, out_whole, bias_out_sums, rows_back, rows, cols_back, _ = mixer_forward(
+        n, shares, sizes, image, cot, params, skip_wide, scale_wide, in_part, out_part
+    )
+    grad, branch, _, _, *halves, gain_sums, shift_sums = mlp(
         n,
+        shares,
         mixed,
         back,
-        in_turned,
-        in_turned.T,
-        out_full,
-        out_full.T,
+        in_whole.reshape(-1, channels + side),
+        out_whole.reshape(-1, channels),
         jnp.broadcast_to(norm_gain[:, None], (channels, side)),
         jnp.broadcast_to(norm_bias[:, None], (channels, side)),
-        bias_full[:, None],
-    )
-    out_weight_grad = lax.psum_scatter(dot_nt(active, cots), "chan", scatter_dimension=0, tiled=True)
-    in_weight_grad = lax.psum_scatter(dot_nt(before_grad, normed), "chan", scatter_dimension=0, tiled=True)
-    in_bias_grad = lax.psum_scatter(
-        jnp.sum(before_grad.astype(jnp.float32), axis=1), "chan", scatter_dimension=0, tiled=True
-    )
-    output, input_grad, rows_sums, cols_sums, skip_sums, scale_sums = mixer_back(
+    )
+    output, input_grad, rows_sums, cols_sums, skip_sums, scale_sums, out_final, in_final = mixer_back(
+        n,
+        shares,
         sizes,
         image,
         cot,
         grad.reshape(side, count, side),
-        branch.reshape(side, count, side),
-        rows_pair,
-        cols_pair,
-        skip_wide,
-        scale_wide,
-        bias_wide,
-    )
-    params_grad = taps_pull(
+        branch,
+        (rows_back, rows, cols_back, skip_wide, scale_wide, bias_wide),
+        halves,
+    )
+    in_final = in_final.reshape(hidden, channels + side)
+    params_grad = jax.vjp(both_taps, *params)[1](
         (jnp.roll(rows_sums, 1, axis=1), cols_sums[:, ::-1])
     )
-    in_weight_grad, out_weight_grad = lax.psum((in_weight_grad, out_weight_grad), "dp")
     small = lax.psum(
         (
             *params_grad,
             jnp.sum(skip_sums, axis=1),
-            in_bias_grad,
             jnp.sum(bias_out_sums, axis=1),
             jnp.sum(scale_sums, axis=1),
         ),
         "dp",
     )
-    norm_sums = lax.psum((jnp.sum(gain_sums, axis=1), jnp.sum(shift_sums, axis=1)), ("dp", "chan"))
+    gain_grad, shift_grad = lax.psum(
+        (jnp.sum(gain_sums, axis=1), jnp.sum(shift_sums, axis=1)), ("dp", "chan")
+    )
     return (
         output[None],
         input_grad[None],
         *small[:9],
-        *norm_sums,
-        in_weight_grad.T,
+        gain_grad,
+        shift_grad,
+        in_final[:, :channels].T,
+        jnp.sum(in_final[:, channels:], axis=1),
+        out_final.reshape(hidden, channels),
         small[9],
-        out_weight_grad,
         small[10],
-        small[11],
     )
 
 
@@ -881,7 +1269,9 @@
         and side == 128
         and count % GROUP == 0
         and side % (n * LINES) == 0
-        and (rest[15].shape[0] * n) % STEP_HIDDEN == 0
+        and n % 2 == 0
+        and (rest[15].shape[0] * n) % (2 * STEP_HIDDEN) == 0
+        and rest[15].shape[0] % (16 * lax.axis_size("dp")) == 0
     )
     return pixel_body(n, images, *rest) if fits else plain_body(images, *rest)
 

time: 781 us -> 584 us (0.75)
  waiting for transfers between devices: 146 us -> 6.56 us
  blocking collectives: 76 us -> 40.6 us
  matrix products: 32.4 us -> 0 us
  Pallas kernels: 413 us -> 436 us
  other arithmetic: 43.5 us -> 25.3 us
    psum x2 -> x1, waiting for transfers between devices: 78 us -> 6.54 us  [pixel_body(): lax.psum((*params_grad, jnp.sum(skip_sums, axis=1), jnp.sum(bias_out_sums...]
    reduce_scatter x2 -> x0, waiting for transfers between devices: 67.7 us -> none  [the longest x1 67.6 us: pixel_body(): lax.psum_scatter(dot_nt(before_grad, normed), 'chan', scatter_dimension=0...]
    dot_general x2 -> x0, matrix products: 32.4 us -> none  [dot_nt(): lax.dot_general(left, right, (((1,), (1,)), ((), ())), preferred_element_...]
    pallas_call x3, Pallas kernels: 413 us -> 436 us  [the longest x1 169 us: mixer_forward(): pl.pallas_call(functools.partial(mixer_kernel, n, shares), out_shape=(jax...]
    unnamed x1 -> x0, blocking collectives: 21.5 us -> none
    reduce_sum x3 -> x1, other arithmetic: 20.1 us -> 0.72 us  [pixel_body(): jnp.sum(in_final[:, channels:], axis=1)]
    all_gather x1 -> x0, blocking collectives: 13.6 us -> none  [pixel_body(): lax.all_gather(bias_in, 'chan', axis=0, tiled=True).astype(jnp.float32)]
    all_gather x2 -> x0, local copies, waits for them, and re-layouts: 13.3 us -> none  [the longest x1 6.64 us: pixel_body(): out_full = lax.all_gather(weight_out, 'chan', axis=0, tiled=True)]
  transfers between devices with their start and end apart: 6 -> 1, of which waited for: 3 -> 1; matrix products, arithmetic and copies ran while one was open for 11% -> 0% of each run, Pallas kernels for 32% -> 0%
where the time goes in v2:
time: 584 us; the launch traced here: 574 us
  Pallas kernels  436 us (75%)
  local copies, waits for them, and re-layouts  48.8 us (8%)
  blocking collectives  40.6 us (7%)
  other arithmetic  25.3 us (4%)
  between operations  16.7 us (3%)
  waiting for transfers between devices  6.56 us (1%)
    pallas_call x1, Pallas kernels, mixer_forward(): pl.pallas_call(functools.partial(mixer_kernel, n, shares), out_shape=(jax...  169 us
    pallas_call x1, Pallas kernels, mixer_back(): pl.pallas_call(functools.partial(back_kernel, n, shares), out_shape=(jax....  136 us
    pallas_call x1, Pallas kernels, mlp(): pl.pallas_call(functools.partial(mlp_kernel, n, shares), out_shape=(low(s...  131 us
    unnamed x77, local copies, waits for them, and re-layouts  41.7 us
    psum x1, blocking collectives, pixel_body(): lax.psum((jnp.sum(gain_sums, axis=1), jnp.sum(shift_sums, axis=1)), ('dp'...  40.6 us
    reduce_sum x1, other arithmetic, kernel_taps(): imag_part[:, :, None] * jnp.sin(angles)  17.7 us
  transfers between devices with their start and end apart: 1, of which 1 were waited for; matrix products, arithmetic and copies ran while one was open for 0% of the time, Pallas kernels for 0%

profile of v2, /device:TPU:9, one launch (start us, length us, event | category | flops | bytes accessed | tf_op | source)
XLA Modules:
  0.0 574.4 jit_solution(3119260737756905354)
XLA Ops:
  7.2 0.0 all-reduce.4.cloned.1.call-start
  7.3 1.2 dynamic_slice.6
  9.8 0.8 copy.57.rate_ref
  10.6 0.7 neg.32
  11.3 0.8 copy.61.cols_rate_ref
  12.1 0.7 neg.36
  12.9 0.8 copy.58.freq_ref
  13.7 0.8 copy.59.real_ref
  14.5 0.8 copy.60.imag_ref
  15.3 0.9 copy.62.cols_freq_ref
  16.2 0.8 copy.63.cols_real_ref
  17.0 0.8 copy.64.cols_imag_ref
  17.8 0.7 broadcast_in_dim.22
  18.5 1.1 pad_maximum_fusion
  19.6 0.4 copy.56
  20.7 0.2 dynamic-slice_reduce_fusion.sizes_ref
  20.9 0.1 broadcast_in_dim.20.skip_ref
  21.0 0.1 broadcast_in_dim.21.scale_ref
  21.1 1.9 copy-done.2
  23.0 1.9 copy-done.3
  24.9 169.1 %mixer_forward.1 = (bf16[8,6,16,16,128]{4,3,2,1,0:T(8,128)(2,1)S(1)}, bf16[8,6,16,16,128]{4,3,2,1,0:T(8,128)(2,1)S(1)}, bf16[2,4,4,96,896]{4,3,2,1,0:T(8,128)(2,...) custom-call(s32[2]{0:T(128)S(1)} %dynamic-slice_reduce_fusion.sizes_, ...), custom_call_target="tpu_custom_call" | custom-call | tf_op jit(solution)/shard_map/mixer_forward/pallas_call | solution.py:582
  194.0 1.7 copy-done.4
  195.6 1.7 copy-done.5
  197.3 0.6 copy-done.9
  197.9 0.6 copy-done.10
  198.5 0.6 copy-done.11
  199.1 0.9 broadcast_in_dim.23.gain_ref
  200.0 0.9 broadcast_in_dim.24.shift_ref
  201.0 131.0 %mlp.1 = (bf16[8,4,4,96,128]{4,3,2,1,0:T(8,128)(2,1)}, bf16[8,4,4,96,128]{4,3,2,1,0:T(8,128)(2,1)}, bf16[4,3072,512]{2,1,0:T(8,128)(2,1)}, bf16[4,3072,512]{2,1,...) custom-call(bf16[8,6,16,16,128]{4,3,2,1,0:T(8,128)(2,1)} %copy-done., ...), custom_call_target="tpu_custom_call" | custom-call | tf_op jit(solution)/shard_map/mlp/pallas_call | solution.py:849
  331.9 0.7 broadcast_in_dim.25.bias_ref
  332.6 136.2 %mixer_back.1 = (bf16[96,128,128]{2,1,0:T(8,128)(2,1)}, f32[96,128,128]{2,1,0:T(8,128)}, f32[96,128]{1,0:T(8,128)}, f32[96,128]{1,0:T(8,128)}, f32[96,128]{1,0:T...) custom-call(s32[2]{0:T(128)} %copy-done.12, bf16[96,128,128]{2,1,0:T(8,128)(2,1)} %bitcast.15, ...), custom_call_target="tpu_custom_call" | custom-call | tf_op jit(solution)/shard_map/mixer_back/pallas_call | solution.py:1116
  468.9 0.9 slice.14
  469.8 0.9 rev.3
  470.7 0.1 copy.68
  470.8 0.1 copy.72
  470.8 0.9 pad_maximum_fusion.1
  471.8 17.7 %multiply_reduce_fusion = (f32[96,32]{1,0:T(8,128)}, f32[96,32]{1,0:T(8,128)}, f32[96,32]{1,0:T(8,128)S(1)}, f32[96,32]{1,0:T(8,128)}, f32[96,32]{1,0:T(8,128)},...) fusion(f32[96,32]{1,0:T(8,128)S(1)} %copy.72, f32[96,32]{1,0:T(8,128)S(1)} %copy.62.cols_freq_ref, ...), kind=kLoop, calls=%fused_computation | loop fusion | flops 18063360 | bytes 294912 | tf_op jit(solution)/shard_map/transpose(jvp())/reduce_sum | solution.py:20
  489.5 0.6 neg.33
  490.1 0.6 neg.37
  490.7 0.6 reduce_sum.135
  491.3 0.6 reduce_sum.146
  492.0 0.6 reduce_sum.142
  492.6 0.0 all-reduce.4.cloned.1.call-update
  492.6 0.2 reduce_sum.139
  492.8 0.2 reduce_sum.140
  493.0 0.1 slice.18
  493.1 1.4 copy.82
  494.5 40.6 %all-reduce = (f32[768]{0:T(1024)}, f32[768]{0:T(1024)}) all-reduce(f32[768]{0:T(1024)S(1)} %reduce_sum.139, f32[768]{0:T(1024)S(1)} %reduce_sum.140), channel_id=1, replica_groups=mesh['dp'=4,'chan'=8] {'dp','chan'}, use_global_device_ids=true, to_apply=%region_19.20 | all-reduce | flops 1536 | bytes 12288 | tf_op jit(solution)/shard_map/psum | solution.py:1248
  535.1 0.7 slice_reduce_fusion
  535.8 6.5 %all-reduce.4.cloned.1.call-done = (f32[96,32]{1,0:T(8,128)}, f32[96,32]{1,0:T(8,128)}, f32[96,32]{1,0:T(8,128)}, f32[96,32]{1,0:T(8,128)}, f32[96,32]{1,0:T(8,1...) async-done(((f32[96,32]{1,0:T(8,128)}, f32[96,32]{1,0:T(8,128)}, f32[96,32]{1,0:T(8,128)}, ...) | async-done | bytes 99472 | tf_op jit(solution)/shard_map/psum | solution.py:1239
  542.4 1.5 copy.74
  543.9 1.5 copy.75
  545.3 1.5 copy.76
  546.8 1.5 copy.77
  548.3 1.5 copy.78
  549.8 1.5 copy.79
  551.2 1.5 copy.80
  552.7 1.5 copy.81
  554.2 4.0 copy.97
  558.2 6.4 %copy.98 = f32[1,96,128,128]{3,2,1,0:T(8,128)} copy(f32[1,96,128,128]{3,2,1,0:T(8,128)} %bitcast.21) | data formatting | bytes 12582912
  564.6 0.5 copy.99
  565.1 1.0 copy.100
  566.1 0.5 copy.101
  566.6 0.5 copy.102
  (47 shorter events, 0.1 us)
Async XLA Ops:
  7.2 13.5 %copy-start = (s32[4,2]{0,1:T(2,128)S(1)}, s32[4,2]{0,1:T(2,128)}, u32[]{:S(2)}) copy-start(s32[4,2]{0,1:T(2,128)} %param.22) | copy-start | bytes 100
  7.2 535.2 %all-reduce.4.cloned.1.call-start = ((), (), s32[]{:S(2)}) async-start(), calls=%async_computation | async-start | bytes 789504 | tf_op jit(solution)/shard_map/psum | solution.py:1239
  14.5 6.4 %copy-start.21 = (f32[96]{0:T(128)S(1)}, f32[96]{0:T(128)}, u32[]{:S(2)}) copy-start(f32[96]{0:T(128)} %param.32) | copy-start | bytes 1156
  14.5 6.5 %copy-start.22 = (f32[96]{0:T(128)S(1)}, f32[96]{0:T(128)}, u32[]{:S(2)}) copy-start(f32[96]{0:T(128)} %param.39) | copy-start | bytes 1156
  15.3 5.7 copy-start.6
  20.9 173.1 %copy-start.12 = (s32[2]{0:T(128)}, s32[2]{0:T(128)S(1)}, u32[]{:S(2)}) copy-start(s32[2]{0:T(128)S(1)} %dynamic-slice_reduce_fusion.sizes_ref) | copy-start | bytes 28
  21.0 173.0 %copy-start.7 = (f32[96,128]{1,0:T(8,128)}, f32[96,128]{1,0:T(8,128)S(1)}, u32[]{:S(2)}) copy-start(f32[96,128]{1,0:T(8,128)S(1)} %broadcast_in_dim.20.skip_ref) | copy-start | bytes 147460
  21.0 172.9 %copy-start.8 = (f32[96,128]{1,0:T(8,128)}, f32[96,128]{1,0:T(8,128)S(1)}, u32[]{:S(2)}) copy-start(f32[96,128]{1,0:T(8,128)S(1)} %broadcast_in_dim.21.scale_ref) | copy-start | bytes 147460
  21.0 1.9 copy-start.2
  23.0 1.9 copy-start.3
  24.8 174.3 %copy-start.19 = (f32[768]{0:T(1024)S(1)}, f32[768]{0:T(1024)}, u32[]{:S(2)}) copy-start(f32[768]{0:T(1024)} %param.33) | copy-start | bytes 9220
  24.8 175.2 %copy-start.20 = (f32[768]{0:T(1024)S(1)}, f32[768]{0:T(1024)}, u32[]{:S(2)}) copy-start(f32[768]{0:T(1024)} %param.34) | copy-start | bytes 9220
  193.9 1.7 copy-start.4
  195.6 1.7 copy-start.5
  197.3 0.6 copy-start.9
  197.9 0.6 copy-start.10
  198.5 0.6 copy-start.11
  200.9 131.0 %copy-start.23 = (f32[96]{0:T(128)S(1)}, f32[96]{0:T(128)}, u32[]{:S(2)}) copy-start(f32[96]{0:T(128)} %param.38) | copy-start | bytes 1156
  471.7 19.0 %copy-start.18 = (f32[96,128]{1,0:T(8,128)S(1)}, f32[96,128]{1,0:T(8,128)}, u32[]{:S(2)}) copy-start(f32[96,128]{1,0:T(8,128)} %get-tuple-element.59) | copy-start | bytes 147460
  471.7 19.6 %copy-start.17 = (f32[96,128]{1,0:T(8,128)S(1)}, f32[96,128]{1,0:T(8,128)}, u32[]{:S(2)}) copy-start(f32[96,128]{1,0:T(8,128)} %get-tuple-element.65) | copy-start | bytes 147460
  471.8 20.9 %copy-start.16 = (f32[768,128]{1,0:T(8,128)S(1)}, f32[768,128]{1,0:T(8,128)}, u32[]{:S(2)}) copy-start(f32[768,128]{1,0:T(8,128)} %get-tuple-element.60) | copy-start | bytes 1179652
  471.8 21.0 %copy-start.15 = (f32[768,128]{1,0:T(8,128)S(1)}, f32[768,128]{1,0:T(8,128)}, u32[]{:S(2)}) copy-start(f32[768,128]{1,0:T(8,128)} %get-tuple-element.61) | copy-start | bytes 1179652
  489.5 3.5 copy-start.13
  558.2 6.4 %copy-start.26 = (f32[96]{0:T(128)S(1)}, f32[96]{0:T(128)}, u32[]{:S(2)}) copy-start(f32[96]{0:T(128)} %get-tuple-element.141) | copy-start | bytes 1156
  558.2 6.9 %copy-start.14 = (f32[4,96,768]{2,1,0:T(8,128)S(1)}, f32[4,96,768]{2,1,0:T(8,128)}, u32[]{:S(2)}) copy-start(f32[4,96,768]{2,1,0:T(8,128)} %get-tuple-element.63) | copy-start | bytes 3538948
  558.2 8.9 %copy-start.1 = (s32[4,2]{0,1:T(2,128)S(1)}, s32[4,2]{0,1:T(2,128)}, u32[]{:S(2)}) copy-start(s32[4,2]{0,1:T(2,128)} %param.22) | copy-start | bytes 100
  564.6 1.5 copy-start.25
  564.6 2.0 copy-start.24
Sparse Core Ops, SparseCore 0:
  492.7 49.6 all-reduce.3

commit v3 on v2

--- a/solution.py
+++ b/solution.py
@@ -307,18 +307,58 @@
     return value
 
 
-def taps_tile(rate, freq, real, imag, lag):
-    turns = freq * 0.15915494309189535
-    total = jnp.zeros((rate.shape[0], lag.shape[1]), jnp.float32)
-    for mode in range(rate.shape[1]):
-        one = slice(mode, mode + 1)
-        angle = turns[:, one] * lag
-        angle = angle - jnp.floor(angle + 0.5)
-        square = angle * angle
-        wave = real[:, one] * polynomial(cos_terms, square)
-        wave = wave - (imag[:, one] * angle) * polynomial(sin_terms, square)
-        total = total + jnp.exp(-rate[:, one] * lag) * wave
-    return total
+TILE = 16
+
+
+def power(rate, freq, lag):
+    angle = freq * 0.15915494309189535 * lag
+    angle = angle - jnp.floor(angle + 0.5)
+    square = angle * angle
+    decay = jnp.exp(-rate * lag)
+    return decay * polynomial(cos_terms, square), decay * (angle * polynomial(sin_terms, square))
+
+
+def product(left, right):
+    return left[0] * right[0] - left[1] * right[1], left[0] * right[1] + left[1] * right[0]
+
+
+def taps_lines(rate, freq, real, imag, side, store):
+    first = power(rate, freq, 1.0)
+
+    @pl.loop(0, side // TILE)
+    def _(tile):
+        state = product((real, imag), power(rate, freq, (tile * TILE).astype(jnp.float32)))
+        for step in range(TILE):
+            store(tile * TILE + step, jnp.sum(state[0], axis=0, keepdims=True))
+            state = product(state, first)
+
+
+def taps_adjoint(rate, freq, real, imag, side, load):
+    first = power(rate, freq, 1.0)
+
+    def tile_sums(tile, totals):
+        state = power(rate, freq, (tile * TILE).astype(jnp.float32))
+        even, odd, even_lag, odd_lag = totals
+        for step in range(TILE):
+            grad = load(tile * TILE + step)
+            late = grad * (tile * TILE + step).astype(jnp.float32)
+            even = even + grad * state[0]
+            odd = odd + grad * state[1]
+            even_lag = even_lag + late * state[0]
+            odd_lag = odd_lag + late * state[1]
+            state = product(state, first)
+        return even, odd, even_lag, odd_lag
+
+    zero = jnp.zeros_like(rate)
+    even, odd, even_lag, odd_lag = lax.fori_loop(0, side // TILE, tile_sums, (zero,) * 4)
+    return imag * odd_lag - real * even_lag, -real * odd_lag - imag * even_lag, even, -odd
+
+
+def lane_sums(values):
+    ones = jnp.ones((8, values.shape[1]), jnp.bfloat16)
+    high, rest = split_low(values)
+    low = (values - high.astype(jnp.float32) - rest.astype(jnp.float32)).astype(jnp.bfloat16)
+    return dot_nt(ones, high) + dot_nt(ones, rest) + dot_nt(ones, low)
 
 
 def meet(n, shares):
@@ -475,6 +515,7 @@
     mixed_stage,
     back_stage,
     wide,
+    taps,
     send_m,
     recv_m,
     send_b,
@@ -490,6 +531,7 @@
         n, shares, me, share, ((in_part_ref, in_whole_ref), (out_part_ref, out_whole_ref)), weight_sems
     )
     start_first()
+    taps[...] = jnp.zeros_like(taps)
     row_at = lax.broadcasted_iota(jnp.int32, (side, side), 0)
     col_at = lax.broadcasted_iota(jnp.int32, (side, side), 1)
     inside = (row_at < sizes_ref[0]) & (col_at < sizes_ref[1])
@@ -520,19 +562,18 @@
         turn(back_stage, part)
         send(back_stage, back_ref, part, send_b, recv_b)
 
-    lag = lax.broadcasted_iota(jnp.int32, (1, side), 1)
-    lag_back = jnp.where(lag == 0, 0, side - lag).astype(jnp.float32)
-    lag = lag.astype(jnp.float32)
-
-    @pl.loop(0, count // 8)
-    def _(tile):
-        few = pl.ds(pl.multiple_of(tile * 8, 8), 8)
-        rows = (rate_ref[few, :], freq_ref[few, :], real_ref[few, :], imag_ref[few, :])
-        cols = (cols_rate_ref[few, :], cols_freq_ref[few, :], cols_real_ref[few, :], cols_imag_ref[few, :])
-        rows_back_ref[few, :] = taps_tile(*rows, lag_back)
-        rows_ref[few, :] = taps_tile(*rows, lag)
-        cols_back_ref[few, :] = taps_tile(*cols, lag_back)
-        cols_ref[few, :] = taps_tile(*cols, lag)
+    for (rate, freq, real, imag), back_out, out in (
+        ((rate_ref, freq_ref, real_ref, imag_ref), rows_back_ref, rows_ref),
+        ((cols_rate_ref, cols_freq_ref, cols_real_ref, cols_imag_ref), cols_back_ref, cols_ref),
+    ):
+
+        def store(lag, line):
+            taps[0, pl.ds(lax.rem(side - lag, side), 1), :count] = line
+            taps[1, pl.ds(lag, 1), :count] = line
+
+        taps_lines(rate[...], freq[...], real[...], imag[...], side, store)
+        back_out[...] = taps[0].T[:count]
+        out[...] = taps[1].T[:count]
 
     start_second()
 
@@ -596,6 +637,7 @@
             pltpu.VMEM(shape, jnp.bfloat16),
             pltpu.VMEM(shape, jnp.bfloat16),
             pltpu.VMEM((GROUP * side, side), jnp.float32),
+            pltpu.VMEM((2, side, side), jnp.float32),
             pltpu.SemaphoreType.DMA((n,)),
             pltpu.SemaphoreType.DMA((n,)),
             pltpu.SemaphoreType.DMA((n,)),
@@ -640,8 +682,7 @@
     branch_ref,
     active_ref,
     before_grad_ref,
-    out_own_ref,
-    out_got_ref,
+    out_take_ref,
     in_own_ref,
     in_got_ref,
     gain_grad_ref,
@@ -659,6 +700,7 @@
     hidden_sum,
     pieces,
     rows_stage,
+    out_got,
     send_g,
     recv_g,
     own_sem,
@@ -667,6 +709,8 @@
     half_sem,
     send_h,
     recv_h,
+    send_2,
+    recv_2,
 ):
     side = mixed_ref.shape[-1]
     groups = mixed_ref.shape[1]
@@ -677,7 +721,7 @@
     width = LINES * side
     parts = hidden // STEP_HIDDEN
     ring = active_ring.shape[0]
-    me, _ = meet(n, shares)
+    me, share = meet(n, shares)
     core = lax.rem(me, 2)
     sibling = me + 1 - 2 * core
     gain_grad_ref[...] = jnp.zeros_like(gain_grad_ref)
@@ -779,16 +823,17 @@
             copy.wait()
 
     half = parts // 2
-
     kinds = (
-        (active_ref, cots_keep, out_own_ref, out_got_ref, channels),
+        (active_ref, cots_keep, None, out_got, channels),
         (before_grad_ref, normed_keep, in_own_ref, in_got_ref, channels + side),
     )
 
-    def fetch(whole, job, slot):
-        place = lax.rem((1 - core) * half + job, parts)
-        span = pl.ds(pl.multiple_of(place * STEP_HIDDEN, STEP_HIDDEN), STEP_HIDDEN)
-        return pltpu.make_async_copy(whole.at[:, span], pieces.at[slot], piece_sem.at[slot])
+    def place(job):
+        at = lax.rem((1 - core) * half + job, parts)
+        return pl.ds(pl.multiple_of(at * STEP_HIDDEN, STEP_HIDDEN), STEP_HIDDEN)
+
+    def fetch(kind, job, slot):
+        return pltpu.make_async_copy(kinds[kind][0].at[:, place(job)], pieces.at[slot], piece_sem.at[slot])
 
     def give(kind, job):
         _, _, _, got, wide = kinds[kind]
@@ -800,35 +845,52 @@
             chan=sibling,
         )
 
-    def keep(kind, job):
-        _, _, own, _, wide = kinds[kind]
+    def keep(job):
         return pltpu.make_async_copy(
-            rows_stage.at[job, :, pl.ds(0, wide)],
-            own.at[pl.ds((job - half) * STEP_HIDDEN, STEP_HIDDEN)],
-            half_sem.at[kind, job],
-        )
+            rows_stage.at[job],
+            in_own_ref.at[pl.ds((job - half) * STEP_HIDDEN, STEP_HIDDEN)],
+            half_sem.at[job],
+        )
+
+    block_rows = hidden // 2 // shares
+
+    def second(turn):
+        peer = lax.rem(share + turn, shares)
+        span = pl.ds(pl.multiple_of(peer * block_rows, block_rows), block_rows)
+        if turn == 0:
+            return pltpu.make_async_copy(out_got.at[span], out_take_ref.at[0], send_2.at[0])
+        return push(out_got.at[span], out_take_ref.at[turn], send_2.at[turn], recv_2.at[turn], dp=peer)
 
     jobs = [(kind, job) for kind in range(2) for job in range(parts)]
-    fetch(kinds[0][0], 0, 0).start()
+    fetch(0, 0, 0).start()
     for at, (kind, job) in enumerate(jobs):
-        whole, right = kinds[kind][:2]
         slot = at % 2
         if at + 1 < len(jobs):
-            fetch(kinds[jobs[at + 1][0]][0], jobs[at + 1][1], (at + 1) % 2).start()
-        fetch(whole, job, slot).wait()
-        if kind == 1:
-            (give if job < half else keep)(0, job).wait()
+            fetch(*jobs[at + 1], (at + 1) % 2).start()
+        if at == parts:
+            for done in range(half):
+                give(0, done).wait()
+                span = pl.ds(done * STEP_HIDDEN, STEP_HIDDEN)
+                mine = rows_stage[half + done, :, :channels].astype(jnp.float32)
+                out_got[span, :] = (mine + out_got[span, :].astype(jnp.float32)).astype(jnp.bfloat16)
+            for turn in range(shares):
+                second(turn).start()
+        fetch(kind, job, slot).wait()
+        right = kinds[kind][1]
         total = dot_nt(pieces[slot, 0], right[0])
         for step in range(1, steps):
             total = total + dot_nt(pieces[slot, step], right[step])
         rows_stage[job, :, :channels] = total.astype(jnp.bfloat16)
         if kind == 1:
-            place = lax.rem((1 - core) * half + job, parts)
-            span = pl.ds(pl.multiple_of(place * STEP_HIDDEN, STEP_HIDDEN), STEP_HIDDEN)
-            rows_stage[job, :, channels:] = hidden_sum[span, :].astype(jnp.bfloat16)
-        (give if job < half else keep)(kind, job).start()
+            rows_stage[job, :, channels:] = hidden_sum[place(job), :].astype(jnp.bfloat16)
+        if job < half:
+            give(kind, job).start()
+        elif kind == 1:
+            keep(job).start()
     for job in range(parts):
-        (give if job < half else keep)(1, job).wait()
+        (give(1, job) if job < half else keep(job)).wait()
+    for turn in range(shares):
+        second(turn).wait()
     own_g.wait()
     own_r.wait()
     wait_parts(grad_stage, grad_ref, me, n, send_g, recv_g)
@@ -853,15 +915,14 @@
             low(shape),
             low((steps, hidden, width)),
             low((steps, hidden, width)),
-            low((hidden // 2, channels)),
-            low((hidden // 2, channels)),
+            low((shares, hidden // 2 // shares, channels)),
             low((hidden // 2, channels + side)),
             low((hidden // 2, channels + side)),
             jax.ShapeDtypeStruct((channels, side), jnp.float32),
             jax.ShapeDtypeStruct((channels, side), jnp.float32),
         ),
         in_specs=[vmem] * 6,
-        out_specs=(hbm,) * 8 + (vmem, vmem),
+        out_specs=(hbm,) * 7 + (vmem, vmem),
         scratch_shapes=[
             pltpu.VMEM(shape, jnp.bfloat16),
             pltpu.VMEM(shape, jnp.bfloat16),
@@ -876,14 +937,17 @@
             pltpu.VMEM((hidden, side), jnp.float32),
             pltpu.VMEM((2, steps, STEP_HIDDEN, width), jnp.bfloat16),
             pltpu.VMEM((parts, STEP_HIDDEN, channels + side), jnp.bfloat16),
+            pltpu.VMEM((hidden // 2, channels), jnp.bfloat16),
             pltpu.SemaphoreType.DMA((n,)),
             pltpu.SemaphoreType.DMA((n,)),
             pltpu.SemaphoreType.DMA((2,)),
             pltpu.SemaphoreType.DMA((2, ring)),
             pltpu.SemaphoreType.DMA((2,)),
+            pltpu.SemaphoreType.DMA((parts,)),
             pltpu.SemaphoreType.DMA((2, parts)),
             pltpu.SemaphoreType.DMA((2, parts)),
-            pltpu.SemaphoreType.DMA((2, parts)),
+            pltpu.SemaphoreType.DMA((shares,)),
+            pltpu.SemaphoreType.DMA((shares,)),
         ],
         compiler_params=pltpu.CompilerParams(
             collective_id=1, has_side_effects=True, vmem_limit_bytes=63 * mebi
@@ -892,16 +956,9 @@
     )(mixed, back, in_full, out_full, gain, shift)
 
 
-def sum_rounds(n, shares, me, share, own, got, final, stage2, take2, stage3, take3, keep3, sems):
+def sum_rounds(n, shares, me, share, part, final, stage3, take3, keep3, send3, recv3, send4, recv4, own_sem):
     near, far = n // 2, me // 2
     core = lax.rem(me, 2)
-    send2, recv2, send3, recv3, send4, recv4, own_sem = sems
-    rows = keep3.shape[0]
-    block = near * rows
-
-    def second(turn):
-        peer = lax.rem(share + turn, shares)
-        return push(stage2.at[peer], take2.at[turn], send2.at[turn], recv2.at[turn], dp=peer)
 
     def third(turn):
         peer = lax.rem(far + turn, near)
@@ -915,22 +972,9 @@
     def mine():
         return pltpu.make_async_copy(keep3, final.at[share], own_sem.at[0])
 
-    def start_second():
-        for at in range(shares):
-            span = slice(at * block, (at + 1) * block)
-            stage2[at] = (own[span].astype(jnp.float32) + got[span].astype(jnp.float32)).astype(jnp.bfloat16)
-        for turn in range(1, shares):
-            second(turn).start()
-
     def start_third():
-        for turn in range(1, shares):
-            second(turn).wait()
         for at in range(near):
-            base = pl.ds(pl.multiple_of(share * block + at * rows, rows), rows)
-            span = slice(at * rows, (at + 1) * rows)
-            total = own[base, :].astype(jnp.float32) + got[base, :].astype(jnp.float32)
-            for turn in range(1, shares):
-                total = total + take2[turn, span].astype(jnp.float32)
+            total = part(at)
             stage3[at] = total.astype(jnp.bfloat16)
 
             @pl.when(far == at)
@@ -957,7 +1001,7 @@
             fourth(turn, True).wait_recv()
             fourth(turn).wait_send()
 
-    return start_second, start_third, start_fourth, finish
+    return start_third, start_fourth, finish
 
 
 def back_kernel(
@@ -974,48 +1018,125 @@
     skip_ref,
     scale_ref,
     bias_ref,
-    out_own_ref,
-    out_got_ref,
+    bias_sums_ref,
+    gain_sums_ref,
+    shift_sums_ref,
+    out_take_ref,
     in_own_ref,
     in_got_ref,
     output_ref,
     input_grad_ref,
-    rows_sums_ref,
-    cols_sums_ref,
-    skip_sums_ref,
-    scale_sums_ref,
+    small_ref,
+    norm_ref,
     out_final_ref,
     in_final_ref,
     wide,
     branch_got,
+    rows_sums,
+    cols_sums,
+    skip_sums,
+    scale_sums,
+    small_own,
+    small_got,
+    norm_own,
+    norm_near,
+    norm_mid,
+    norm_far,
+    stage2,
+    take2,
+    out_stage3,
+    out_take3,
+    out_keep3,
+    in_stage3,
+    in_take3,
+    in_keep3,
     send_sem,
     recv_sem,
     own_sem,
-    *rest,
+    send_2,
+    recv_2,
+    send_s,
+    recv_s,
+    send_n,
+    recv_n,
+    send_f,
+    recv_f,
+    *round_sems,
 ):
     count, side, _ = image_ref.shape
     steps, lines = branch_ref.shape[1], branch_ref.shape[2]
+    near = n // 2
+    rows = in_keep3.shape[0]
+    block = near * rows
     me, share = meet(n, shares)
-    out_rounds = sum_rounds(
-        n, shares, me, share, out_own_ref, out_got_ref, out_final_ref, *rest[:5], rest[10:17]
-    )
-    in_rounds = sum_rounds(
-        n, shares, me, share, in_own_ref, in_got_ref, in_final_ref, *rest[5:10], rest[17:24]
-    )
-    out_rounds[0]()
+
+    def out_part(at):
+        span = slice(at * rows, (at + 1) * rows)
+        return sum(out_take_ref[turn, span].astype(jnp.float32) for turn in range(shares))
+
+    def in_part(at):
+        base = pl.ds(pl.multiple_of(share * block + at * rows, rows), rows)
+        total = in_own_ref[base, :].astype(jnp.float32) + in_got_ref[base, :].astype(jnp.float32)
+        for turn in range(1, shares):
+            total = total + take2[turn, at * rows : (at + 1) * rows].astype(jnp.float32)
+        return total
+
+    out_third, out_fourth, out_finish = sum_rounds(
+        n, shares, me, share, out_part, out_final_ref, out_stage3, out_take3, out_keep3, *round_sems[:5]
+    )
+    in_third, in_fourth, in_finish = sum_rounds(
+        n, shares, me, share, in_part, in_final_ref, in_stage3, in_take3, in_keep3, *round_sems[5:]
+    )
+
+    def in_second(turn):
+        peer = lax.rem(share + turn, shares)
+        return push(stage2.at[peer], take2.at[turn], send_2.at[turn], recv_2.at[turn], dp=peer)
+
+    def norm_first(turn):
+        peer = lax.rem(share + turn, shares)
+        return push(norm_own, norm_near.at[turn], send_n.at[turn], recv_n.at[turn], dp=peer)
+
+    def norm_second(turn):
+        peer = lax.rem(me + turn, n)
+        return push(norm_mid, norm_far.at[turn], send_f.at[turn], recv_f.at[turn], chan=peer)
+
+    def small_push(turn):
+        peer = lax.rem(share + turn, shares)
+        return push(small_own, small_got.at[turn], send_s.at[turn], recv_s.at[turn], dp=peer)
+
+    def norm_pass():
+        total = norm_own[...]
+        for turn in range(1, shares):
+            norm_first(turn).wait()
+            total = total + norm_near[turn]
+        norm_mid[...] = total
+        for turn in range(1, n):
+            norm_second(turn).start()
+
+    def in_pass():
+        for turn in range(1, shares):
+            in_second(turn).wait()
+        in_third()
+
+    out_third()
+    for at in range(shares):
+        span = slice(at * block, (at + 1) * block)
+        stage2[at] = (in_own_ref[span].astype(jnp.float32) + in_got_ref[span].astype(jnp.float32)).astype(
+            jnp.bfloat16
+        )
+    for turn in range(1, shares):
+        in_second(turn).start()
+    top = lax.broadcasted_iota(jnp.int32, norm_own.shape, 0) == 0
+    norm_own[...] = jnp.where(top, lane_sums(gain_sums_ref[...]), lane_sums(shift_sums_ref[...]))
+    for turn in range(1, shares):
+        norm_first(turn).start()
     for shift in range(1, n):
         peer = lax.rem(me + shift, n)
-        pltpu.make_async_remote_copy(
-            src_ref=branch_ref.at[peer],
-            dst_ref=branch_got.at[me],
-            send_sem=send_sem.at[shift],
-            recv_sem=recv_sem.at[shift],
-            device_id={"chan": peer},
-            device_id_type=MESH,
+        push(
+            branch_ref.at[peer], branch_got.at[me], send_sem.at[shift], recv_sem.at[shift], chan=peer
         ).start()
     own = pltpu.make_async_copy(branch_ref.at[me], branch_got.at[me], own_sem.at[0])
     own.start()
-    in_rounds[0]()
     row_at = lax.broadcasted_iota(jnp.int32, (side, side), 0)
     col_at = lax.broadcasted_iota(jnp.int32, (side, side), 1)
     inside = (row_at < sizes_ref[0]) & (col_at < sizes_ref[1])
@@ -1030,15 +1151,15 @@
 
     @pl.loop(0, count)
     def _(chan):
-        pl.when(chan == count // 2)(out_rounds[1])
-        pl.when(chan == count * 3 // 4)(out_rounds[2])
-        pl.when(chan == count * 15 // 16)(in_rounds[1])
+        pl.when(chan == count // 3)(out_fourth)
+        pl.when(chan == count // 3)(norm_pass)
+        pl.when(chan == count * 3 // 4)(in_pass)
         one = pl.ds(chan, 1)
         grad = wide[pl.ds(chan, side, stride=count), :]
         image = image_ref[chan].astype(jnp.float32)
         grad_out = jnp.where(inside, cot_ref[chan].astype(jnp.float32), 0.0)
         masked = jnp.where(inside, image, 0.0)
-        skip_sums_ref[one, :] = jnp.sum(grad * masked, axis=0, keepdims=True)
+        skip_sums[one, :] = jnp.sum(grad * masked, axis=0, keepdims=True)
         masked_low = masked.astype(jnp.bfloat16)
         grad_low = grad.astype(jnp.bfloat16)
         grad_turned = dot_nt(flip, grad_low).astype(jnp.bfloat16)
@@ -1070,9 +1191,12 @@
         ) + dot_nn(turned_high, grad_rest)
         masked_grad = masked_grad + skip_ref[one, :] * grad
         input_grad_ref[chan] = jnp.where(inside, grad_out + masked_grad, 0.0)
-        rows_sums_ref[one, :] = lag_sums(rows_grad, side, row_at + col_at >= side - 1)
-        cols_sums_ref[one, :] = lag_sums(cols_grad, side, row_at + col_at <= side - 1)
-
+        rows_sums[one, :] = lag_sums(rows_grad, side, row_at + col_at >= side - 1)
+        cols_sums[one, :] = lag_sums(cols_grad, side, row_at + col_at <= side - 1)
+
+    small_own[:, :side] = rows_sums[...]
+    small_own[:, side : 2 * side] = cols_sums[...]
+    in_fourth()
     own.wait()
     for shift in range(1, n):
         peer = lax.rem(me + shift, n)
@@ -1098,62 +1222,131 @@
         image = image_ref[chan].astype(jnp.float32)
         grad_out = jnp.where(inside, cot_ref[chan].astype(jnp.float32), 0.0)
         output_ref[chan] = jnp.where(inside, image + scale_ref[one, :] * shifted, 0.0).astype(jnp.bfloat16)
-        scale_sums_ref[one, :] = jnp.sum(grad_out * shifted, axis=0, keepdims=True)
-
-    in_rounds[2]()
-    out_rounds[3]()
-    in_rounds[3]()
-
-
-def mixer_back(n, shares, sizes, images, cotangent, grad, branch, lines, halves):
+        scale_sums[one, :] = jnp.sum(grad_out * shifted, axis=0, keepdims=True)
+
+    lane = lax.broadcasted_iota(jnp.int32, (count, side), 1)
+    last = jnp.zeros((count, side), jnp.float32)
+    for at, sums in enumerate((skip_sums, bias_sums_ref, scale_sums)):
+        last = jnp.where(lane == at, jnp.sum(sums[...], axis=1, keepdims=True), last)
+    small_own[:, 2 * side :] = last
+    for turn in range(1, shares):
+        small_push(turn).start()
+    total = norm_mid[...]
+    for turn in range(1, n):
+        norm_second(turn).wait()
+        total = total + norm_far[turn]
+    norm_ref[...] = total
+    out_finish()
+    in_finish()
+    total = small_own[...]
+    for turn in range(1, shares):
+        small_push(turn).wait()
+        total = total + small_got[turn]
+    small_ref[...] = total
+
+
+def mixer_back(n, shares, sizes, images, cotangent, grad, branch, lines, norms, sums):
     count, side, _ = images.shape
     near = n // 2
-    rows = halves[0].shape[0] // (shares * near)
-    wides = (halves[0].shape[1], halves[2].shape[1])
+    out_take, in_own, _ = sums
+    block, channels = out_take.shape[1:]
+    rows = block // near
+    wide = in_own.shape[1]
+    line = pltpu.VMEM((count, side), jnp.float32)
+    norm = pltpu.VMEM((8, channels), jnp.float32)
+    vmem = pl.BlockSpec(memory_space=pltpu.VMEM)
     hbm = pl.BlockSpec(memory_space=pl.ANY)
-    line = jax.ShapeDtypeStruct((count, side), jnp.float32)
-    vmem = pl.BlockSpec(memory_space=pltpu.VMEM)
+    full = functools.partial(jax.ShapeDtypeStruct, dtype=jnp.float32)
     return pl.pallas_call(
         functools.partial(back_kernel, n, shares),
         out_shape=(
             jax.ShapeDtypeStruct(images.shape, jnp.bfloat16),
-            jax.ShapeDtypeStruct(images.shape, jnp.float32),
+            full(images.shape),
+            full((count, 3 * side)),
+            full((8, channels)),
+            full((shares, rows, channels)),
+            full((shares, rows, wide)),
+        ),
+        in_specs=[pl.BlockSpec(memory_space=pltpu.SMEM)]
+        + [vmem] * 3
+        + [hbm]
+        + [vmem] * (len(lines) + len(norms) + len(sums)),
+        out_specs=(vmem,) * 4 + (hbm,) * 2,
+        scratch_shapes=[
+            pltpu.VMEM((count * side, side), jnp.float32),
+            pltpu.VMEM(branch.shape, jnp.bfloat16),
             line,
             line,
             line,
             line,
-        )
-        + tuple(jax.ShapeDtypeStruct((shares, rows, wide), jnp.float32) for wide in wides),
-        in_specs=[pl.BlockSpec(memory_space=pltpu.SMEM)] + [vmem] * 3 + [hbm] + [vmem] * 10,
-        out_specs=(vmem,) * 6 + (hbm,) * 2,
-        scratch_shapes=[
-            pltpu.VMEM((count * side, side), jnp.float32),
-            pltpu.VMEM(branch.shape, jnp.bfloat16),
-            pltpu.SemaphoreType.DMA((n,)),
-            pltpu.SemaphoreType.DMA((n,)),
-            pltpu.SemaphoreType.DMA((1,)),
+            pltpu.VMEM((count, 3 * side), jnp.float32),
+            pltpu.VMEM((shares, count, 3 * side), jnp.float32),
+            norm,
+            pltpu.VMEM((shares, 8, channels), jnp.float32),
+            norm,
+            pltpu.VMEM((n, 8, channels), jnp.float32),
+            pltpu.VMEM((shares, block, wide), jnp.bfloat16),
+            pltpu.VMEM((shares, block, wide), jnp.bfloat16),
         ]
         + [
             kind
-            for wide in wides
+            for columns in (channels, wide)
             for kind in (
-                pltpu.VMEM((shares, near * rows, wide), jnp.bfloat16),
-                pltpu.VMEM((shares, near * rows, wide), jnp.bfloat16),
-                pltpu.VMEM((near, rows, wide), jnp.bfloat16),
-                pltpu.VMEM((near, rows, wide), jnp.bfloat16),
-                pltpu.VMEM((rows, wide), jnp.float32),
+                pltpu.VMEM((near, rows, columns), jnp.bfloat16),
+                pltpu.VMEM((near, rows, columns), jnp.bfloat16),
+                pltpu.VMEM((rows, columns), jnp.float32),
             )
         ]
         + [
             pltpu.SemaphoreType.DMA((size,))
-            for _ in wides
-            for size in (shares, shares, near, near, shares, shares, 1)
+            for size in (n, n, 1, shares, shares, shares, shares, shares, shares, n, n)
+            + (near, near, shares, shares, 1) * 2
         ],
         compiler_params=pltpu.CompilerParams(
             collective_id=2, has_side_effects=True, vmem_limit_bytes=62 * mebi
         ),
         name="mixer_back",
-    )(sizes, images, cotangent, grad, branch, *lines, *halves)
+    )(sizes, images, cotangent, grad, branch, *lines, *norms, *sums)
+
+
+def taps_kernel(small_ref, *refs):
+    params, (*grads, rest_ref), wide = refs[:8], refs[8:17], refs[17]
+    count = small_ref.shape[0]
+    side = wide.shape[0]
+    wide[...] = jnp.zeros_like(wide)
+    turned = refs[18]
+
+    def turn(at):
+        wide[:count, :] = small_ref[:, at * side : (at + 1) * side]
+        turned[...] = wide[...].T
+
+    def rows_load(lag):
+        return turned[pl.ds(lax.rem(lag + side - 1, side), 1), :count]
+
+    def cols_load(lag):
+        return turned[pl.ds(side - 1 - lag, 1), :count]
+
+    for at, load in enumerate((rows_load, cols_load)):
+        turn(at)
+        found = taps_adjoint(*(ref[...] for ref in params[4 * at : 4 * at + 4]), side, load)
+        for ref, grad in zip(grads[4 * at : 4 * at + 4], found):
+            ref[...] = grad
+    turn(2)
+    rest_ref[...] = turned[:8, :count]
+
+
+def taps_back(small, params, side):
+    modes, count = params[0].shape
+    full = functools.partial(jax.ShapeDtypeStruct, dtype=jnp.float32)
+    vmem = pl.BlockSpec(memory_space=pltpu.VMEM)
+    return pl.pallas_call(
+        taps_kernel,
+        out_shape=(full((modes, count)),) * 8 + (full((8, count)),),
+        in_specs=[vmem] * 9,
+        out_specs=(vmem,) * 9,
+        scratch_shapes=[pltpu.VMEM((side, side), jnp.float32), pltpu.VMEM((side, side), jnp.float32)],
+        name="taps_back",
+    )(small, *params)
 
 
 def pixel_body(
@@ -1185,20 +1378,19 @@
     sizes = image_sizes[picked]
     image, cot = images[0], cotangent[0]
 
-    params = (
-        rows_rate,
-        rows_freq,
-        rows_real,
-        rows_imag,
-        cols_rate,
-        cols_freq,
-        cols_real,
-        cols_imag,
-    )
-
-    def both_taps(*params):
-        return kernel_taps(*params[:4], side), kernel_taps(*params[4:], side)
-
+    params = tuple(
+        param.T
+        for param in (
+            rows_rate,
+            rows_freq,
+            rows_real,
+            rows_imag,
+            cols_rate,
+            cols_freq,
+            cols_real,
+            cols_imag,
+        )
+    )
     skip_wide = jnp.broadcast_to(skip_gain[:, None], (count, side))
     scale_wide = jnp.broadcast_to(layer_scale[:, None], (count, side))
     bias_wide = jnp.broadcast_to(bias_out[:, None], (count, side))
@@ -1211,7 +1403,7 @@
     mixed, back, in_whole, out_whole, bias_out_sums, rows_back, rows, cols_back, _ = mixer_forward(
         n, shares, sizes, image, cot, params, skip_wide, scale_wide, in_part, out_part
     )
-    grad, branch, _, _, *halves, gain_sums, shift_sums = mlp(
+    grad, branch, _, _, *sums, gain_sums, shift_sums = mlp(
         n,
         shares,
         mixed,
@@ -1221,7 +1413,7 @@
         jnp.broadcast_to(norm_gain[:, None], (channels, side)),
         jnp.broadcast_to(norm_bias[:, None], (channels, side)),
     )
-    output, input_grad, rows_sums, cols_sums, skip_sums, scale_sums, out_final, in_final = mixer_back(
+    output, input_grad, small, norms, out_final, in_final = mixer_back(
         n,
         shares,
         sizes,
@@ -1230,35 +1422,23 @@
         grad.reshape(side, count, side),
         branch,
         (rows_back, rows, cols_back, skip_wide, scale_wide, bias_wide),
-        halves,
-    )
+        (bias_out_sums, gain_sums, shift_sums),
+        sums,
+    )
+    *params_grad, rest = taps_back(small, params, side)
     in_final = in_final.reshape(hidden, channels + side)
-    params_grad = jax.vjp(both_taps, *params)[1](
-        (jnp.roll(rows_sums, 1, axis=1), cols_sums[:, ::-1])
-    )
-    small = lax.psum(
-        (
-            *params_grad,
-            jnp.sum(skip_sums, axis=1),
-            jnp.sum(bias_out_sums, axis=1),
-            jnp.sum(scale_sums, axis=1),
-        ),
-        "dp",
-    )
-    gain_grad, shift_grad = lax.psum(
-        (jnp.sum(gain_sums, axis=1), jnp.sum(shift_sums, axis=1)), ("dp", "chan")
-    )
     return (
         output[None],
         input_grad[None],
-        *small[:9],
-        gain_grad,
-        shift_grad,
+        *(grad.T for grad in params_grad),
+        rest[0],
+        norms[0],
+        norms[1],
         in_final[:, :channels].T,
         jnp.sum(in_final[:, channels:], axis=1),
         out_final.reshape(hidden, channels),
-        small[9],
-        small[10],
+        rest[1],
+        rest[2],
     )
 
 
@@ -1267,6 +1447,7 @@
     fits = (
         slots == 1
         and side == 128
+        and count <= side
         and count % GROUP == 0
         and side % (n * LINES) == 0
         and n % 2 == 0

time: 584 us -> 490 us (0.84); the launches traced: 574 us -> 489 us
  blocking collectives: 40.6 us -> 0 us
  other arithmetic: 25.3 us -> 2.79 us
  between operations: 16.7 us -> 2.75 us
  local copies, waits for them, and re-layouts: 48.8 us -> 35.5 us
  Pallas kernels: 436 us -> 448 us
  waiting for transfers between devices: 6.56 us -> 0 us
    psum x1 -> x0, blocking collectives: 40.6 us -> none  [pixel_body(): lax.psum((jnp.sum(gain_sums, axis=1), jnp.sum(shift_sums, axis=1)), ('dp'...]
    reduce_sum x6 -> x0, other arithmetic: 19.9 us -> none  [the longest x1 17.7 us: kernel_taps(): imag_part[:, :, None] * jnp.sin(angles)]
    unnamed x77 -> x58, local copies, waits for them, and re-layouts: 41.7 us -> 24.9 us
    psum x1 -> x0, waiting for transfers between devices: 6.54 us -> none  [pixel_body(): lax.psum((*params_grad, jnp.sum(skip_sums, axis=1), jnp.sum(bias_out_sums...]
    pallas_call x1, Pallas kernels: 131 us -> 137 us  [mlp(): pl.pallas_call(functools.partial(mlp_kernel, n, shares), out_shape=(low(s...]
  transfers between devices with their start and end apart: 1 -> 0, of which waited for: 1 -> 0; matrix products, arithmetic and copies ran while one was open for 0% -> 0% of each run, Pallas kernels for 0% -> 0%
where the time goes in v3:
time: 490 us; the launch traced here: 489 us
  Pallas kernels  448 us (91%)
  local copies, waits for them, and re-layouts  35.5 us (7%)
    pallas_call x1, Pallas kernels, mixer_forward(): pl.pallas_call(functools.partial(mixer_kernel, n, shares), out_shape=(jax...  169 us
    pallas_call x1, Pallas kernels, mixer_back(): pl.pallas_call(functools.partial(back_kernel, n, shares), out_shape=(jax....  138 us
    pallas_call x1, Pallas kernels, mlp(): pl.pallas_call(functools.partial(mlp_kernel, n, shares), out_shape=(low(s...  137 us
    unnamed x58, local copies, waits for them, and re-layouts  24.9 us

profile of v3, /device:TPU:9, one launch (start us, length us, event | category | flops | bytes accessed | tf_op | source)
XLA Modules:
  0.0 489.3 jit_solution(1628585725832361935)
XLA Ops:
  0.7 0.0 copy-start
  0.7 0.0 copy-start.6
  0.7 1.3 dynamic_slice.6
  3.9 0.0 copy-done
  3.9 0.2 dynamic-slice_reduce_fusion.sizes_ref
  4.1 0.7 broadcast_in_dim.16.skip_ref
  4.9 0.0 copy-start.7
  4.9 0.8 broadcast_in_dim.17.scale_ref
  5.6 0.0 copy-start.8
  5.6 0.7 broadcast_in_dim.18
  6.3 1.1 pad_maximum_fusion
  7.5 0.4 copy.38
  7.8 0.0 copy-done.6
  7.8 0.0 copy-start.2
  7.9 1.9 copy-done.2
  9.7 0.0 copy-start.3
  9.7 1.9 copy-done.3
  11.6 0.0 copy-start.9
  11.6 0.7 copy-done.9
  12.3 0.0 copy-start.10
  12.4 0.7 copy-done.10
  13.1 0.0 copy-start.11
  13.1 0.7 copy-done.11
  13.8 0.0 copy-start.12
  13.8 0.7 copy-done.12
  14.5 0.0 copy-start.13
  14.5 0.7 copy-done.13
  15.2 0.0 copy-start.14
  15.2 0.7 copy-done.14
  15.9 0.0 copy-start.15
  15.9 0.7 copy-done.15
  16.7 0.0 copy-start.16
  16.7 0.7 copy-done.16
  17.4 169.1 %mixer_forward.1 = (bf16[8,6,16,16,128]{4,3,2,1,0:T(8,128)(2,1)S(1)}, bf16[8,6,16,16,128]{4,3,2,1,0:T(8,128)(2,1)S(1)}, bf16[2,4,4,96,896]{4,3,2,1,0:T(8,128)(2,...) custom-call(s32[2]{0:T(128)S(1)} %dynamic-slice_reduce_fusion.sizes_, ...), custom_call_target="tpu_custom_call" | custom-call | tf_op jit(solution)/shard_map/mixer_forward/pallas_call | solution.py:623
  186.4 0.0 copy-done.21
  186.5 0.0 copy-done.7
  186.5 0.0 copy-done.8
  186.5 0.0 copy-start.4
  186.5 1.7 copy-done.4
  188.1 1.7 copy-done.5
  189.8 0.6 copy-done.17
  190.4 0.6 copy-done.18
  191.0 0.6 copy-done.19
  191.7 0.6 copy-done.20
  192.3 0.0 copy-done.24
  192.3 0.9 broadcast_in_dim.19.gain_ref
  193.2 0.0 copy-done.25
  193.2 0.9 broadcast_in_dim.20.shift_ref
  194.1 137.1 %mlp.1 = (bf16[8,4,4,96,128]{4,3,2,1,0:T(8,128)(2,1)}, bf16[8,4,4,96,128]{4,3,2,1,0:T(8,128)(2,1)}, bf16[4,3072,512]{2,1,0:T(8,128)(2,1)}, bf16[4,3072,512]{2,1,...) custom-call(bf16[8,6,16,16,128]{4,3,2,1,0:T(8,128)(2,1)} %copy-done., ...), custom_call_target="tpu_custom_call" | custom-call | tf_op jit(solution)/shard_map/mlp/pallas_call | solution.py:911
  331.3 0.0 copy-done.26
  331.3 0.7 broadcast_in_dim.21.bias_ref
  332.0 137.8 %mixer_back.1 = (bf16[96,128,128]{2,1,0:T(8,128)(2,1)}, f32[96,128,128]{2,1,0:T(8,128)}, f32[96,384]{1,0:T(8,128)}, f32[8,768]{1,0:T(8,128)}, f32[4,96,768]{2,1,0:T(8,128)}, /*index=5*/f32[4,96,896]{2,1,0:T(8,128)}) custom-call(s32[2]{0:T(128)} %copy-done.21, bf16[96,128,128]{2,1,0:T(8,128)(2,1)} %bitcast.36, bf16[96,128,128]{2,1,0:T(8,128)(2,1)} %bitcast.38, ...), custom_call_target="tpu_custom_call" | custom-call | tf_op jit(solution)/shard_map/mixer_back/pallas_call | solution.py:1260
  469.8 1.3 slice.28
  471.1 1.4 copy.40
  472.5 4.2 taps_back.1
  476.7 1.3 slice_bitcast_fusion
  478.1 1.4 slice_reduce_fusion.1
  479.5 1.6 slice_reduce_fusion
  481.1 4.1 copy.44
  485.3 0.3 copy-done.22
  485.6 2.7 copy.45
  488.3 0.0 copy-done.23
  488.3 1.0 copy.46
  489.3 0.0 copy-done.1
  (12 shorter events, 0.0 us)
Async XLA Ops:
  0.7 3.3 copy-start
  0.7 7.2 %copy-start.6 = (bf16[384,768]{1,0:T(8,128)(2,1)S(1)}, bf16[384,768]{1,0:T(8,128)(2,1)}, u32[]{:S(2)}) copy-start(bf16[384,768]{1,0:T(8,128)(2,1)} %param.37) | copy-start | bytes 1769476
  4.1 182.3 %copy-start.21 = (s32[2]{0:T(128)}, s32[2]{0:T(128)S(1)}, u32[]{:S(2)}) copy-start(s32[2]{0:T(128)S(1)} %dynamic-slice_reduce_fusion.sizes_ref) | copy-start | bytes 28
  4.9 181.6 %copy-start.7 = (f32[96,128]{1,0:T(8,128)}, f32[96,128]{1,0:T(8,128)S(1)}, u32[]{:S(2)}) copy-start(f32[96,128]{1,0:T(8,128)S(1)} %broadcast_in_dim.16.skip_ref) | copy-start | bytes 147460
  5.6 180.9 %copy-start.8 = (f32[96,128]{1,0:T(8,128)}, f32[96,128]{1,0:T(8,128)S(1)}, u32[]{:S(2)}) copy-start(f32[96,128]{1,0:T(8,128)S(1)} %broadcast_in_dim.17.scale_ref) | copy-start | bytes 147460
  7.8 1.9 copy-start.2
  9.7 1.9 copy-start.3
  11.6 0.7 copy-start.9
  12.3 0.7 copy-start.10
  13.1 0.7 copy-start.11
  13.8 0.7 copy-start.12
  14.5 0.7 copy-start.13
  15.2 0.7 copy-start.14
  15.9 0.7 copy-start.15
  16.7 0.7 copy-start.16
  17.4 174.9 %copy-start.24 = (f32[768]{0:T(1024)S(1)}, f32[768]{0:T(1024)}, u32[]{:S(2)}) copy-start(f32[768]{0:T(1024)} %param.33) | copy-start | bytes 9220
  17.4 175.8 %copy-start.25 = (f32[768]{0:T(1024)S(1)}, f32[768]{0:T(1024)}, u32[]{:S(2)}) copy-start(f32[768]{0:T(1024)} %param.34) | copy-start | bytes 9220
  186.5 1.7 copy-start.4
  188.1 1.7 copy-start.5
  189.8 0.6 copy-start.17
  190.4 0.6 copy-start.18
  191.0 0.6 copy-start.19
  191.7 0.6 copy-start.20
  194.1 137.2 %copy-start.26 = (f32[96]{0:T(128)S(1)}, f32[96]{0:T(128)}, u32[]{:S(2)}) copy-start(f32[96]{0:T(128)} %param.38) | copy-start | bytes 1156
  481.1 4.4 copy-start.22
  485.6 2.7 copy-start.23
  485.6 3.7 copy-start.1

commit v4 on v3

--- a/solution.py
+++ b/solution.py
@@ -262,6 +262,7 @@
 
 MESH = pl.DeviceIdType.MESH
 GROUP = 16
+ABREAST = 2
 LINES = 4
 STEP_HIDDEN = 512
 mebi = 1024 * 1024
@@ -491,19 +492,26 @@
     sizes_ref,
     image_ref,
     cot_ref,
-    rate_ref,
-    freq_ref,
-    real_ref,
-    imag_ref,
-    cols_rate_ref,
-    cols_freq_ref,
-    cols_real_ref,
-    cols_imag_ref,
     skip_ref,
     scale_ref,
+    *rest,
+):
+    mixer_body(n, shares, sizes_ref, image_ref, cot_ref, skip_ref, scale_ref, rest[:8], *rest[8:])
+
+
+def mixer_body(
+    n,
+    shares,
+    sizes_ref,
+    image_ref,
+    cot_ref,
+    skip_ref,
+    scale_ref,
+    param_refs,
     in_part_ref,
     out_part_ref,
     mixed_ref,
+    first_ref,
     back_ref,
     in_whole_ref,
     out_whole_ref,
@@ -516,11 +524,14 @@
     back_stage,
     wide,
     taps,
+    params_got,
+    params_sem,
     send_m,
     recv_m,
     send_b,
     recv_b,
     own_sem,
+    keep_sem,
     *weight_sems,
 ):
     count, side, _ = image_ref.shape
@@ -531,6 +542,11 @@
         n, shares, me, share, ((in_part_ref, in_whole_ref), (out_part_ref, out_whole_ref)), weight_sems
     )
     start_first()
+    param_copies = [
+        pltpu.make_async_copy(ref, params_got.at[at], params_sem.at[at]) for at, ref in enumerate(param_refs)
+    ]
+    for copy in param_copies:
+        copy.start()
     taps[...] = jnp.zeros_like(taps)
     row_at = lax.broadcasted_iota(jnp.int32, (side, side), 0)
     col_at = lax.broadcasted_iota(jnp.int32, (side, side), 1)
@@ -549,38 +565,37 @@
         for shift in range(1, n):
             send_part(stage, target, me, lax.rem(me + shift, n), part, send_sem, recv_sem, shift).start()
 
-    @pl.loop(0, parts)
-    def _(part):
-        @pl.loop(0, GROUP)
-        def _(item):
-            chan = part * GROUP + item
-            grad_out = jnp.where(inside, cot_ref[chan].astype(jnp.float32), 0.0)
-            scaled = grad_out * scale_ref[pl.ds(chan, 1), :]
-            sums_ref[pl.ds(chan, 1), :] = jnp.sum(scaled, axis=0, keepdims=True)
-            wide[pl.ds(pl.multiple_of(item * side, side), side), :] = scaled
-
-        turn(back_stage, part)
-        send(back_stage, back_ref, part, send_b, recv_b)
-
-    for (rate, freq, real, imag), back_out, out in (
-        ((rate_ref, freq_ref, real_ref, imag_ref), rows_back_ref, rows_ref),
-        ((cols_rate_ref, cols_freq_ref, cols_real_ref, cols_imag_ref), cols_back_ref, cols_ref),
-    ):
+    def own_back(part):
+        return pltpu.make_async_copy(back_stage.at[:, part], back_ref.at[:, part], keep_sem.at[part])
+
+    def first_push(shift, back=False):
+        peer = lax.rem(me + shift, n)
+        return push(
+            back_stage.at[peer, :, pl.ds(0, LINES)],
+            first_ref.at[lax.rem(me + n - shift, n) if back else me],
+            send_b.at[shift],
+            recv_b.at[shift],
+            chan=peer,
+        )
+
+    for copy in param_copies:
+        copy.wait()
+    for axis, (back_out, out) in enumerate(((rows_back_ref, rows_ref), (cols_back_ref, cols_ref))):
 
         def store(lag, line):
             taps[0, pl.ds(lax.rem(side - lag, side), 1), :count] = line
             taps[1, pl.ds(lag, 1), :count] = line
 
-        taps_lines(rate[...], freq[...], real[...], imag[...], side, store)
+        taps_lines(*(params_got[4 * axis + at] for at in range(4)), side, store)
         back_out[...] = taps[0].T[:count]
         out[...] = taps[1].T[:count]
 
-    start_second()
 
     @pl.loop(0, parts)
     def _(part):
-        @pl.loop(0, GROUP)
-        def _(item):
+        pl.when(part == parts // 2)(start_second)
+
+        def one_channel(item):
             chan = part * GROUP + item
             masked = jnp.where(inside, image_ref[chan].astype(jnp.float32), 0.0)
             masked_low = masked.astype(jnp.bfloat16)
@@ -595,35 +610,62 @@
                 jnp.concatenate([along_high, along_low], axis=1),
                 jnp.concatenate([cols_high, cols_high], axis=0),
             ) + dot_nn(along_high, cols_low)
-            mixed = mixed + skip_ref[pl.ds(chan, 1), :] * masked
+            mixed = mixed + skip_ref[chan] * masked
             wide[pl.ds(pl.multiple_of(item * side, side), side), :] = mixed
+
+        @pl.loop(0, GROUP // ABREAST)
+        def _(few):
+            for at in range(ABREAST):
+                one_channel(few * ABREAST + at)
 
         turn(mixed_stage, part)
         send(mixed_stage, mixed_ref, part, send_m, recv_m)
 
-    start_third()
-    own_b = pltpu.make_async_copy(back_stage.at[me], back_ref.at[me], own_sem.at[0])
+    @pl.loop(0, parts)
+    def _(part):
+        @pl.loop(0, GROUP)
+        def _(item):
+            chan = part * GROUP + item
+            grad_out = jnp.where(inside, cot_ref[chan].astype(jnp.float32), 0.0)
+            scaled = grad_out * scale_ref[chan]
+            sums_ref[pl.ds(chan, 1), :] = jnp.sum(scaled, axis=0, keepdims=True)
+            wide[pl.ds(pl.multiple_of(item * side, side), side), :] = scaled
+
+        turn(back_stage, part)
+        own_back(part).start()
+
+    for shift in range(1, n):
+        first_push(shift).start()
+    own_b = pltpu.make_async_copy(back_stage.at[me, :, pl.ds(0, LINES)], first_ref.at[me], own_sem.at[0])
     own_m = pltpu.make_async_copy(mixed_stage.at[me], mixed_ref.at[me], own_sem.at[1])
     own_b.start()
     own_m.start()
+    start_third()
+    for part in range(parts):
+        own_back(part).wait()
     own_b.wait()
     own_m.wait()
-    wait_parts(back_stage, back_ref, me, n, send_b, recv_b)
     wait_parts(mixed_stage, mixed_ref, me, n, send_m, recv_m)
+    for shift in range(1, n):
+        first_push(shift, True).wait_recv()
+        first_push(shift).wait_send()
     finish()
 
 
-def mixer_forward(n, shares, sizes, images, cotangent, params, skip_wide, scale_wide, in_part, out_part):
+def mixer_forward(n, shares, sizes, images, cotangent, skip, scale, params, in_part, out_part):
     near = n // 2
+    smem = pl.BlockSpec(memory_space=pltpu.SMEM)
     count, side, _ = images.shape
     line = jax.ShapeDtypeStruct((count, side), jnp.float32)
     shape = (n, count // GROUP, side // n, GROUP, side)
+    first_shape = (n, count // GROUP, LINES, GROUP, side)
     vmem = pl.BlockSpec(memory_space=pltpu.VMEM)
     hbm = pl.BlockSpec(memory_space=pl.ANY)
     return pl.pallas_call(
         functools.partial(mixer_kernel, n, shares),
         out_shape=(
             jax.ShapeDtypeStruct(shape, jnp.bfloat16),
+            jax.ShapeDtypeStruct(first_shape, jnp.bfloat16),
             jax.ShapeDtypeStruct(shape, jnp.bfloat16),
         )
         + tuple(
@@ -631,18 +673,21 @@
             for part in (in_part, out_part)
         )
         + (line,) * 5,
-        in_specs=[pl.BlockSpec(memory_space=pltpu.SMEM)] + [vmem] * 12 + [hbm] * 2,
-        out_specs=(hbm,) * 4 + (vmem,) * 5,
+        in_specs=[smem] + [vmem] * 2 + [smem] * 2 + [hbm] * 10,
+        out_specs=(hbm,) * 5 + (vmem,) * 5,
         scratch_shapes=[
             pltpu.VMEM(shape, jnp.bfloat16),
             pltpu.VMEM(shape, jnp.bfloat16),
             pltpu.VMEM((GROUP * side, side), jnp.float32),
             pltpu.VMEM((2, side, side), jnp.float32),
+            pltpu.VMEM((8, *params[0].shape), jnp.float32),
+            pltpu.SemaphoreType.DMA((8,)),
             pltpu.SemaphoreType.DMA((n,)),
             pltpu.SemaphoreType.DMA((n,)),
             pltpu.SemaphoreType.DMA((n,)),
             pltpu.SemaphoreType.DMA((n,)),
             pltpu.SemaphoreType.DMA((2,)),
+            pltpu.SemaphoreType.DMA((count // GROUP,)),
             pltpu.SemaphoreType.DMA((2,)),
             pltpu.SemaphoreType.DMA((2, near)),
             pltpu.SemaphoreType.DMA((2, near)),
@@ -655,7 +700,7 @@
             collective_id=0, has_side_effects=True, vmem_limit_bytes=40 * mebi
         ),
         name="mixer_forward",
-    )(sizes, images, cotangent, *params, skip_wide, scale_wide, in_part, out_part)
+    )(sizes, images, cotangent, skip, scale, *params, in_part, out_part)
 
 
 def gelu_parts(value):
@@ -673,18 +718,19 @@
     n,
     shares,
     mixed_ref,
-    back_ref,
+    first_ref,
     in_ref,
     out_ref,
     gain_ref,
     shift_ref,
+    back_ref,
     grad_ref,
+    branch_sent_ref,
     branch_ref,
     active_ref,
     before_grad_ref,
     out_take_ref,
-    in_own_ref,
-    in_got_ref,
+    in_half_ref,
     gain_grad_ref,
     shift_grad_ref,
     grad_stage,
@@ -701,12 +747,17 @@
     pieces,
     rows_stage,
     out_got,
+    in_got,
+    back_got,
     send_g,
     recv_g,
+    send_c,
+    recv_c,
+    send_r,
+    recv_r,
     own_sem,
     ring_sem,
     piece_sem,
-    half_sem,
     send_h,
     recv_h,
     send_2,
@@ -724,6 +775,35 @@
     me, share = meet(n, shares)
     core = lax.rem(me, 2)
     sibling = me + 1 - 2 * core
+    early = branch_sent_ref.shape[1]
+
+    def cot_push(step, shift, back=False):
+        peer = lax.rem(me + shift, n)
+        origin = lax.rem(me + n - shift, n) if back else me
+        span = pl.ds(step * LINES, LINES)
+        return push(
+            back_ref.at[peer, :, span],
+            back_got.at[origin, :, span],
+            send_c.at[step, shift],
+            recv_c.at[step, shift],
+            chan=peer,
+        )
+
+    def branch_push(shift, back=False):
+        peer = lax.rem(me + shift, n)
+        return push(
+            branch_stage.at[peer, pl.ds(0, early)],
+            branch_sent_ref.at[lax.rem(me + n - shift, n) if back else me],
+            send_r.at[shift],
+            recv_r.at[shift],
+            chan=peer,
+        )
+
+    for step in range(1, steps):
+        for shift in range(1, n):
+            cot_push(step, shift).start()
+    own_c = pltpu.make_async_copy(back_ref.at[me], back_got.at[me], own_sem.at[2])
+    own_c.start()
     gain_grad_ref[...] = jnp.zeros_like(gain_grad_ref)
     shift_grad_ref[...] = jnp.zeros_like(shift_grad_ref)
     hidden_sum[...] = jnp.zeros_like(hidden_sum)
@@ -738,6 +818,13 @@
 
     @pl.loop(0, steps)
     def _(step):
+        pl.when(step == 1)(own_c.wait)
+
+        @pl.when(step > 0)
+        def _():
+            for shift in range(1, n):
+                cot_push(step, shift, True).wait_recv()
+
         for line in range(LINES):
             row = step * LINES + line
             lanes = pl.ds(line * side, side)
@@ -753,9 +840,18 @@
             normed_keep[step, :, lanes] = (scaled * gain_ref[...] + shift_ref[...]).astype(jnp.bfloat16)
             scaled_keep[:, lanes] = scaled
             inverse_keep[:, lanes] = inverse
-            cots_keep[step, :, lanes] = jnp.concatenate(
-                [back_ref[owner, group, row] for owner, group in order], axis=0
-            )
+
+            @pl.when(step == 0)
+            def _():
+                cots_keep[step, :, lanes] = jnp.concatenate(
+                    [first_ref[owner, group, line] for owner, group in order], axis=0
+                )
+
+            @pl.when(step > 0)
+            def _():
+                cots_keep[step, :, lanes] = jnp.concatenate(
+                    [back_got[owner, group, row] for owner, group in order], axis=0
+                )
 
         @pl.loop(0, parts)
         def _(part):
@@ -814,95 +910,109 @@
             send_part(grad_stage, grad_ref, me, lax.rem(me + shift, n), step, send_g, recv_g, shift).start()
 
     own_g = pltpu.make_async_copy(grad_stage.at[me], grad_ref.at[me], own_sem.at[0])
-    own_r = pltpu.make_async_copy(branch_stage, branch_ref, own_sem.at[1])
+    own_r = pltpu.make_async_copy(branch_stage.at[:, pl.ds(early, steps - early)], branch_ref, own_sem.at[1])
+    own_s = pltpu.make_async_copy(branch_stage.at[me, pl.ds(0, early)], branch_sent_ref.at[me], own_sem.at[3])
+    for shift in range(1, n):
+        branch_push(shift).start()
     own_g.start()
     own_r.start()
+    own_s.start()
     turns = steps * parts
     for turn in range(turns - ring, turns):
         for copy in keeps(turn):
             copy.wait()
 
-    half = parts // 2
+    block_rows = hidden // 2 // shares
     kinds = (
-        (active_ref, cots_keep, None, out_got, channels),
-        (before_grad_ref, normed_keep, in_own_ref, in_got_ref, channels + side),
-    )
-
-    def place(job):
-        at = lax.rem((1 - core) * half + job, parts)
-        return pl.ds(pl.multiple_of(at * STEP_HIDDEN, STEP_HIDDEN), STEP_HIDDEN)
+        (active_ref, cots_keep, out_got, out_take_ref),
+        (before_grad_ref, normed_keep, in_got, in_half_ref),
+    )
+
+    def block_span(job, base=0):
+        at = lax.rem(share + 1 + lax.rem(job, shares), shares)
+        return pl.ds(pl.multiple_of(base + at * block_rows, block_rows), block_rows)
+
+    def whole_span(job):
+        owner = 1 - core if job < shares else core
+        return block_span(job, owner * (hidden // 2))
 
     def fetch(kind, job, slot):
-        return pltpu.make_async_copy(kinds[kind][0].at[:, place(job)], pieces.at[slot], piece_sem.at[slot])
+        return pltpu.make_async_copy(
+            kinds[kind][0].at[:, whole_span(job)], pieces.at[slot], piece_sem.at[slot]
+        )
 
     def give(kind, job):
-        _, _, _, got, wide = kinds[kind]
+        got = kinds[kind][2]
         return push(
-            rows_stage.at[job, :, pl.ds(0, wide)],
-            got.at[pl.ds(job * STEP_HIDDEN, STEP_HIDDEN)],
+            rows_stage.at[job, :, pl.ds(0, got.shape[1])],
+            got.at[block_span(job)],
             send_h.at[kind, job],
             recv_h.at[kind, job],
             chan=sibling,
         )
 
-    def keep(job):
-        return pltpu.make_async_copy(
-            rows_stage.at[job],
-            in_own_ref.at[pl.ds((job - half) * STEP_HIDDEN, STEP_HIDDEN)],
-            half_sem.at[job],
-        )
-
-    block_rows = hidden // 2 // shares
-
-    def second(turn):
-        peer = lax.rem(share + turn, shares)
-        span = pl.ds(pl.multiple_of(peer * block_rows, block_rows), block_rows)
-        if turn == 0:
-            return pltpu.make_async_copy(out_got.at[span], out_take_ref.at[0], send_2.at[0])
-        return push(out_got.at[span], out_take_ref.at[turn], send_2.at[turn], recv_2.at[turn], dp=peer)
-
-    jobs = [(kind, job) for kind in range(2) for job in range(parts)]
+    def second(kind, job):
+        _, _, got, take = kinds[kind]
+        turn = job + 1 - shares
+        if kind == 1:
+            at = lax.rem(share + turn, shares)
+            return pltpu.make_async_copy(got.at[block_span(job)], take.at[at], send_2.at[1, turn - 1])
+        if turn == shares:
+            return pltpu.make_async_copy(got.at[block_span(job)], take.at[0], send_2.at[0, 0])
+        return push(
+            got.at[block_span(job)],
+            take.at[turn],
+            send_2.at[kind, turn],
+            recv_2.at[kind, turn],
+            dp=lax.rem(share + turn, shares),
+        )
+
+    jobs = [(kind, job) for kind in range(2) for job in range(2 * shares)]
     fetch(0, 0, 0).start()
     for at, (kind, job) in enumerate(jobs):
         slot = at % 2
         if at + 1 < len(jobs):
             fetch(*jobs[at + 1], (at + 1) % 2).start()
-        if at == parts:
-            for done in range(half):
-                give(0, done).wait()
-                span = pl.ds(done * STEP_HIDDEN, STEP_HIDDEN)
-                mine = rows_stage[half + done, :, :channels].astype(jnp.float32)
-                out_got[span, :] = (mine + out_got[span, :].astype(jnp.float32)).astype(jnp.bfloat16)
-            for turn in range(shares):
-                second(turn).start()
         fetch(kind, job, slot).wait()
-        right = kinds[kind][1]
-        total = dot_nt(pieces[slot, 0], right[0])
-        for step in range(1, steps):
-            total = total + dot_nt(pieces[slot, step], right[step])
-        rows_stage[job, :, :channels] = total.astype(jnp.bfloat16)
-        if kind == 1:
-            rows_stage[job, :, channels:] = hidden_sum[place(job), :].astype(jnp.bfloat16)
-        if job < half:
+        right, got = kinds[kind][1:3]
+        total = dot_nt(
+            jnp.concatenate([pieces[slot, step] for step in range(steps)], axis=1),
+            jnp.concatenate([right[step] for step in range(steps)], axis=1),
+        )
+        if job < shares:
+            rows_stage[job, :, :channels] = total.astype(jnp.bfloat16)
+            if kind == 1:
+                rows_stage[job, :, channels:] = hidden_sum[whole_span(job), :].astype(jnp.bfloat16)
             give(kind, job).start()
-        elif kind == 1:
-            keep(job).start()
-    for job in range(parts):
-        (give(1, job) if job < half else keep(job)).wait()
-    for turn in range(shares):
-        second(turn).wait()
+        else:
+            give(kind, job - shares).wait()
+            span = block_span(job)
+            got[span, :channels] = (total + got[span, :channels].astype(jnp.float32)).astype(jnp.bfloat16)
+            if kind == 1:
+                got[span, channels:] = (
+                    hidden_sum[whole_span(job), :] + got[span, channels:].astype(jnp.float32)
+                ).astype(jnp.bfloat16)
+            second(kind, job).start()
+    for kind in range(2):
+        for job in range(shares, 2 * shares):
+            second(kind, job).wait()
     own_g.wait()
     own_r.wait()
+    own_s.wait()
     wait_parts(grad_stage, grad_ref, me, n, send_g, recv_g)
-
-
-def mlp(n, shares, mixed, back, in_full, out_full, gain, shift):
+    for shift in range(1, n):
+        branch_push(shift, True).wait_recv()
+        branch_push(shift).wait_send()
+        for step in range(1, steps):
+            cot_push(step, shift).wait_send()
+
+
+def mlp(n, shares, mixed, first, back, in_full, out_full, gain, shift):
     _, groups, block, group, side = mixed.shape
     hidden, channels = out_full.shape
     local = channels // n
     steps = block // LINES
     width = LINES * side
-    parts = hidden // STEP_HIDDEN
     shape = (n, steps, LINES, local, side)
     ring = 4
     low = functools.partial(jax.ShapeDtypeStruct, dtype=jnp.bfloat16)
@@ -912,16 +1022,16 @@
         functools.partial(mlp_kernel, n, shares),
         out_shape=(
             low(shape),
-            low(shape),
+            low((n, steps // 4, *shape[2:])),
+            low((n, steps - steps // 4, *shape[2:])),
             low((steps, hidden, width)),
             low((steps, hidden, width)),
             low((shares, hidden // 2 // shares, channels)),
-            low((hidden // 2, channels + side)),
-            low((hidden // 2, channels + side)),
+            low((shares, hidden // 2 // shares, channels + side)),
             jax.ShapeDtypeStruct((channels, side), jnp.float32),
             jax.ShapeDtypeStruct((channels, side), jnp.float32),
         ),
-        in_specs=[vmem] * 6,
+        in_specs=[vmem] * 6 + [hbm],
         out_specs=(hbm,) * 7 + (vmem, vmem),
         scratch_shapes=[
             pltpu.VMEM(shape, jnp.bfloat16),
@@ -935,28 +1045,33 @@
             pltpu.VMEM((channels, width), jnp.float32),
             pltpu.VMEM((channels, width), jnp.float32),
             pltpu.VMEM((hidden, side), jnp.float32),
-            pltpu.VMEM((2, steps, STEP_HIDDEN, width), jnp.bfloat16),
-            pltpu.VMEM((parts, STEP_HIDDEN, channels + side), jnp.bfloat16),
+            pltpu.VMEM((2, steps, hidden // 2 // shares, width), jnp.bfloat16),
+            pltpu.VMEM((shares, hidden // 2 // shares, channels + side), jnp.bfloat16),
             pltpu.VMEM((hidden // 2, channels), jnp.bfloat16),
+            pltpu.VMEM((hidden // 2, channels + side), jnp.bfloat16),
+            pltpu.VMEM(back.shape, jnp.bfloat16),
             pltpu.SemaphoreType.DMA((n,)),
             pltpu.SemaphoreType.DMA((n,)),
-            pltpu.SemaphoreType.DMA((2,)),
+            pltpu.SemaphoreType.DMA((steps, n)),
+            pltpu.SemaphoreType.DMA((steps, n)),
+            pltpu.SemaphoreType.DMA((n,)),
+            pltpu.SemaphoreType.DMA((n,)),
+            pltpu.SemaphoreType.DMA((4,)),
             pltpu.SemaphoreType.DMA((2, ring)),
             pltpu.SemaphoreType.DMA((2,)),
-            pltpu.SemaphoreType.DMA((parts,)),
-            pltpu.SemaphoreType.DMA((2, parts)),
-            pltpu.SemaphoreType.DMA((2, parts)),
-            pltpu.SemaphoreType.DMA((shares,)),
-            pltpu.SemaphoreType.DMA((shares,)),
+            pltpu.SemaphoreType.DMA((2, shares)),
+            pltpu.SemaphoreType.DMA((2, shares)),
+            pltpu.SemaphoreType.DMA((2, shares)),
+            pltpu.SemaphoreType.DMA((2, shares)),
         ],
         compiler_params=pltpu.CompilerParams(
             collective_id=1, has_side_effects=True, vmem_limit_bytes=63 * mebi
         ),
         name="mlp",
-    )(mixed, back, in_full, out_full, gain, shift)
-
-
-def sum_rounds(n, shares, me, share, part, final, stage3, take3, keep3, send3, recv3, send4, recv4, own_sem):
+    )(mixed, first, in_full, out_full, gain, shift, back)
+
+
+def sum_rounds(n, shares, me, share, part, final, stage3, take3, keep3, keep4, send3, recv3, send4, recv4, own_sem):
     near, far = n // 2, me // 2
     core = lax.rem(me, 2)
 
@@ -967,10 +1082,10 @@
     def fourth(turn, back=False):
         holder = lax.rem(share + shares - turn, shares) if back else share
         peer = lax.rem(share + turn, shares)
-        return push(keep3, final.at[holder], send4.at[turn], recv4.at[turn], dp=peer)
+        return push(keep4, final.at[holder], send4.at[turn], recv4.at[turn], dp=peer)
 
     def mine():
-        return pltpu.make_async_copy(keep3, final.at[share], own_sem.at[0])
+        return pltpu.make_async_copy(keep4, final.at[share], own_sem.at[0])
 
     def start_third():
         for at in range(near):
@@ -990,7 +1105,7 @@
         total = keep3[...]
         for turn in range(1, near):
             total = total + take3[turn].astype(jnp.float32)
-        keep3[...] = total
+        keep4[...] = total.astype(jnp.bfloat16)
         mine().start()
         for turn in range(1, shares):
             fourth(turn).start()
@@ -1011,6 +1126,7 @@
     image_ref,
     cot_ref,
     grad_ref,
+    branch_sent_ref,
     branch_ref,
     rows_back_ref,
     rows_ref,
@@ -1022,11 +1138,11 @@
     gain_sums_ref,
     shift_sums_ref,
     out_take_ref,
-    in_own_ref,
-    in_got_ref,
+    in_half_ref,
     output_ref,
     input_grad_ref,
     small_ref,
+    late_ref,
     norm_ref,
     out_final_ref,
     in_final_ref,
@@ -1038,18 +1154,21 @@
     scale_sums,
     small_own,
     small_got,
+    late_own,
+    late_got,
     norm_own,
     norm_near,
     norm_mid,
     norm_far,
-    stage2,
-    take2,
+    in_take,
     out_stage3,
     out_take3,
     out_keep3,
+    out_keep4,
     in_stage3,
     in_take3,
     in_keep3,
+    in_keep4,
     send_sem,
     recv_sem,
     own_sem,
@@ -1057,6 +1176,8 @@
     recv_2,
     send_s,
     recv_s,
+    send_l,
+    recv_l,
     send_n,
     recv_n,
     send_f,
@@ -1064,33 +1185,41 @@
     *round_sems,
 ):
     count, side, _ = image_ref.shape
-    steps, lines = branch_ref.shape[1], branch_ref.shape[2]
+    late, lines = branch_ref.shape[1], branch_ref.shape[2]
+    early = branch_sent_ref.shape[1]
     near = n // 2
     rows = in_keep3.shape[0]
-    block = near * rows
     me, share = meet(n, shares)
 
-    def out_part(at):
-        span = slice(at * rows, (at + 1) * rows)
-        return sum(out_take_ref[turn, span].astype(jnp.float32) for turn in range(shares))
-
-    def in_part(at):
-        base = pl.ds(pl.multiple_of(share * block + at * rows, rows), rows)
-        total = in_own_ref[base, :].astype(jnp.float32) + in_got_ref[base, :].astype(jnp.float32)
-        for turn in range(1, shares):
-            total = total + take2[turn, at * rows : (at + 1) * rows].astype(jnp.float32)
-        return total
+    def summed(take):
+        return lambda at: sum(take[turn, at * rows : (at + 1) * rows].astype(jnp.float32) for turn in range(shares))
 
     out_third, out_fourth, out_finish = sum_rounds(
-        n, shares, me, share, out_part, out_final_ref, out_stage3, out_take3, out_keep3, *round_sems[:5]
+        n, shares, me, share, summed(out_take_ref), out_final_ref, out_stage3, out_take3, out_keep3, out_keep4, *round_sems[:5]
     )
     in_third, in_fourth, in_finish = sum_rounds(
-        n, shares, me, share, in_part, in_final_ref, in_stage3, in_take3, in_keep3, *round_sems[5:]
+        n, shares, me, share, summed(in_take), in_final_ref, in_stage3, in_take3, in_keep3, in_keep4, *round_sems[5:]
     )
 
     def in_second(turn):
         peer = lax.rem(share + turn, shares)
-        return push(stage2.at[peer], take2.at[turn], send_2.at[turn], recv_2.at[turn], dp=peer)
+        if turn == 0:
+            return pltpu.make_async_copy(in_half_ref.at[peer], in_take.at[0], send_2.at[0])
+        return push(in_half_ref.at[peer], in_take.at[turn], send_2.at[turn], recv_2.at[turn], dp=peer)
+
+    def branch_push(step, shift, back=False):
+        peer = lax.rem(me + shift, n)
+        return push(
+            branch_ref.at[peer, step],
+            branch_got.at[lax.rem(me + n - shift, n) if back else me, step],
+            send_sem.at[step, shift],
+            recv_sem.at[step, shift],
+            chan=peer,
+        )
+
+    def start_branch(step):
+        for shift in range(1, n):
+            branch_push(step, shift).start()
 
     def norm_first(turn):
         peer = lax.rem(share + turn, shares)
@@ -1103,6 +1232,10 @@
     def small_push(turn):
         peer = lax.rem(share + turn, shares)
         return push(small_own, small_got.at[turn], send_s.at[turn], recv_s.at[turn], dp=peer)
+
+    def late_push(turn):
+        peer = lax.rem(share + turn, shares)
+        return push(late_own, late_got.at[turn], send_l.at[turn], recv_l.at[turn], dp=peer)
 
     def norm_pass():
         total = norm_own[...]
@@ -1114,27 +1247,20 @@
             norm_second(turn).start()
 
     def in_pass():
-        for turn in range(1, shares):
+        for turn in range(shares):
             in_second(turn).wait()
         in_third()
-
-    out_third()
-    for at in range(shares):
-        span = slice(at * block, (at + 1) * block)
-        stage2[at] = (in_own_ref[span].astype(jnp.float32) + in_got_ref[span].astype(jnp.float32)).astype(
-            jnp.bfloat16
-        )
-    for turn in range(1, shares):
-        in_second(turn).start()
+        for step in range(1, late):
+            start_branch(step)
+
     top = lax.broadcasted_iota(jnp.int32, norm_own.shape, 0) == 0
     norm_own[...] = jnp.where(top, lane_sums(gain_sums_ref[...]), lane_sums(shift_sums_ref[...]))
     for turn in range(1, shares):
         norm_first(turn).start()
-    for shift in range(1, n):
-        peer = lax.rem(me + shift, n)
-        push(
-            branch_ref.at[peer], branch_got.at[me], send_sem.at[shift], recv_sem.at[shift], chan=peer
-        ).start()
+    for turn in range(shares):
+        in_second(turn).start()
+    out_third()
+    start_branch(0)
     own = pltpu.make_async_copy(branch_ref.at[me], branch_got.at[me], own_sem.at[0])
     own.start()
     row_at = lax.broadcasted_iota(jnp.int32, (side, side), 0)
@@ -1149,11 +1275,7 @@
         span = pl.ds(pl.multiple_of(row * count, count), count)
         wide[span, :] = grad_ref[row].astype(jnp.float32)
 
-    @pl.loop(0, count)
-    def _(chan):
-        pl.when(chan == count // 3)(out_fourth)
-        pl.when(chan == count // 3)(norm_pass)
-        pl.when(chan == count * 3 // 4)(in_pass)
+    def one_channel(chan):
         one = pl.ds(chan, 1)
         grad = wide[pl.ds(chan, side, stride=count), :]
         image = image_ref[chan].astype(jnp.float32)
@@ -1189,48 +1311,56 @@
             jnp.concatenate([turned_high, turned_low], axis=1),
             jnp.concatenate([grad_high, grad_high], axis=0),
         ) + dot_nn(turned_high, grad_rest)
-        masked_grad = masked_grad + skip_ref[one, :] * grad
+        masked_grad = masked_grad + skip_ref[chan] * grad
         input_grad_ref[chan] = jnp.where(inside, grad_out + masked_grad, 0.0)
         rows_sums[one, :] = lag_sums(rows_grad, side, row_at + col_at >= side - 1)
         cols_sums[one, :] = lag_sums(cols_grad, side, row_at + col_at <= side - 1)
 
+    @pl.loop(0, count // ABREAST)
+    def _(few):
+        pl.when(few == count // ABREAST // 2)(in_pass)
+        pl.when(few == count // ABREAST * 5 // 8)(out_fourth)
+        pl.when(few == count // ABREAST * 5 // 8)(norm_pass)
+        for at in range(ABREAST):
+            one_channel(few * ABREAST + at)
+
     small_own[:, :side] = rows_sums[...]
     small_own[:, side : 2 * side] = cols_sums[...]
-    in_fourth()
-    own.wait()
-    for shift in range(1, n):
-        peer = lax.rem(me + shift, n)
-        pltpu.make_async_remote_copy(
-            src_ref=branch_ref.at[peer],
-            dst_ref=branch_got.at[lax.rem(me + n - shift, n)],
-            send_sem=send_sem.at[shift],
-            recv_sem=recv_sem.at[shift],
-            device_id={"chan": peer},
-            device_id_type=MESH,
-        ).wait()
-
-    @pl.loop(0, n * steps)
-    def _(step):
-        for line in range(lines):
-            span = pl.ds(pl.multiple_of((step * lines + line) * count, count), count)
-            wide[span, :] = branch_got[step // steps, lax.rem(step, steps), line].astype(jnp.float32)
-
-    @pl.loop(0, count)
-    def _(chan):
-        one = pl.ds(chan, 1)
-        shifted = wide[pl.ds(chan, side, stride=count), :] + bias_ref[one, :]
-        image = image_ref[chan].astype(jnp.float32)
-        grad_out = jnp.where(inside, cot_ref[chan].astype(jnp.float32), 0.0)
-        output_ref[chan] = jnp.where(inside, image + scale_ref[one, :] * shifted, 0.0).astype(jnp.bfloat16)
-        scale_sums[one, :] = jnp.sum(grad_out * shifted, axis=0, keepdims=True)
-
     lane = lax.broadcasted_iota(jnp.int32, (count, side), 1)
     last = jnp.zeros((count, side), jnp.float32)
-    for at, sums in enumerate((skip_sums, bias_sums_ref, scale_sums)):
+    for at, sums in enumerate((skip_sums, bias_sums_ref)):
         last = jnp.where(lane == at, jnp.sum(sums[...], axis=1, keepdims=True), last)
     small_own[:, 2 * side :] = last
     for turn in range(1, shares):
         small_push(turn).start()
+    in_fourth()
+    own.wait()
+    for step in range(late):
+        for shift in range(1, n):
+            branch_push(step, shift, True).wait_recv()
+            branch_push(step, shift).wait_send()
+
+    @pl.loop(0, n)
+    def _(owner):
+        for step in range(early + late):
+            part = branch_sent_ref.at[owner, step] if step < early else branch_got.at[owner, step - early]
+            for line in range(lines):
+                row = (owner * (early + late) + step) * lines + line
+                wide[pl.ds(pl.multiple_of(row * count, count), count), :] = part[line].astype(jnp.float32)
+
+    @pl.loop(0, count)
+    def _(chan):
+        one = pl.ds(chan, 1)
+        shifted = wide[pl.ds(chan, side, stride=count), :] + bias_ref[chan]
+        image = image_ref[chan].astype(jnp.float32)
+        grad_out = jnp.where(inside, cot_ref[chan].astype(jnp.float32), 0.0)
+        output_ref[chan] = jnp.where(inside, image + scale_ref[chan] * shifted, 0.0).astype(jnp.bfloat16)
+        scale_sums[one, :] = jnp.sum(grad_out * shifted, axis=0, keepdims=True)
+
+    late_own[...] = jnp.zeros_like(late_own)
+    late_own[:, :count] = lane_sums(scale_sums[...])
+    for turn in range(1, shares):
+        late_push(turn).start()
     total = norm_mid[...]
     for turn in range(1, n):
         norm_second(turn).wait()
@@ -1243,15 +1373,19 @@
         small_push(turn).wait()
         total = total + small_got[turn]
     small_ref[...] = total
-
-
-def mixer_back(n, shares, sizes, images, cotangent, grad, branch, lines, norms, sums):
+    total = late_own[...]
+    for turn in range(1, shares):
+        late_push(turn).wait()
+        total = total + late_got[turn]
+    late_ref[...] = total
+
+
+def mixer_back(n, shares, sizes, images, cotangent, grad, branch_sent, branch, lines, vectors, norms, sums):
     count, side, _ = images.shape
     near = n // 2
-    out_take, in_own, _ = sums
-    block, channels = out_take.shape[1:]
+    block, channels = sums[0].shape[1:]
     rows = block // near
-    wide = in_own.shape[1]
+    wide = sums[1].shape[2]
     line = pltpu.VMEM((count, side), jnp.float32)
     norm = pltpu.VMEM((8, channels), jnp.float32)
     vmem = pl.BlockSpec(memory_space=pltpu.VMEM)
@@ -1263,15 +1397,19 @@
             jax.ShapeDtypeStruct(images.shape, jnp.bfloat16),
             full(images.shape),
             full((count, 3 * side)),
+            full((8, side)),
             full((8, channels)),
-            full((shares, rows, channels)),
-            full((shares, rows, wide)),
+            jax.ShapeDtypeStruct((shares, rows, channels), jnp.bfloat16),
+            jax.ShapeDtypeStruct((shares, rows, wide), jnp.bfloat16),
         ),
         in_specs=[pl.BlockSpec(memory_space=pltpu.SMEM)]
-        + [vmem] * 3
+        + [vmem] * 4
         + [hbm]
-        + [vmem] * (len(lines) + len(norms) + len(sums)),
-        out_specs=(vmem,) * 4 + (hbm,) * 2,
+        + [vmem] * len(lines)
+        + [pl.BlockSpec(memory_space=pltpu.SMEM)] * len(vectors)
+        + [vmem] * (len(norms) + 1)
+        + [hbm],
+        out_specs=(vmem,) * 5 + (hbm,) * 2,
         scratch_shapes=[
             pltpu.VMEM((count * side, side), jnp.float32),
             pltpu.VMEM(branch.shape, jnp.bfloat16),
@@ -1281,12 +1419,13 @@
             line,
             pltpu.VMEM((count, 3 * side), jnp.float32),
             pltpu.VMEM((shares, count, 3 * side), jnp.float32),
+            pltpu.VMEM((8, side), jnp.float32),
+            pltpu.VMEM((shares, 8, side), jnp.float32),
             norm,
             pltpu.VMEM((shares, 8, channels), jnp.float32),
             norm,
             pltpu.VMEM((n, 8, channels), jnp.float32),
-            pltpu.VMEM((shares, block, wide), jnp.bfloat16),
-            pltpu.VMEM((shares, block, wide), jnp.bfloat16),
+            pltpu.VMEM(sums[1].shape, jnp.bfloat16),
         ]
         + [
             kind
@@ -1295,26 +1434,26 @@
                 pltpu.VMEM((near, rows, columns), jnp.bfloat16),
                 pltpu.VMEM((near, rows, columns), jnp.bfloat16),
                 pltpu.VMEM((rows, columns), jnp.float32),
+                pltpu.VMEM((rows, columns), jnp.bfloat16),
             )
         ]
         + [
-            pltpu.SemaphoreType.DMA((size,))
-            for size in (n, n, 1, shares, shares, shares, shares, shares, shares, n, n)
+            pltpu.SemaphoreType.DMA(size if isinstance(size, tuple) else (size,))
+            for size in ((branch.shape[1], n), (branch.shape[1], n), 1, *(shares,) * 8, n, n)
             + (near, near, shares, shares, 1) * 2
         ],
         compiler_params=pltpu.CompilerParams(
             collective_id=2, has_side_effects=True, vmem_limit_bytes=62 * mebi
         ),
         name="mixer_back",
-    )(sizes, images, cotangent, grad, branch, *lines, *norms, *sums)
+    )(sizes, images, cotangent, grad, branch_sent, branch, *lines, *vectors, *norms, *sums)
 
 
 def taps_kernel(small_ref, *refs):
-    params, (*grads, rest_ref), wide = refs[:8], refs[8:17], refs[17]
+    params, (*grads, rest_ref), wide, turned = refs[:8], refs[8:17], refs[17], refs[18]
     count = small_ref.shape[0]
     side = wide.shape[0]
     wide[...] = jnp.zeros_like(wide)
-    turned = refs[18]
 
     def turn(at):
         wide[:count, :] = small_ref[:, at * side : (at + 1) * side]
@@ -1391,42 +1530,41 @@
             cols_imag,
         )
     )
-    skip_wide = jnp.broadcast_to(skip_gain[:, None], (count, side))
-    scale_wide = jnp.broadcast_to(layer_scale[:, None], (count, side))
-    bias_wide = jnp.broadcast_to(bias_out[:, None], (count, side))
-
     shares = lax.axis_size("dp")
     hidden = weight_out.shape[0]
     spread = jnp.broadcast_to(bias_in[:, None], (hidden, side))
     in_part = jnp.concatenate([weight_in.T, spread], axis=1).reshape(shares, -1, channels + side)
     out_part = weight_out.reshape(shares, -1, channels)
-    mixed, back, in_whole, out_whole, bias_out_sums, rows_back, rows, cols_back, _ = mixer_forward(
-        n, shares, sizes, image, cot, params, skip_wide, scale_wide, in_part, out_part
-    )
-    grad, branch, _, _, *sums, gain_sums, shift_sums = mlp(
+    mixed, first, back, in_whole, out_whole, bias_out_sums, rows_back, rows, cols_back, _ = mixer_forward(
+        n, shares, sizes, image, cot, skip_gain, layer_scale, params, in_part, out_part
+    )
+    grad, branch_sent, branch, _, _, *sums, gain_sums, shift_sums = mlp(
         n,
         shares,
         mixed,
+        first,
         back,
         in_whole.reshape(-1, channels + side),
         out_whole.reshape(-1, channels),
         jnp.broadcast_to(norm_gain[:, None], (channels, side)),
         jnp.broadcast_to(norm_bias[:, None], (channels, side)),
     )
-    output, input_grad, small, norms, out_final, in_final = mixer_back(
+    output, input_grad, small, late, norms, out_final, in_final = mixer_back(
         n,
         shares,
         sizes,
         image,
         cot,
         grad.reshape(side, count, side),
+        branch_sent,
         branch,
-        (rows_back, rows, cols_back, skip_wide, scale_wide, bias_wide),
+        (rows_back, rows, cols_back),
+        (skip_gain, layer_scale, bias_out),
         (bias_out_sums, gain_sums, shift_sums),
         sums,
     )
     *params_grad, rest = taps_back(small, params, side)
-    in_final = in_final.reshape(hidden, channels + side)
+    in_final = in_final.reshape(hidden, channels + side).astype(jnp.float32)
     return (
         output[None],
         input_grad[None],
@@ -1436,9 +1574,9 @@
         norms[1],
         in_final[:, :channels].T,
         jnp.sum(in_final[:, channels:], axis=1),
-        out_final.reshape(hidden, channels),
+        out_final.reshape(hidden, channels).astype(jnp.float32),
         rest[1],
-        rest[2],
+        late[0, :count],
     )
 
 
@@ -1449,10 +1587,11 @@
         and side == 128
         and count <= side
         and count % GROUP == 0
-        and side % (n * LINES) == 0
+        and side % (4 * n * LINES) == 0
         and n % 2 == 0
         and (rest[15].shape[0] * n) % (2 * STEP_HIDDEN) == 0
         and rest[15].shape[0] % (16 * lax.axis_size("dp")) == 0
+        and lax.axis_size("dp") > 1
     )
     return pixel_body(n, images, *rest) if fits else plain_body(images, *rest)
 

time: 490 us -> 421 us (0.86)
  Pallas kernels: 448 us -> 380 us
    pallas_call x1, Pallas kernels: 169 us -> 120 us  [mixer_forward(): pl.pallas_call(functools.partial(mixer_kernel, n, shares), out_shape=(jax...]
    pallas_call x1, Pallas kernels: 138 us -> 110 us  [mixer_back(): pl.pallas_call(functools.partial(back_kernel, n, shares), out_shape=(jax....]
    pallas_call x1, Pallas kernels: 137 us -> 146 us  [mlp(): pl.pallas_call(functools.partial(mlp_kernel, n, shares), out_shape=(low(s...]
    unnamed x58 -> x49, local copies, waits for them, and re-layouts: 24.9 us -> 20.6 us
where the time goes in v4:
time: 421 us; the launch traced here: 420 us
  Pallas kernels  380 us (90%)
  local copies, waits for them, and re-layouts  31.2 us (7%)
  other arithmetic  6.05 us (1%)
    pallas_call x1, Pallas kernels, mlp(): pl.pallas_call(functools.partial(mlp_kernel, n, shares), out_shape=(low(s...  146 us
    pallas_call x1, Pallas kernels, mixer_forward(): pl.pallas_call(functools.partial(mixer_kernel, n, shares), out_shape=(jax...  120 us
    pallas_call x1, Pallas kernels, mixer_back(): pl.pallas_call(functools.partial(back_kernel, n, shares), out_shape=(jax....  110 us
    unnamed x49, local copies, waits for them, and re-layouts  20.6 us

profile of v4, /device:TPU:9, one launch (start us, length us, event | category | flops | bytes accessed | tf_op | source)
XLA Modules:
  0.0 420.1 jit_solution(16790451536075863396)
XLA Ops:
  0.7 0.0 copy-start
  0.7 0.0 copy-start.22
  0.7 0.0 copy-start.21
  0.7 0.0 copy-start.15
  0.7 0.0 copy-start.14
  0.7 0.0 copy-start.13
  0.7 0.0 copy-start.12
  0.7 0.0 copy-start.11
  0.8 0.0 copy-start.10
  0.8 0.0 copy-start.9
  0.8 0.0 copy-start.8
  0.8 1.3 dynamic_slice.6
  4.0 0.0 copy-done
  4.0 0.2 dynamic-slice_reduce_fusion.sizes_ref
  4.2 0.0 copy-start.20
  4.2 0.0 copy-start.2
  4.2 0.8 broadcast_in_dim.10
  5.1 1.7 broadcast_in_dim.11.gain_ref
  6.8 1.6 broadcast_in_dim.12.shift_ref
  8.4 2.0 pad_maximum_fusion
  10.4 2.2 copy.38
  12.6 0.0 copy-done.22
  12.6 0.0 copy-done.21
  12.6 0.0 copy-done.15
  12.6 0.0 copy-done.14
  12.6 0.0 copy-done.13
  12.6 0.0 copy-done.12
  12.6 0.0 copy-done.11
  12.7 0.0 copy-done.10
  12.7 0.0 copy-done.9
  12.7 0.0 copy-done.8
  12.7 0.0 copy-done.2
  12.7 0.0 copy-start.5
  12.7 1.1 copy-done.5
  13.8 0.0 copy-start.7
  13.8 1.1 copy-done.7
  14.9 120.0 %mixer_forward.1 = (bf16[8,6,16,16,128]{4,3,2,1,0:T(8,128)(2,1)S(1)}, bf16[8,6,4,16,128]{4,3,2,1,0:T(8,128)(2,1)S(1)}, bf16[8,6,16,16,128]{4,3,2,1,0:T(8,128)(2,...) custom-call(s32[2]{0:T(128)S(1)} %dynamic-slice_reduce_fusion.sizes_, ...), custom_call_target="tpu_custom_call" | custom-call | tf_op jit(solution)/shard_map/mixer_forward/pallas_call | solution.py:664
  134.8 0.0 copy-done.20
  134.8 0.0 copy-start.3
  134.8 1.7 copy-done.3
  136.5 0.0 copy-start.4
  136.5 1.7 copy-done.4
  138.2 0.9 copy-done.6
  139.0 0.0 copy-start.16
  139.0 0.6 copy-done.16
  139.7 0.0 copy-start.17
  139.7 0.6 copy-done.17
  140.3 0.0 copy-start.18
  140.3 0.6 copy-done.18
  140.9 0.0 copy-start.19
  140.9 0.6 copy-done.19
  141.5 145.8 %mlp.1 = (bf16[8,4,4,96,128]{4,3,2,1,0:T(8,128)(2,1)}, bf16[8,1,4,96,128]{4,3,2,1,0:T(8,128)(2,1)}, bf16[8,3,4,96,128]{4,3,2,1,0:T(8,128)(2,1)}, bf16[4,3072,512...) custom-call(bf16[8,6,16,16,128]{4,3,2,1,0:T(8,128)(2,1)} %copy-done., ...), custom_call_target="tpu_custom_call" | custom-call | tf_op jit(solution)/shard_map/mlp/pallas_call | solution.py:1021
  287.3 110.0 %mixer_back.1 = (bf16[96,128,128]{2,1,0:T(8,128)(2,1)}, f32[96,128,128]{2,1,0:T(8,128)}, f32[96,384]{1,0:T(8,128)}, f32[8,128]{1,0:T(8,128)}, f32[8,768]{1,0:T(8...) custom-call(s32[2]{0:T(128)} %copy-done.20, bf16[96,128,128]{2,1,0:T(8,128)(2,1)} %bitcast.40, ...), custom_call_target="tpu_custom_call" | custom-call | tf_op jit(solution)/shard_map/mixer_back/pallas_call | solution.py:1394
  397.4 1.4 slice_reduce_fusion.1
  398.8 4.2 %taps_back.1 = (f32[32,96]{1,0:T(8,128)}, f32[32,96]{1,0:T(8,128)}, f32[32,96]{1,0:T(8,128)}, f32[32,96]{1,0:T(8,128)}, f32[32,96]{1,0:T(8,128)}, /*index=5*/f32...) custom-call(f32[96,384]{1,0:T(8,128)} %get-tuple-element.68.small_ref, f32[32,96]{1,0:T(8,128)} %bitcast.44, ...), custom_call_target="tpu_custom_call" | custom-call | tf_op jit(solution)/shard_map/taps_back/pallas_call | solution.py:1481
  403.0 1.3 slice_bitcast_fusion.1
  404.3 2.2 bitcast_convert_fusion.1
  406.5 1.2 bitcast_convert_fusion
  407.7 0.7 slice_reduce_fusion
  408.4 0.1 slice.28
  408.5 1.4 copy.40
  409.9 4.0 copy.43
  413.8 6.3 %copy.44 = f32[1,96,128,128]{3,2,1,0:T(8,128)} copy(f32[1,96,128,128]{3,2,1,0:T(8,128)} %bitcast.62) | data formatting | bytes 12582912
  420.1 0.0 copy-done.1
  (2 shorter events, 0.0 us)
Async XLA Ops:
  0.7 3.4 copy-start
  0.7 11.9 %copy-start.22 = (f32[96]{0:T(128)S(1)}, f32[96]{0:T(128)}, u32[]{:S(2)}) copy-start(f32[96]{0:T(128)} %scale_ref.3) | copy-start | bytes 1156
  0.7 11.9 %copy-start.21 = (f32[96]{0:T(128)S(1)}, f32[96]{0:T(128)}, u32[]{:S(2)}) copy-start(f32[96]{0:T(128)} %skip_ref.3) | copy-start | bytes 1156
  0.7 11.9 %copy-start.15 = (f32[96,32]{0,1:T(8,128)S(1)}, f32[96,32]{0,1:T(8,128)}, u32[]{:S(2)}) copy-start(f32[96,32]{0,1:T(8,128)} %param.31) | copy-start | bytes 36868
  0.7 11.9 %copy-start.14 = (f32[96,32]{0,1:T(8,128)S(1)}, f32[96,32]{0,1:T(8,128)}, u32[]{:S(2)}) copy-start(f32[96,32]{0,1:T(8,128)} %param.30) | copy-start | bytes 36868
  0.7 11.9 %copy-start.13 = (f32[96,32]{0,1:T(8,128)S(1)}, f32[96,32]{0,1:T(8,128)}, u32[]{:S(2)}) copy-start(f32[96,32]{0,1:T(8,128)} %param.29) | copy-start | bytes 36868
  0.7 11.9 %copy-start.12 = (f32[96,32]{0,1:T(8,128)S(1)}, f32[96,32]{0,1:T(8,128)}, u32[]{:S(2)}) copy-start(f32[96,32]{0,1:T(8,128)} %param.28) | copy-start | bytes 36868
  0.7 11.9 %copy-start.11 = (f32[96,32]{0,1:T(8,128)S(1)}, f32[96,32]{0,1:T(8,128)}, u32[]{:S(2)}) copy-start(f32[96,32]{0,1:T(8,128)} %param.27) | copy-start | bytes 36868
  0.8 11.9 %copy-start.10 = (f32[96,32]{0,1:T(8,128)S(1)}, f32[96,32]{0,1:T(8,128)}, u32[]{:S(2)}) copy-start(f32[96,32]{0,1:T(8,128)} %param.26) | copy-start | bytes 36868
  0.8 11.9 %copy-start.9 = (f32[96,32]{0,1:T(8,128)S(1)}, f32[96,32]{0,1:T(8,128)}, u32[]{:S(2)}) copy-start(f32[96,32]{0,1:T(8,128)} %param.25) | copy-start | bytes 36868
  0.8 11.9 %copy-start.8 = (f32[96,32]{0,1:T(8,128)S(1)}, f32[96,32]{0,1:T(8,128)}, u32[]{:S(2)}) copy-start(f32[96,32]{0,1:T(8,128)} %param.24) | copy-start | bytes 36868
  4.2 130.6 %copy-start.20 = (s32[2]{0:T(128)}, s32[2]{0:T(128)S(1)}, u32[]{:S(2)}) copy-start(s32[2]{0:T(128)S(1)} %dynamic-slice_reduce_fusion.sizes_ref) | copy-start | bytes 28
  4.2 8.5 %copy-start.2 = (bf16[1,96,128,128]{3,2,1,0:T(8,128)(2,1)S(1)}, bf16[1,96,128,128]{3,2,1,0:T(8,128)(2,1)}, u32[]{:S(2)}) copy-start(bf16[1,96,128,128]{3,2,1,0:T(8,128)(2,1)} %param.20) | copy-start | bytes 9437188
  12.7 1.1 copy-start.5
  13.8 1.1 copy-start.7
  134.8 1.7 copy-start.3
  136.5 1.7 copy-start.4
  138.2 0.9 copy-start.6
  139.0 0.6 copy-start.16
  139.7 0.6 copy-start.17
  140.3 0.6 copy-start.18
  140.9 0.6 copy-start.19
  413.8 6.3 %copy-start.1 = (s32[4,2]{0,1:T(2,128)S(1)}, s32[4,2]{0,1:T(2,128)}, u32[]{:S(2)}) copy-start(s32[4,2]{0,1:T(2,128)} %param.22) | copy-start | bytes 100

commit v5 on v4

--- a/solution.py
+++ b/solution.py
@@ -717,10 +717,10 @@
 def mlp_kernel(
     n,
     shares,
-    mixed_ref,
-    first_ref,
-    in_ref,
-    out_ref,
+    mixed_hbm,
+    first_hbm,
+    in_hbm,
+    out_hbm,
     gain_ref,
     shift_ref,
     back_ref,
@@ -749,6 +749,11 @@
     out_got,
     in_got,
     back_got,
+    mixed_ref,
+    first_ref,
+    in_ref,
+    out_ref,
+    load_sem,
     send_g,
     recv_g,
     send_c,
@@ -763,6 +768,14 @@
     send_2,
     recv_2,
 ):
+    loads = [
+        pltpu.make_async_copy(whole, here, load_sem.at[at])
+        for at, (whole, here) in enumerate(
+            ((mixed_hbm, mixed_ref), (first_hbm, first_ref), (in_hbm, in_ref), (out_hbm, out_ref))
+        )
+    ]
+    for copy in loads:
+        copy.start()
     side = mixed_ref.shape[-1]
     groups = mixed_ref.shape[1]
     block = mixed_ref.shape[2]
@@ -804,6 +817,8 @@
             cot_push(step, shift).start()
     own_c = pltpu.make_async_copy(back_ref.at[me], back_got.at[me], own_sem.at[2])
     own_c.start()
+    for copy in loads:
+        copy.wait()
     gain_grad_ref[...] = jnp.zeros_like(gain_grad_ref)
     shift_grad_ref[...] = jnp.zeros_like(shift_grad_ref)
     hidden_sum[...] = jnp.zeros_like(hidden_sum)
@@ -1031,7 +1046,7 @@
             jax.ShapeDtypeStruct((channels, side), jnp.float32),
             jax.ShapeDtypeStruct((channels, side), jnp.float32),
         ),
-        in_specs=[vmem] * 6 + [hbm],
+        in_specs=[hbm] * 4 + [vmem] * 2 + [hbm],
         out_specs=(hbm,) * 7 + (vmem, vmem),
         scratch_shapes=[
             pltpu.VMEM(shape, jnp.bfloat16),
@@ -1050,6 +1065,8 @@
             pltpu.VMEM((hidden // 2, channels), jnp.bfloat16),
             pltpu.VMEM((hidden // 2, channels + side), jnp.bfloat16),
             pltpu.VMEM(back.shape, jnp.bfloat16),
+            *(pltpu.VMEM(whole.shape, whole.dtype) for whole in (mixed, first, in_full, out_full)),
+            pltpu.SemaphoreType.DMA((4,)),
             pltpu.SemaphoreType.DMA((n,)),
             pltpu.SemaphoreType.DMA((n,)),
             pltpu.SemaphoreType.DMA((steps, n)),
@@ -1123,10 +1140,10 @@
     n,
     shares,
     sizes_ref,
-    image_ref,
-    cot_ref,
-    grad_ref,
-    branch_sent_ref,
+    image_hbm,
+    cot_hbm,
+    grad_hbm,
+    branch_sent_hbm,
     branch_ref,
     rows_back_ref,
     rows_ref,
@@ -1137,7 +1154,7 @@
     bias_sums_ref,
     gain_sums_ref,
     shift_sums_ref,
-    out_take_ref,
+    out_take_hbm,
     in_half_ref,
     output_ref,
     input_grad_ref,
@@ -1161,6 +1178,12 @@
     norm_mid,
     norm_far,
     in_take,
+    image_ref,
+    cot_ref,
+    grad_ref,
+    branch_sent_ref,
+    out_take_ref,
+    load_sem,
     out_stage3,
     out_take3,
     out_keep3,
@@ -1184,6 +1207,20 @@
     recv_f,
     *round_sems,
 ):
+    loads = [
+        pltpu.make_async_copy(whole, here, load_sem.at[at])
+        for at, (whole, here) in enumerate(
+            (
+                (out_take_hbm, out_take_ref),
+                (grad_hbm, grad_ref),
+                (image_hbm, image_ref),
+                (cot_hbm, cot_ref),
+                (branch_sent_hbm, branch_sent_ref),
+            )
+        )
+    ]
+    for copy in loads:
+        copy.start()
     count, side, _ = image_ref.shape
     late, lines = branch_ref.shape[1], branch_ref.shape[2]
     early = branch_sent_ref.shape[1]
@@ -1250,8 +1287,7 @@
         for turn in range(shares):
             in_second(turn).wait()
         in_third()
-        for step in range(1, late):
-            start_branch(step)
+        start_branch(late - 1)
 
     top = lax.broadcasted_iota(jnp.int32, norm_own.shape, 0) == 0
     norm_own[...] = jnp.where(top, lane_sums(gain_sums_ref[...]), lane_sums(shift_sums_ref[...]))
@@ -1259,8 +1295,12 @@
         norm_first(turn).start()
     for turn in range(shares):
         in_second(turn).start()
+    loads[0].wait()
     out_third()
-    start_branch(0)
+    for step in range(late - 1):
+        start_branch(step)
+    for copy in loads[1:]:
+        copy.wait()
     own = pltpu.make_async_copy(branch_ref.at[me], branch_got.at[me], own_sem.at[0])
     own.start()
     row_at = lax.broadcasted_iota(jnp.int32, (side, side), 0)
@@ -1318,9 +1358,9 @@
 
     @pl.loop(0, count // ABREAST)
     def _(few):
-        pl.when(few == count // ABREAST // 2)(in_pass)
-        pl.when(few == count // ABREAST * 5 // 8)(out_fourth)
-        pl.when(few == count // ABREAST * 5 // 8)(norm_pass)
+        pl.when(few == count // ABREAST * 7 // 8)(in_pass)
+        pl.when(few == count // ABREAST * 7 // 8)(out_fourth)
+        pl.when(few == count // ABREAST * 7 // 8)(norm_pass)
         for at in range(ABREAST):
             one_channel(few * ABREAST + at)
 
@@ -1334,28 +1374,34 @@
     for turn in range(1, shares):
         small_push(turn).start()
     in_fourth()
+    def widen(step):
+        part = branch_sent_ref if step < early else branch_got
+        at = step if step < early else step - early
+
+        @pl.loop(0, n)
+        def _(owner):
+            for line in range(lines):
+                row = (owner * (early + late) + step) * lines + line
+                wide[pl.ds(pl.multiple_of(row * count, count), count), :] = part[owner, at, line].astype(jnp.float32)
+
     own.wait()
+    for step in range(early):
+        widen(step)
     for step in range(late):
         for shift in range(1, n):
             branch_push(step, shift, True).wait_recv()
             branch_push(step, shift).wait_send()
-
-    @pl.loop(0, n)
-    def _(owner):
-        for step in range(early + late):
-            part = branch_sent_ref.at[owner, step] if step < early else branch_got.at[owner, step - early]
-            for line in range(lines):
-                row = (owner * (early + late) + step) * lines + line
-                wide[pl.ds(pl.multiple_of(row * count, count), count), :] = part[line].astype(jnp.float32)
-
-    @pl.loop(0, count)
-    def _(chan):
-        one = pl.ds(chan, 1)
-        shifted = wide[pl.ds(chan, side, stride=count), :] + bias_ref[chan]
-        image = image_ref[chan].astype(jnp.float32)
-        grad_out = jnp.where(inside, cot_ref[chan].astype(jnp.float32), 0.0)
-        output_ref[chan] = jnp.where(inside, image + scale_ref[chan] * shifted, 0.0).astype(jnp.bfloat16)
-        scale_sums[one, :] = jnp.sum(grad_out * shifted, axis=0, keepdims=True)
+        widen(early + step)
+
+    @pl.loop(0, count // 4)
+    def _(few):
+        for at in range(4):
+            chan = few * 4 + at
+            shifted = wide[pl.ds(chan, side, stride=count), :] + bias_ref[chan]
+            image = image_ref[chan].astype(jnp.float32)
+            grad_out = jnp.where(inside, cot_ref[chan].astype(jnp.float32), 0.0)
+            output_ref[chan] = jnp.where(inside, image + scale_ref[chan] * shifted, 0.0).astype(jnp.bfloat16)
+            scale_sums[pl.ds(chan, 1), :] = jnp.sum(grad_out * shifted, axis=0, keepdims=True)
 
     late_own[...] = jnp.zeros_like(late_own)
     late_own[:, :count] = lane_sums(scale_sums[...])
@@ -1403,12 +1449,11 @@
             jax.ShapeDtypeStruct((shares, rows, wide), jnp.bfloat16),
         ),
         in_specs=[pl.BlockSpec(memory_space=pltpu.SMEM)]
-        + [vmem] * 4
-        + [hbm]
+        + [hbm] * 5
         + [vmem] * len(lines)
         + [pl.BlockSpec(memory_space=pltpu.SMEM)] * len(vectors)
-        + [vmem] * (len(norms) + 1)
-        + [hbm],
+        + [vmem] * len(norms)
+        + [hbm] * 2,
         out_specs=(vmem,) * 5 + (hbm,) * 2,
         scratch_shapes=[
             pltpu.VMEM((count * side, side), jnp.float32),
@@ -1426,6 +1471,8 @@
             norm,
             pltpu.VMEM((n, 8, channels), jnp.float32),
             pltpu.VMEM(sums[1].shape, jnp.bfloat16),
+            *(pltpu.VMEM(whole.shape, whole.dtype) for whole in (images, cotangent, grad, branch_sent, sums[0])),
+            pltpu.SemaphoreType.DMA((5,)),
         ]
         + [
             kind
@@ -1589,7 +1636,7 @@
         and count % GROUP == 0
         and side % (4 * n * LINES) == 0
         and n % 2 == 0
-        and (rest[15].shape[0] * n) % (2 * STEP_HIDDEN) == 0
+        and (rest[15].shape[0] * n) % STEP_HIDDEN == 0
         and rest[15].shape[0] % (16 * lax.axis_size("dp")) == 0
         and lax.axis_size("dp") > 1
     )

time: 421 us -> 408 us (0.969)
  Pallas kernels: 380 us -> 367 us
    pallas_call x1, Pallas kernels: 110 us -> 101 us  [mixer_back(): pl.pallas_call(functools.partial(back_kernel, n, shares), out_shape=(jax....]
where the time goes in v5:
time: 408 us; the launch traced here: 407 us
  Pallas kernels  367 us (90%)
  local copies, waits for them, and re-layouts  31.2 us (8%)
  other arithmetic  6.05 us (1%)
    pallas_call x1, Pallas kernels, mlp(): pl.pallas_call(functools.partial(mlp_kernel, n, shares), out_shape=(low(s...  142 us
    pallas_call x1, Pallas kernels, mixer_forward(): pl.pallas_call(functools.partial(mixer_kernel, n, shares), out_shape=(jax...  120 us
    pallas_call x1, Pallas kernels, mixer_back(): pl.pallas_call(functools.partial(back_kernel, n, shares), out_shape=(jax....  101 us
    unnamed x49, local copies, waits for them, and re-layouts  20.6 us

profile of v5, /device:TPU:9, one launch (start us, length us, event | category | flops | bytes accessed | tf_op | source)
XLA Modules:
  0.0 407.5 jit_solution(18151503807408296715)
XLA Ops:
  0.7 0.0 copy-start
  0.7 0.0 copy-start.22
  0.7 0.0 copy-start.21
  0.7 0.0 copy-start.15
  0.7 0.0 copy-start.14
  0.7 0.0 copy-start.13
  0.7 0.0 copy-start.12
  0.7 0.0 copy-start.11
  0.8 0.0 copy-start.10
  0.8 0.0 copy-start.9
  0.8 0.0 copy-start.8
  0.8 1.3 dynamic_slice.6
  4.0 0.0 copy-done
  4.0 0.2 dynamic-slice_reduce_fusion.sizes_ref
  4.2 0.0 copy-start.20
  4.2 0.0 copy-start.2
  4.2 0.8 broadcast_in_dim.10
  5.1 1.7 broadcast_in_dim.11.gain_ref
  6.8 1.6 broadcast_in_dim.12.shift_ref
  8.4 2.0 pad_maximum_fusion
  10.4 2.2 copy.38
  12.6 0.0 copy-done.22
  12.6 0.0 copy-done.21
  12.6 0.0 copy-done.15
  12.6 0.0 copy-done.14
  12.6 0.0 copy-done.13
  12.6 0.0 copy-done.12
  12.6 0.0 copy-done.11
  12.7 0.0 copy-done.10
  12.7 0.0 copy-done.9
  12.7 0.0 copy-done.8
  12.7 0.0 copy-done.2
  12.7 0.0 copy-start.5
  12.7 1.1 copy-done.5
  13.8 0.0 copy-start.7
  13.8 1.1 copy-done.7
  14.9 120.0 %mixer_forward.1 = (bf16[8,6,16,16,128]{4,3,2,1,0:T(8,128)(2,1)S(1)}, bf16[8,6,4,16,128]{4,3,2,1,0:T(8,128)(2,1)S(1)}, bf16[8,6,16,16,128]{4,3,2,1,0:T(8,128)(2,...) custom-call(s32[2]{0:T(128)S(1)} %dynamic-slice_reduce_fusion.sizes_, ...), custom_call_target="tpu_custom_call" | custom-call | tf_op jit(solution)/shard_map/mixer_forward/pallas_call | solution.py:664
  134.8 0.0 copy-done.20
  134.8 0.0 copy-start.3
  134.8 1.7 copy-done.3
  136.5 0.0 copy-start.4
  136.5 1.7 copy-done.4
  138.2 0.0 copy-start.6
  138.2 0.9 copy-done.6
  139.0 0.0 copy-start.16
  139.0 0.6 copy-done.16
  139.7 0.0 copy-start.17
  139.7 0.6 copy-done.17
  140.3 0.0 copy-start.18
  140.3 0.6 copy-done.18
  140.9 0.6 copy-done.19
  141.5 141.8 %mlp.1 = (bf16[8,4,4,96,128]{4,3,2,1,0:T(8,128)(2,1)}, bf16[8,1,4,96,128]{4,3,2,1,0:T(8,128)(2,1)}, bf16[8,3,4,96,128]{4,3,2,1,0:T(8,128)(2,1)}, bf16[4,3072,512...) custom-call(bf16[8,6,16,16,128]{4,3,2,1,0:T(8,128)(2,1)} %copy-done., ...), custom_call_target="tpu_custom_call" | custom-call | tf_op jit(solution)/shard_map/mlp/pallas_call | solution.py:1036
  283.3 101.4 %mixer_back.1 = (bf16[96,128,128]{2,1,0:T(8,128)(2,1)}, f32[96,128,128]{2,1,0:T(8,128)}, f32[96,384]{1,0:T(8,128)}, f32[8,128]{1,0:T(8,128)}, f32[8,768]{1,0:T(8...) custom-call(s32[2]{0:T(128)} %copy-done.20, bf16[96,128,128]{2,1,0:T(8,128)(2,1)} %bitcast.40, ...), custom_call_target="tpu_custom_call" | custom-call | tf_op jit(solution)/shard_map/mixer_back/pallas_call | solution.py:1440
  384.7 1.4 slice_reduce_fusion.1
  386.2 4.2 %taps_back.1 = (f32[32,96]{1,0:T(8,128)}, f32[32,96]{1,0:T(8,128)}, f32[32,96]{1,0:T(8,128)}, f32[32,96]{1,0:T(8,128)}, f32[32,96]{1,0:T(8,128)}, /*index=5*/f32...) custom-call(f32[96,384]{1,0:T(8,128)} %get-tuple-element.68.small_ref, f32[32,96]{1,0:T(8,128)} %bitcast.44, ...), custom_call_target="tpu_custom_call" | custom-call | tf_op jit(solution)/shard_map/taps_back/pallas_call | solution.py:1528
  390.4 1.3 slice_bitcast_fusion.1
  391.7 2.2 bitcast_convert_fusion.1
  393.8 1.2 bitcast_convert_fusion
  395.0 0.7 slice_reduce_fusion
  395.7 0.1 slice.28
  395.8 1.4 copy.40
  397.2 4.0 copy.43
  401.2 6.3 %copy.44 = f32[1,96,128,128]{3,2,1,0:T(8,128)} copy(f32[1,96,128,128]{3,2,1,0:T(8,128)} %bitcast.62) | data formatting | bytes 12582912
  407.5 0.0 copy-done.1
  (2 shorter events, 0.0 us)
Async XLA Ops:
  0.7 3.4 copy-start
  0.7 11.9 %copy-start.22 = (f32[96]{0:T(128)S(1)}, f32[96]{0:T(128)}, u32[]{:S(2)}) copy-start(f32[96]{0:T(128)} %scale_ref.3) | copy-start | bytes 1156
  0.7 11.9 %copy-start.21 = (f32[96]{0:T(128)S(1)}, f32[96]{0:T(128)}, u32[]{:S(2)}) copy-start(f32[96]{0:T(128)} %skip_ref.3) | copy-start | bytes 1156
  0.7 11.9 %copy-start.15 = (f32[96,32]{0,1:T(8,128)S(1)}, f32[96,32]{0,1:T(8,128)}, u32[]{:S(2)}) copy-start(f32[96,32]{0,1:T(8,128)} %param.31) | copy-start | bytes 36868
  0.7 11.9 %copy-start.14 = (f32[96,32]{0,1:T(8,128)S(1)}, f32[96,32]{0,1:T(8,128)}, u32[]{:S(2)}) copy-start(f32[96,32]{0,1:T(8,128)} %param.30) | copy-start | bytes 36868
  0.7 11.9 %copy-start.13 = (f32[96,32]{0,1:T(8,128)S(1)}, f32[96,32]{0,1:T(8,128)}, u32[]{:S(2)}) copy-start(f32[96,32]{0,1:T(8,128)} %param.29) | copy-start | bytes 36868
  0.7 11.9 %copy-start.12 = (f32[96,32]{0,1:T(8,128)S(1)}, f32[96,32]{0,1:T(8,128)}, u32[]{:S(2)}) copy-start(f32[96,32]{0,1:T(8,128)} %param.28) | copy-start | bytes 36868
  0.7 11.9 %copy-start.11 = (f32[96,32]{0,1:T(8,128)S(1)}, f32[96,32]{0,1:T(8,128)}, u32[]{:S(2)}) copy-start(f32[96,32]{0,1:T(8,128)} %param.27) | copy-start | bytes 36868
  0.8 11.9 %copy-start.10 = (f32[96,32]{0,1:T(8,128)S(1)}, f32[96,32]{0,1:T(8,128)}, u32[]{:S(2)}) copy-start(f32[96,32]{0,1:T(8,128)} %param.26) | copy-start | bytes 36868
  0.8 11.9 %copy-start.9 = (f32[96,32]{0,1:T(8,128)S(1)}, f32[96,32]{0,1:T(8,128)}, u32[]{:S(2)}) copy-start(f32[96,32]{0,1:T(8,128)} %param.25) | copy-start | bytes 36868
  0.8 11.9 %copy-start.8 = (f32[96,32]{0,1:T(8,128)S(1)}, f32[96,32]{0,1:T(8,128)}, u32[]{:S(2)}) copy-start(f32[96,32]{0,1:T(8,128)} %param.24) | copy-start | bytes 36868
  4.2 130.6 %copy-start.20 = (s32[2]{0:T(128)}, s32[2]{0:T(128)S(1)}, u32[]{:S(2)}) copy-start(s32[2]{0:T(128)S(1)} %dynamic-slice_reduce_fusion.sizes_ref) | copy-start | bytes 28
  4.2 8.5 %copy-start.2 = (bf16[1,96,128,128]{3,2,1,0:T(8,128)(2,1)S(1)}, bf16[1,96,128,128]{3,2,1,0:T(8,128)(2,1)}, u32[]{:S(2)}) copy-start(bf16[1,96,128,128]{3,2,1,0:T(8,128)(2,1)} %param.20) | copy-start | bytes 9437188
  12.7 1.1 copy-start.5
  13.8 1.1 copy-start.7
  134.8 1.7 copy-start.3
  136.5 1.7 copy-start.4
  138.2 0.9 copy-start.6
  139.0 0.6 copy-start.16
  139.7 0.6 copy-start.17
  140.3 0.6 copy-start.18
  140.9 0.6 copy-start.19
  401.2 6.3 %copy-start.1 = (s32[4,2]{0,1:T(2,128)S(1)}, s32[4,2]{0,1:T(2,128)}, u32[]{:S(2)}) copy-start(s32[4,2]{0,1:T(2,128)} %param.22) | copy-start | bytes 100

commit v6 on v5

--- a/solution.py
+++ b/solution.py
@@ -389,34 +389,52 @@
 
 
 def weight_rounds(n, shares, me, share, pairs, sems):
-    near, far = n // 2, me // 2
+    far = me // 2
     core = lax.rem(me, 2)
+    mate = far + 1 - 2 * lax.rem(far, 2)
+    mine = far // 2 * 2
+    beyond = 2 - mine
+    inner = lax.rem(far + 1, 4) >= 2
     own_sem, send1, recv1, send2, recv2, send3, recv3 = sems
+    both = range(len(pairs))
+    origins = (mate, beyond, beyond + 1)
 
     def own(at):
         local, whole = pairs[at]
         return pltpu.make_async_copy(local, whole.at[core, :, far], own_sem.at[at])
 
-    def first(at, shift, back=False):
+    def first(at, back=False):
         local, whole = pairs[at]
-        origin = lax.rem(far + near - shift, near) if back else far
         return push(
             local.at[share],
-            whole.at[core, share, origin],
-            send1.at[at, shift],
-            recv1.at[at, shift],
-            chan=lax.rem(far + shift, near) * 2 + core,
-        )
-
-    def second(at, shift, turn, back=False):
+            whole.at[core, share, mate if back else far],
+            send1.at[at, 0],
+            recv1.at[at, 0],
+            chan=mate * 2 + core,
+        )
+
+    def across(at, half, back=False):
         whole = pairs[at][1]
-        origin = lax.rem(far + near - shift, near)
+        return push(
+            whole.at[core, share, mine + half],
+            whole.at[core, share, (beyond if back else mine) + half],
+            send1.at[at, 1 + half],
+            recv1.at[at, 1 + half],
+            chan=(3 - far) * 2 + core,
+        )
+
+    def onward(at, half):
+        block = pairs[at][1].at[core, share, beyond + half]
+        return push(block, block, send1.at[at, 3 + half], recv1.at[at, 1 + half], chan=mate * 2 + core)
+
+    def second(at, place, turn, back=False):
+        whole = pairs[at][1]
         holder = lax.rem(share + shares - turn, shares) if back else share
         return push(
-            whole.at[core, share, origin],
-            whole.at[core, holder, origin],
-            send2.at[at, shift, turn],
-            recv2.at[at, shift, turn],
+            whole.at[core, share, origins[place]],
+            whole.at[core, holder, origins[place]],
+            send2.at[at, place, turn],
+            recv2.at[at, place, turn],
             dp=lax.rem(share + turn, shares),
         )
 
@@ -426,39 +444,67 @@
             whole.at[core], whole.at[1 - core if back else core], send3.at[at], recv3.at[at], chan=far * 2 + 1 - core
         )
 
-    both = range(len(pairs))
+    def start_second(at, place):
+        for turn in range(1, shares):
+            second(at, place, turn).start()
 
     def start_first():
         for at in both:
             own(at).start()
-            for shift in range(1, near):
-                first(at, shift).start()
-
-    def start_second():
+            first(at).start()
+
+    def start_across():
         for at in both:
-            for shift in range(1, near):
-                first(at, shift, True).wait_recv()
-                for turn in range(1, shares):
-                    second(at, shift, turn).start()
+            own(at).wait()
+            first(at, True).wait_recv()
+
+            @pl.when(inner)
+            def _():
+                for half in range(2):
+                    across(at, half).start()
+
+            start_second(at, 0)
+
+    def start_onward():
+        @pl.when(inner)
+        def _():
+            for at in both:
+                for half in range(2):
+                    across(at, half, True).wait_recv()
+                    onward(at, half).start()
+                    start_second(at, 1 + half)
+
+    def start_last():
+        @pl.when(jnp.logical_not(inner))
+        def _():
+            for at in both:
+                for half in range(2):
+                    across(at, half, True).wait_recv()
+                    start_second(at, 1 + half)
 
     def start_third():
         for at in both:
-            own(at).wait()
-            for shift in range(1, near):
+            for place in range(3):
                 for turn in range(1, shares):
-                    second(at, shift, turn, True).wait_recv()
+                    second(at, place, turn, True).wait_recv()
             third(at).start()
 
     def finish():
         for at in both:
             third(at, True).wait_recv()
             third(at).wait_send()
-            for shift in range(1, near):
-                first(at, shift).wait_send()
+            first(at).wait_send()
+            for place in range(3):
                 for turn in range(1, shares):
-                    second(at, shift, turn).wait_send()
-
-    return start_first, start_second, start_third, finish
+                    second(at, place, turn).wait_send()
+
+            @pl.when(inner)
+            def _():
+                for half in range(2):
+                    across(at, half).wait_send()
+                    onward(at, half).wait_send()
+
+    return start_first, start_across, start_onward, start_last, start_third, finish
 
 
 def send_part(stage, target, me, peer, part, send_sem, recv_sem, shift):
@@ -538,7 +584,7 @@
     parts = count // GROUP
     block = side // n
     me, share = meet(n, shares)
-    start_first, start_second, start_third, finish = weight_rounds(
+    start_first, start_across, start_onward, start_last, start_third, finish = weight_rounds(
         n, shares, me, share, ((in_part_ref, in_whole_ref), (out_part_ref, out_whole_ref)), weight_sems
     )
     start_first()
@@ -593,7 +639,8 @@
 
     @pl.loop(0, parts)
     def _(part):
-        pl.when(part == parts // 2)(start_second)
+        pl.when(part == 1)(start_across)
+        pl.when(part == parts * 2 // 3)(start_onward)
 
         def one_channel(item):
             chan = part * GROUP + item
@@ -640,6 +687,7 @@
     own_m = pltpu.make_async_copy(mixed_stage.at[me], mixed_ref.at[me], own_sem.at[1])
     own_b.start()
     own_m.start()
+    start_last()
     start_third()
     for part in range(parts):
         own_back(part).wait()
@@ -689,10 +737,10 @@
             pltpu.SemaphoreType.DMA((2,)),
             pltpu.SemaphoreType.DMA((count // GROUP,)),
             pltpu.SemaphoreType.DMA((2,)),
-            pltpu.SemaphoreType.DMA((2, near)),
-            pltpu.SemaphoreType.DMA((2, near)),
-            pltpu.SemaphoreType.DMA((2, near, shares)),
-            pltpu.SemaphoreType.DMA((2, near, shares)),
+            pltpu.SemaphoreType.DMA((2, 5)),
+            pltpu.SemaphoreType.DMA((2, 3)),
+            pltpu.SemaphoreType.DMA((2, 3, shares)),
+            pltpu.SemaphoreType.DMA((2, 3, shares)),
             pltpu.SemaphoreType.DMA((2,)),
             pltpu.SemaphoreType.DMA((2,)),
         ],
@@ -1635,7 +1683,7 @@
         and count <= side
         and count % GROUP == 0
         and side % (4 * n * LINES) == 0
-        and n % 2 == 0
+        and n == 8
         and (rest[15].shape[0] * n) % STEP_HIDDEN == 0
         and rest[15].shape[0] % (16 * lax.axis_size("dp")) == 0
         and lax.axis_size("dp") > 1

time: 408 us -> 401 us (0.983)
  Pallas kernels: 367 us -> 360 us
    pallas_call x1, Pallas kernels: 120 us -> 112 us  [mixer_forward(): pl.pallas_call(functools.partial(mixer_kernel, n, shares), out_shape=(jax...]
where the time goes in v6:
time: 401 us; the launch traced here: 400 us
  Pallas kernels  360 us (90%)
  local copies, waits for them, and re-layouts  31.2 us (8%)
  other arithmetic  6.05 us (2%)
    pallas_call x1, Pallas kernels, mlp(): pl.pallas_call(functools.partial(mlp_kernel, n, shares), out_shape=(low(s...  142 us
    pallas_call x1, Pallas kernels, mixer_forward(): pl.pallas_call(functools.partial(mixer_kernel, n, shares), out_shape=(jax...  112 us
    pallas_call x1, Pallas kernels, mixer_back(): pl.pallas_call(functools.partial(back_kernel, n, shares), out_shape=(jax....  101 us
    unnamed x49, local copies, waits for them, and re-layouts  20.6 us

profile of v6, /device:TPU:9, one launch (start us, length us, event | category | flops | bytes accessed | tf_op | source)
XLA Modules:
  0.0 399.8 jit_solution(1088632321698884627)
XLA Ops:
  0.7 0.0 copy-start
  0.7 0.0 copy-start.22
  0.7 0.0 copy-start.21
  0.7 0.0 copy-start.15
  0.7 0.0 copy-start.14
  0.7 0.0 copy-start.13
  0.7 0.0 copy-start.12
  0.7 0.0 copy-start.11
  0.8 0.0 copy-start.10
  0.8 0.0 copy-start.9
  0.8 0.0 copy-start.8
  0.8 1.3 dynamic_slice.6
  4.0 0.0 copy-done
  4.0 0.2 dynamic-slice_reduce_fusion.sizes_ref
  4.2 0.0 copy-start.20
  4.2 0.0 copy-start.2
  4.2 0.8 broadcast_in_dim.10
  5.1 1.7 broadcast_in_dim.11.gain_ref
  6.8 1.6 broadcast_in_dim.12.shift_ref
  8.4 2.0 pad_maximum_fusion
  10.4 2.2 copy.38
  12.6 0.0 copy-done.22
  12.6 0.0 copy-done.21
  12.6 0.0 copy-done.15
  12.6 0.0 copy-done.14
  12.6 0.0 copy-done.13
  12.6 0.0 copy-done.12
  12.6 0.0 copy-done.11
  12.7 0.0 copy-done.10
  12.7 0.0 copy-done.9
  12.7 0.0 copy-done.8
  12.7 0.0 copy-done.2
  12.7 0.0 copy-start.5
  12.7 1.1 copy-done.5
  13.8 0.0 copy-start.7
  13.8 1.1 copy-done.7
  14.9 112.3 %mixer_forward.1 = (bf16[8,6,16,16,128]{4,3,2,1,0:T(8,128)(2,1)S(1)}, bf16[8,6,4,16,128]{4,3,2,1,0:T(8,128)(2,1)S(1)}, bf16[8,6,16,16,128]{4,3,2,1,0:T(8,128)(2,...) custom-call(s32[2]{0:T(128)S(1)} %dynamic-slice_reduce_fusion.sizes_, ...), custom_call_target="tpu_custom_call" | custom-call | tf_op jit(solution)/shard_map/mixer_forward/pallas_call | solution.py:712
  127.2 0.0 copy-done.20
  127.2 0.0 copy-start.3
  127.2 1.7 copy-done.3
  128.9 0.0 copy-start.4
  128.9 1.7 copy-done.4
  130.5 0.0 copy-start.6
  130.5 0.9 copy-done.6
  131.4 0.0 copy-start.16
  131.4 0.6 copy-done.16
  132.0 0.0 copy-start.17
  132.0 0.6 copy-done.17
  132.6 0.0 copy-start.18
  132.6 0.6 copy-done.18
  133.3 0.6 copy-done.19
  133.9 141.9 %mlp.1 = (bf16[8,4,4,96,128]{4,3,2,1,0:T(8,128)(2,1)}, bf16[8,1,4,96,128]{4,3,2,1,0:T(8,128)(2,1)}, bf16[8,3,4,96,128]{4,3,2,1,0:T(8,128)(2,1)}, bf16[4,3072,512...) custom-call(bf16[8,6,16,16,128]{4,3,2,1,0:T(8,128)(2,1)} %copy-done., ...), custom_call_target="tpu_custom_call" | custom-call | tf_op jit(solution)/shard_map/mlp/pallas_call | solution.py:1084
  275.8 101.2 %mixer_back.1 = (bf16[96,128,128]{2,1,0:T(8,128)(2,1)}, f32[96,128,128]{2,1,0:T(8,128)}, f32[96,384]{1,0:T(8,128)}, f32[8,128]{1,0:T(8,128)}, f32[8,768]{1,0:T(8...) custom-call(s32[2]{0:T(128)} %copy-done.20, bf16[96,128,128]{2,1,0:T(8,128)(2,1)} %bitcast.40, ...), custom_call_target="tpu_custom_call" | custom-call | tf_op jit(solution)/shard_map/mixer_back/pallas_call | solution.py:1488
  377.0 1.4 slice_reduce_fusion.1
  378.5 4.2 %taps_back.1 = (f32[32,96]{1,0:T(8,128)}, f32[32,96]{1,0:T(8,128)}, f32[32,96]{1,0:T(8,128)}, f32[32,96]{1,0:T(8,128)}, f32[32,96]{1,0:T(8,128)}, /*index=5*/f32...) custom-call(f32[96,384]{1,0:T(8,128)} %get-tuple-element.68.small_ref, f32[32,96]{1,0:T(8,128)} %bitcast.44, ...), custom_call_target="tpu_custom_call" | custom-call | tf_op jit(solution)/shard_map/taps_back/pallas_call | solution.py:1576
  382.7 1.3 slice_bitcast_fusion.1
  384.0 2.2 bitcast_convert_fusion.1
  386.1 1.2 bitcast_convert_fusion
  387.3 0.7 slice_reduce_fusion
  388.1 0.1 slice.28
  388.1 1.4 copy.40
  389.5 4.0 copy.43
  393.5 6.3 %copy.44 = f32[1,96,128,128]{3,2,1,0:T(8,128)} copy(f32[1,96,128,128]{3,2,1,0:T(8,128)} %bitcast.62) | data formatting | bytes 12582912
  399.8 0.0 copy-done.1
  (2 shorter events, 0.0 us)
Async XLA Ops:
  0.7 3.4 copy-start
  0.7 11.9 %copy-start.22 = (f32[96]{0:T(128)S(1)}, f32[96]{0:T(128)}, u32[]{:S(2)}) copy-start(f32[96]{0:T(128)} %scale_ref.3) | copy-start | bytes 1156
  0.7 11.9 %copy-start.21 = (f32[96]{0:T(128)S(1)}, f32[96]{0:T(128)}, u32[]{:S(2)}) copy-start(f32[96]{0:T(128)} %skip_ref.3) | copy-start | bytes 1156
  0.7 11.9 %copy-start.15 = (f32[96,32]{0,1:T(8,128)S(1)}, f32[96,32]{0,1:T(8,128)}, u32[]{:S(2)}) copy-start(f32[96,32]{0,1:T(8,128)} %param.31) | copy-start | bytes 36868
  0.7 11.9 %copy-start.14 = (f32[96,32]{0,1:T(8,128)S(1)}, f32[96,32]{0,1:T(8,128)}, u32[]{:S(2)}) copy-start(f32[96,32]{0,1:T(8,128)} %param.30) | copy-start | bytes 36868
  0.7 11.9 %copy-start.13 = (f32[96,32]{0,1:T(8,128)S(1)}, f32[96,32]{0,1:T(8,128)}, u32[]{:S(2)}) copy-start(f32[96,32]{0,1:T(8,128)} %param.29) | copy-start | bytes 36868
  0.7 11.9 %copy-start.12 = (f32[96,32]{0,1:T(8,128)S(1)}, f32[96,32]{0,1:T(8,128)}, u32[]{:S(2)}) copy-start(f32[96,32]{0,1:T(8,128)} %param.28) | copy-start | bytes 36868
  0.7 11.9 %copy-start.11 = (f32[96,32]{0,1:T(8,128)S(1)}, f32[96,32]{0,1:T(8,128)}, u32[]{:S(2)}) copy-start(f32[96,32]{0,1:T(8,128)} %param.27) | copy-start | bytes 36868
  0.8 11.9 %copy-start.10 = (f32[96,32]{0,1:T(8,128)S(1)}, f32[96,32]{0,1:T(8,128)}, u32[]{:S(2)}) copy-start(f32[96,32]{0,1:T(8,128)} %param.26) | copy-start | bytes 36868
  0.8 11.9 %copy-start.9 = (f32[96,32]{0,1:T(8,128)S(1)}, f32[96,32]{0,1:T(8,128)}, u32[]{:S(2)}) copy-start(f32[96,32]{0,1:T(8,128)} %param.25) | copy-start | bytes 36868
  0.8 11.9 %copy-start.8 = (f32[96,32]{0,1:T(8,128)S(1)}, f32[96,32]{0,1:T(8,128)}, u32[]{:S(2)}) copy-start(f32[96,32]{0,1:T(8,128)} %param.24) | copy-start | bytes 36868
  4.2 123.0 %copy-start.20 = (s32[2]{0:T(128)}, s32[2]{0:T(128)S(1)}, u32[]{:S(2)}) copy-start(s32[2]{0:T(128)S(1)} %dynamic-slice_reduce_fusion.sizes_ref) | copy-start | bytes 28
  4.2 8.5 %copy-start.2 = (bf16[1,96,128,128]{3,2,1,0:T(8,128)(2,1)S(1)}, bf16[1,96,128,128]{3,2,1,0:T(8,128)(2,1)}, u32[]{:S(2)}) copy-start(bf16[1,96,128,128]{3,2,1,0:T(8,128)(2,1)} %param.20) | copy-start | bytes 9437188
  12.7 1.1 copy-start.5
  13.8 1.1 copy-start.7
  127.2 1.7 copy-start.3
  128.9 1.7 copy-start.4
  130.5 0.9 copy-start.6
  131.4 0.6 copy-start.16
  132.0 0.6 copy-start.17
  132.6 0.6 copy-start.18
  133.3 0.6 copy-start.19
  393.5 6.3 %copy-start.1 = (s32[4,2]{0,1:T(2,128)S(1)}, s32[4,2]{0,1:T(2,128)}, u32[]{:S(2)}) copy-start(s32[4,2]{0,1:T(2,128)} %param.22) | copy-start | bytes 100

commit v7 on v6

--- a/solution.py
+++ b/solution.py
@@ -262,7 +262,7 @@
 
 MESH = pl.DeviceIdType.MESH
 GROUP = 16
-ABREAST = 2
+ABREAST = 4
 LINES = 4
 STEP_HIDDEN = 512
 mebi = 1024 * 1024
@@ -640,7 +640,7 @@
     @pl.loop(0, parts)
     def _(part):
         pl.when(part == 1)(start_across)
-        pl.when(part == parts * 2 // 3)(start_onward)
+        pl.when(part == parts // 2)(start_onward)
 
         def one_channel(item):
             chan = part * GROUP + item
@@ -668,6 +668,8 @@
         turn(mixed_stage, part)
         send(mixed_stage, mixed_ref, part, send_m, recv_m)
 
+    start_last()
+
     @pl.loop(0, parts)
     def _(part):
         @pl.loop(0, GROUP)
@@ -687,7 +689,6 @@
     own_m = pltpu.make_async_copy(mixed_stage.at[me], mixed_ref.at[me], own_sem.at[1])
     own_b.start()
     own_m.start()
-    start_last()
     start_third()
     for part in range(parts):
         own_back(part).wait()

time: 401 us -> 400 us (level)
  no operation moved by 1% of the time
where the time goes in v7:
time: 400 us
  Pallas kernels  359 us (90%)
  local copies, waits for them, and re-layouts  31.2 us (8%)
  other arithmetic  6.05 us (2%)
    pallas_call x1, Pallas kernels, mlp(): pl.pallas_call(functools.partial(mlp_kernel, n, shares), out_shape=(low(s...  142 us
    pallas_call x1, Pallas kernels, mixer_forward(): pl.pallas_call(functools.partial(mixer_kernel, n, shares), out_shape=(jax...  112 us
    pallas_call x1, Pallas kernels, mixer_back(): pl.pallas_call(functools.partial(back_kernel, n, shares), out_shape=(jax....  101 us
    unnamed x49, local copies, waits for them, and re-layouts  20.6 us

profile of v7, /device:TPU:9, one launch (start us, length us, event | category | flops | bytes accessed | tf_op | source)
XLA Modules:
  0.0 399.6 jit_solution(8595374759340291161)
XLA Ops:
  0.7 0.0 copy-start
  0.7 0.0 copy-start.22
  0.7 0.0 copy-start.21
  0.7 0.0 copy-start.15
  0.7 0.0 copy-start.14
  0.7 0.0 copy-start.13
  0.7 0.0 copy-start.12
  0.7 0.0 copy-start.11
  0.8 0.0 copy-start.10
  0.8 0.0 copy-start.9
  0.8 0.0 copy-start.8
  0.8 1.3 dynamic_slice.6
  4.0 0.0 copy-done
  4.0 0.2 dynamic-slice_reduce_fusion.sizes_ref
  4.2 0.0 copy-start.20
  4.2 0.0 copy-start.2
  4.2 0.8 broadcast_in_dim.10
  5.1 1.7 broadcast_in_dim.11.gain_ref
  6.8 1.6 broadcast_in_dim.12.shift_ref
  8.4 2.0 pad_maximum_fusion
  10.4 2.2 copy.38
  12.6 0.0 copy-done.22
  12.6 0.0 copy-done.21
  12.6 0.0 copy-done.15
  12.6 0.0 copy-done.14
  12.6 0.0 copy-done.13
  12.6 0.0 copy-done.12
  12.6 0.0 copy-done.11
  12.7 0.0 copy-done.10
  12.7 0.0 copy-done.9
  12.7 0.0 copy-done.8
  12.7 0.0 copy-done.2
  12.7 0.0 copy-start.5
  12.7 1.1 copy-done.5
  13.8 0.0 copy-start.7
  13.8 1.1 copy-done.7
  14.9 111.9 %mixer_forward.1 = (bf16[8,6,16,16,128]{4,3,2,1,0:T(8,128)(2,1)S(1)}, bf16[8,6,4,16,128]{4,3,2,1,0:T(8,128)(2,1)S(1)}, bf16[8,6,16,16,128]{4,3,2,1,0:T(8,128)(2,...) custom-call(s32[2]{0:T(128)S(1)} %dynamic-slice_reduce_fusion.sizes_, ...), custom_call_target="tpu_custom_call" | custom-call | tf_op jit(solution)/shard_map/mixer_forward/pallas_call | solution.py:713
  126.8 0.0 copy-done.20
  126.8 0.0 copy-start.3
  126.8 1.7 copy-done.3
  128.5 0.0 copy-start.4
  128.5 1.7 copy-done.4
  130.2 0.9 copy-done.6
  131.0 0.0 copy-start.16
  131.0 0.6 copy-done.16
  131.6 0.0 copy-start.17
  131.6 0.6 copy-done.17
  132.3 0.0 copy-start.18
  132.3 0.6 copy-done.18
  132.9 0.0 copy-start.19
  132.9 0.6 copy-done.19
  133.5 142.1 %mlp.1 = (bf16[8,4,4,96,128]{4,3,2,1,0:T(8,128)(2,1)}, bf16[8,1,4,96,128]{4,3,2,1,0:T(8,128)(2,1)}, bf16[8,3,4,96,128]{4,3,2,1,0:T(8,128)(2,1)}, bf16[4,3072,512...) custom-call(bf16[8,6,16,16,128]{4,3,2,1,0:T(8,128)(2,1)} %copy-done., ...), custom_call_target="tpu_custom_call" | custom-call | tf_op jit(solution)/shard_map/mlp/pallas_call | solution.py:1085
  275.6 101.2 %mixer_back.1 = (bf16[96,128,128]{2,1,0:T(8,128)(2,1)}, f32[96,128,128]{2,1,0:T(8,128)}, f32[96,384]{1,0:T(8,128)}, f32[8,128]{1,0:T(8,128)}, f32[8,768]{1,0:T(8...) custom-call(s32[2]{0:T(128)} %copy-done.20, bf16[96,128,128]{2,1,0:T(8,128)(2,1)} %bitcast.40, ...), custom_call_target="tpu_custom_call" | custom-call | tf_op jit(solution)/shard_map/mixer_back/pallas_call | solution.py:1489
  376.8 1.4 slice_reduce_fusion.1
  378.2 4.2 %taps_back.1 = (f32[32,96]{1,0:T(8,128)}, f32[32,96]{1,0:T(8,128)}, f32[32,96]{1,0:T(8,128)}, f32[32,96]{1,0:T(8,128)}, f32[32,96]{1,0:T(8,128)}, /*index=5*/f32...) custom-call(f32[96,384]{1,0:T(8,128)} %get-tuple-element.68.small_ref, f32[32,96]{1,0:T(8,128)} %bitcast.44, ...), custom_call_target="tpu_custom_call" | custom-call | tf_op jit(solution)/shard_map/taps_back/pallas_call | solution.py:1577
  382.5 1.3 slice_bitcast_fusion.1
  383.8 2.2 bitcast_convert_fusion.1
  385.9 1.2 bitcast_convert_fusion
  387.1 0.7 slice_reduce_fusion
  387.8 0.1 slice.28
  387.9 1.4 copy.40
  389.3 4.0 copy.43
  393.3 6.3 %copy.44 = f32[1,96,128,128]{3,2,1,0:T(8,128)} copy(f32[1,96,128,128]{3,2,1,0:T(8,128)} %bitcast.62) | data formatting | bytes 12582912
  399.6 0.0 copy-done.1
  (2 shorter events, 0.0 us)
Async XLA Ops:
  0.7 3.4 copy-start
  0.7 11.9 %copy-start.22 = (f32[96]{0:T(128)S(1)}, f32[96]{0:T(128)}, u32[]{:S(2)}) copy-start(f32[96]{0:T(128)} %scale_ref.3) | copy-start | bytes 1156
  0.7 11.9 %copy-start.21 = (f32[96]{0:T(128)S(1)}, f32[96]{0:T(128)}, u32[]{:S(2)}) copy-start(f32[96]{0:T(128)} %skip_ref.3) | copy-start | bytes 1156
  0.7 11.9 %copy-start.15 = (f32[96,32]{0,1:T(8,128)S(1)}, f32[96,32]{0,1:T(8,128)}, u32[]{:S(2)}) copy-start(f32[96,32]{0,1:T(8,128)} %param.31) | copy-start | bytes 36868
  0.7 11.9 %copy-start.14 = (f32[96,32]{0,1:T(8,128)S(1)}, f32[96,32]{0,1:T(8,128)}, u32[]{:S(2)}) copy-start(f32[96,32]{0,1:T(8,128)} %param.30) | copy-start | bytes 36868
  0.7 11.9 %copy-start.13 = (f32[96,32]{0,1:T(8,128)S(1)}, f32[96,32]{0,1:T(8,128)}, u32[]{:S(2)}) copy-start(f32[96,32]{0,1:T(8,128)} %param.29) | copy-start | bytes 36868
  0.7 11.9 %copy-start.12 = (f32[96,32]{0,1:T(8,128)S(1)}, f32[96,32]{0,1:T(8,128)}, u32[]{:S(2)}) copy-start(f32[96,32]{0,1:T(8,128)} %param.28) | copy-start | bytes 36868
  0.7 11.9 %copy-start.11 = (f32[96,32]{0,1:T(8,128)S(1)}, f32[96,32]{0,1:T(8,128)}, u32[]{:S(2)}) copy-start(f32[96,32]{0,1:T(8,128)} %param.27) | copy-start | bytes 36868
  0.8 11.9 %copy-start.10 = (f32[96,32]{0,1:T(8,128)S(1)}, f32[96,32]{0,1:T(8,128)}, u32[]{:S(2)}) copy-start(f32[96,32]{0,1:T(8,128)} %param.26) | copy-start | bytes 36868
  0.8 11.9 %copy-start.9 = (f32[96,32]{0,1:T(8,128)S(1)}, f32[96,32]{0,1:T(8,128)}, u32[]{:S(2)}) copy-start(f32[96,32]{0,1:T(8,128)} %param.25) | copy-start | bytes 36868
  0.8 11.9 %copy-start.8 = (f32[96,32]{0,1:T(8,128)S(1)}, f32[96,32]{0,1:T(8,128)}, u32[]{:S(2)}) copy-start(f32[96,32]{0,1:T(8,128)} %param.24) | copy-start | bytes 36868
  4.2 122.6 %copy-start.20 = (s32[2]{0:T(128)}, s32[2]{0:T(128)S(1)}, u32[]{:S(2)}) copy-start(s32[2]{0:T(128)S(1)} %dynamic-slice_reduce_fusion.sizes_ref) | copy-start | bytes 28
  4.2 8.5 %copy-start.2 = (bf16[1,96,128,128]{3,2,1,0:T(8,128)(2,1)S(1)}, bf16[1,96,128,128]{3,2,1,0:T(8,128)(2,1)}, u32[]{:S(2)}) copy-start(bf16[1,96,128,128]{3,2,1,0:T(8,128)(2,1)} %param.20) | copy-start | bytes 9437188
  12.7 1.1 copy-start.5
  13.8 1.1 copy-start.7
  126.8 1.7 copy-start.3
  128.5 1.7 copy-start.4
  130.2 0.9 copy-start.6
  131.0 0.6 copy-start.16
  131.6 0.6 copy-start.17
  132.3 0.6 copy-start.18
  132.9 0.6 copy-start.19
  393.3 6.3 %copy-start.1 = (s32[4,2]{0,1:T(2,128)S(1)}, s32[4,2]{0,1:T(2,128)}, u32[]{:S(2)}) copy-start(s32[4,2]{0,1:T(2,128)} %param.22) | copy-start | bytes 100
